TPU v7x, 32 devices: a whole 2x2x4 slice. The times are simulated.
32 devices in a mesh: unit: 8 (over y, x, core), tm: 4 (over z).
Axes of the slice: x: 2, y: 2, z: 4, core: 2. Of those that a mesh axis runs over, the one named last changes fastest.
Arguments:
- spikes: int32 [2048, 8192], P('tm', 'unit'), may hold values from 0 to 2
- stimulus: bfloat16 [2048, 64], P('tm'), may hold values from -6 to 6
- bias: float32 [8192], P('unit'), may hold values from -1.5 to 0
- hist_weight: float32 [10, 8192], P(None, 'unit'), may hold values from -0.9 to 0.9
- stim_filter: bfloat16 [8192, 64], P('unit'), may hold values from -0.5 to 0.5
- coupling_mix: float32 [10], replicated, may hold values from -3 to 3
- coupling_target: int32 [64, 4], P('unit'), may hold values from 0 to 63, as said below
- coupling_weight: bfloat16 [64, 4, 128, 128], P('unit'), may hold values from -0.059814453 to 0.059814453
Outputs:
- grad_bias: float32 [8192], P('unit')
- grad_hist: float32 [10, 8192], P(None, 'unit')
- grad_stim: float32 [8192, 64], P(('unit', 'tm'))
- grad_coupling: float32 [64, 4, 128, 128], P('unit', None, 'tm')
Inputs may be any that keep to these rules, and one draw needn't show every extreme that they name: `coupling_target`: the 4 entries of a row are distinct. Among the rows of one device (8 aligned rows), the targets owned by any one device (tiles k * 8 to k * 8 + 7) are at most 2 distinct tiles, and every owner that is named gets exactly 2.
All inputs are finite; a program needn't handle non-finite values.
Results may differ from a plain program's by a relative error of at most 0.0041.
Values may be sent and summed in bfloat16 or wider, within the bound.
No kernel may reach another device: no remote copies, remote signals or barrier semaphores. Data moves between devices by JAX's collectives and lax.ppermute only.
A program may use at most 256 MiB of HBM per device.

v0:
```python
import math

import jax
import jax.numpy as jnp
from jax import lax
from jax.sharding import PartitionSpec as P

TILE = 128
FAN = 4
CAP = 2
NB = 10
LAG = 128


def passed_along(value, axis, steps):
    count = lax.axis_size(axis)
    leading, last = (max(0, -steps), min(count, count - steps))
    return lax.ppermute(value, axis, [(source, source + steps) for source in range(leading, last)])


def raised_cosine(count, lag):
    low = math.log(2.0)
    high = math.log(lag + 1.0)
    spacing = (high - low) / (count - 1)
    stretched = jnp.log(jnp.arange(1, lag + 1).astype(jnp.float32) + 1.0)
    centers = low + spacing * jnp.arange(count).astype(jnp.float32)
    phases = jnp.clip(
        (stretched[None, :] - centers[:, None]) * (math.pi / (2.0 * spacing)), -math.pi, math.pi
    )
    shapes = 0.5 * (1.0 + jnp.cos(phases))
    return (shapes / jnp.sum(shapes, axis=1, keepdims=True)).astype(jnp.bfloat16)


def shards(
    spikes, stimulus, bias, hist_weight, stim_filter, coupling_mix, coupling_target, coupling_weight
):
    time_dev, units_dev = spikes.shape
    tiles_dev = units_dev // TILE
    unit_count = lax.axis_size("unit")
    time_count = lax.axis_size("tm")
    time_total = time_dev * time_count
    block_rows = min(time_dev, 4 * LAG)
    counts_bf = spikes.astype(jnp.bfloat16)
    previous = passed_along(counts_bf[time_dev - LAG :], "tm", 1)
    extended = jnp.concatenate([previous, counts_bf], axis=0)
    basis = raised_cosine(NB, LAG)
    row_index = jnp.arange(block_rows, dtype=jnp.int32)[:, None]
    col_index = jnp.arange(block_rows + LAG, dtype=jnp.int32)[None, :]
    lag_index = LAG + row_index - col_index
    inside = (lag_index >= 1) & (lag_index <= LAG)
    toeplitz = jnp.where(
        inside[None, :, :],
        basis[:, jnp.clip(lag_index - 1, 0, LAG - 1)],
        jnp.zeros((), jnp.bfloat16),
    )
    history_blocks = jnp.einsum(
        "bkw,wu->bku", toeplitz, extended, preferred_element_type=jnp.float32
    )
    mixed = jnp.sum(coupling_mix[:, None, None] * history_blocks, axis=0).astype(jnp.bfloat16)
    mixed_tiles = mixed.reshape(time_dev, tiles_dev, TILE)
    slot_count = unit_count * CAP
    flat_target = coupling_target.reshape(-1)
    entry_count = flat_target.shape[0]
    owner = flat_target // tiles_dev
    local_tile = flat_target % tiles_dev
    entry_index = jnp.arange(entry_count, dtype=jnp.int32)
    same_tile = flat_target[:, None] == flat_target[None, :]
    first_seen = jnp.logical_not(
        jnp.any(same_tile & (entry_index[None, :] < entry_index[:, None]), axis=1)
    )
    lower_rank = (
        (owner[:, None] == owner[None, :])
        & (local_tile[None, :] < local_tile[:, None])
        & first_seen[None, :]
    )
    slot_of = owner * CAP + jnp.sum(lower_rank.astype(jnp.int32), axis=1)
    slot_hit = slot_of[None, :] == jnp.arange(slot_count, dtype=jnp.int32)[:, None]
    slot_ids = jnp.max(jnp.where(slot_hit, local_tile[None, :], -1), axis=1)
    slot_table = slot_hit.reshape(slot_count, tiles_dev, FAN).astype(jnp.bfloat16)
    slot_weight = jnp.einsum(
        "csf,sfkn->cskn", slot_table, coupling_weight, preferred_element_type=jnp.float32
    ).astype(jnp.bfloat16)
    partials = jnp.einsum(
        "tsk,cskn->ctn", mixed_tiles, slot_weight, preferred_element_type=jnp.float32
    ).astype(jnp.bfloat16)
    received, received_ids = (
        lax.all_to_all(
            partials.reshape(unit_count, CAP, time_dev, TILE),
            "unit",
            split_axis=0,
            concat_axis=0,
            tiled=True,
        ),
        lax.all_to_all(
            slot_ids.reshape(unit_count, CAP), "unit", split_axis=0, concat_axis=0, tiled=True
        ),
    )
    flat_ids = received_ids.reshape(-1)
    placing = (flat_ids[None, :] == jnp.arange(tiles_dev, dtype=jnp.int32)[:, None]).astype(
        jnp.bfloat16
    )
    coupling = jnp.einsum(
        "jc,ctn->tjn",
        placing,
        received.reshape(slot_count, time_dev, TILE),
        preferred_element_type=jnp.float32,
    ).reshape(time_dev, units_dev)
    drive = jnp.einsum("tc,uc->tu", stimulus, stim_filter, preferred_element_type=jnp.float32)
    logit = (
        bias[None, :] + drive + jnp.sum(history_blocks * hist_weight[:, None, :], axis=0) + coupling
    )
    resid = spikes.astype(jnp.float32) - jnp.exp(logit)
    resid_bf = resid.astype(jnp.bfloat16)
    bias_total, hist_total = lax.psum(
        (jnp.sum(resid, axis=0), jnp.sum(history_blocks * resid[None, :, :], axis=1)), "tm"
    )
    grad_bias = bias_total / time_total
    grad_hist = hist_total / time_total
    everyone = lax.all_gather(resid_bf, "unit", axis=1, tiled=True)
    picking = (
        flat_target[:, None] == jnp.arange(tiles_dev * unit_count, dtype=jnp.int32)[None, :]
    ).astype(jnp.bfloat16)
    selected = jnp.einsum(
        "ej,tjn->ten",
        picking,
        everyone.reshape(time_dev, tiles_dev * unit_count, TILE),
        preferred_element_type=jnp.float32,
    ).astype(jnp.bfloat16)
    selected = selected.reshape(time_dev, tiles_dev, FAN, TILE)
    coupling_terms = jnp.einsum(
        "tsk,tsfn->sfkn", mixed_tiles, selected, preferred_element_type=jnp.float32
    )
    grad_coupling = (
        lax.psum_scatter(coupling_terms, "tm", scatter_dimension=2, tiled=True) / time_total
    )
    swapped = lax.all_to_all(resid_bf, "tm", split_axis=1, concat_axis=0, tiled=True)
    stim_total = jnp.einsum(
        "tu,tc->uc",
        swapped,
        lax.all_gather(stimulus, "tm", axis=0, tiled=True),
        preferred_element_type=jnp.float32,
    )
    grad_stim = stim_total / time_total
    return (grad_bias, grad_hist, grad_stim, grad_coupling)


def solution(mesh):
    return jax.shard_map(
        shards,
        mesh=mesh,
        in_specs=(
            P("tm", "unit"),
            P("tm", None),
            P("unit"),
            P(None, "unit"),
            P("unit", None),
            P(),
            P("unit", None),
            P("unit", None, None, None),
        ),
        out_specs=(
            P("unit"),
            P(None, "unit"),
            P(("unit", "tm"), None),
            P("unit", None, "tm", None),
        ),
        check_vma=False,
    )
```

profile of v0, /device:TPU:0, one launch (start us, length us, event | category | flops | bytes accessed | tf_op | source)
XLA Modules:
  0.0 1472.0 jit_solution(279839320856647576)
XLA Ops:
  7.2 1.9 convert_element_type.65
  9.8 5.6 collective-permute-start
  16.9 3.7 all-to-all-start.1
  20.7 1.5 compare_select_fusion
  25.1 3.5 convert_bitcast_fusion
  28.9 1133.5 %gather_fusion = bf16[327680,10]{1,0:T(8,128)(2,1)} fusion(bf16[10,128]{0,1:T(8,128)(2,1)S(1)} %copy.67, s32[327680]{0:T(1024)S(1)} %copy-done.4), kind=kCustom, calls=%fused_computation | custom fusion | bytes 14417920 | tf_op jit(solution)/shard_map/gather | solution.py:53
  1162.3 62.6 %copy.68 = bf16[512,640,10]{1,0,2:T(8,128)(2,1)} copy(bf16[512,640,10]{2,1,0:T(8,128)(2,1)} %bitcast) | data formatting | bytes 13107200 | tf_op jit(solution)/shard_map/gather | solution.py:53
  1225.3 18.5 %multiply_reduce_fusion.2 = (f32[512,1024]{1,0:T(8,128)}, bf16[512,1024]{1,0:T(8,128)(2,1)S(1)}, f32[10,512,1024]{2,1,0:T(8,128)}) fusion(f32[10,1024]{1,0:T(8,128)S(1)} %copy-done.10, f32[10]{0:T(128)S(1)} %copy-done.11, bf16[512,1024]{1,0:T(8,128)(2,1)S(1)} %convert_element_type.65, bf16[128,1024]{1,0:T(8,128)(2,1)} %collective-permute-done, ...), kind=kOutput, calls=%fused_computation.3 | convolution fusion | flops 6736707584 | bytes 32350248 | tf_op jit(solution)/shard_map/bkw,wu->bku/dot_general | solution.py:56
  1244.4 6.1 bitcast_convert_fusion
  1250.5 4.4 all-to-all-start
  1256.2 25.3 %all-to-all-done = bf16[8,2,512,128]{2,3,1,0:T(8,128)(2,1)S(1)} async-done(((bf16[8,2,512,128]{2,3,1,0:T(8,128)(2,1)}), bf16[8,2,512,128]{2,3,1,0:T(8,128)(2,1)S(1)}, u32[]{:S(2)}, u32[]{:S(2)}) %all-to-all-start) | async-done | bytes 2097184 | tf_op jit(solution)/shard_map/all_to_all | solution.py:87
  1281.5 4.0 copy.78
  1285.6 2.2 fusion.36
  1288.4 1.9 fusion.41
  1290.4 52.2 %all-gather.2.cloned.1.call-done = bf16[512,8192]{1,0:T(8,128)(2,1)} async-done(((bf16[512,1024]{1,0:T(8,128)(2,1)}), bf16[512,8192]{1,0:T(8,128)(2,1)}) %all-gather.2.cloned.1.call-update) | async-done | bytes 8388624 | tf_op jit(solution)/shard_map/all_gather | solution.py:119
  1342.6 9.4 copy.94
  1352.1 4.7 convolution_convert_fusion
  1356.7 3.3 fusion.13
  1360.0 3.1 copy.83
  1365.4 4.6 all-to-all-start.2
  1370.0 62.4 %all_gather.6 = bf16[2048,64]{0,1:T(8,128)(2,1)S(1)} all-gather(bf16[512,64]{0,1:T(8,128)(2,1)S(1)} %copy-done.6), channel_id=1, replica_groups=mesh['unit'=8,'tm'=4] {'tm'}, dimensions={0}, use_global_device_ids=true | all-gather | bytes 327680 | tf_op jit(solution)/shard_map/all_gather | solution.py:140
  1432.4 8.6 multiply_reduce_fusion
  1441.0 18.6 %all-reduce = (f32[1024]{0:T(1024)S(1)}, f32[10,1024]{1,0:T(8,128)S(1)}) all-reduce(f32[1024]{0:T(1024)S(1)} %get-tuple-element.29, f32[10,1024]{1,0:T(8,128)S(1)} %multiply_reduce_fusion), channel_id=1, replica_groups=mesh['unit'=8,'tm'=4] {'tm'}, use_global_device_ids=true, to_apply=%region_7.8 | all-reduce | flops 11264 | bytes 90112 | tf_op jit(solution)/shard_map/psum | solution.py:114
  1460.8 2.1 convolution_multiply_fusion
  (62 shorter events, 13.9 us)
Async XLA Ops:
  7.2 17.9 %copy-start = (bf16[8,4,128,128]{3,2,1,0:T(8,128)(2,1)S(1)}, bf16[8,4,128,128]{3,2,1,0:T(8,128)(2,1)}, u32[]{:S(2)}) copy-start(bf16[8,4,128,128]{3,2,1,0:T(8,128)(2,1)} %param.15) | copy-start | bytes 3145732
  7.2 8.3 copy-start.9
  9.8 1215.4 %collective-permute-start = (bf16[128,1024]{1,0:T(8,128)(2,1)}, bf16[128,1024]{1,0:T(8,128)(2,1)}, u32[]{:S(2)}, u32[]{:S(2)}) collective-permute-start(bf16[128,1024]{1,0:T(8,128)(2,1)} %slice.6), channel_id=1, source_target_pairs={{0,1},{1,2},{2,3},{4,5},{5,6},{6,7},{8,9},{9,10},{10,11},{12,13},{... | collective-permute-start | bytes 786440 | tf_op jit(solution)/shard_map/ppermute | solution.py:18
  16.9 1233.6 %all-to-all-start.1 = ((s32[8,1,2]{2,1,0:T(1,128)}), s32[8,1,2]{2,1,0:T(1,128)S(1)}, u32[]{:S(2)}, u32[]{:S(2)}) async-start(s32[8,1,2]{2,1,0:T(1,128)} %bitcast.13), calls=%async_computation.1 | async-start | bytes 8192 | tf_op jit(solution)/shard_map/all_to_all | solution.py:94
  25.1 3.8 copy-start.4
  1162.3 62.9 %copy-start.10 = (f32[10,1024]{1,0:T(8,128)S(1)}, f32[10,1024]{1,0:T(8,128)}, u32[]{:S(2)}) copy-start(f32[10,1024]{1,0:T(8,128)} %param.11) | copy-start | bytes 122884
  1162.3 62.9 %copy-start.11 = (f32[10]{0:T(128)S(1)}, f32[10]{0:T(128)}, u32[]{:S(2)}) copy-start(f32[10]{0:T(128)} %param.13) | copy-start | bytes 124
  1250.5 31.0 %all-to-all-start = ((bf16[8,2,512,128]{2,3,1,0:T(8,128)(2,1)}), bf16[8,2,512,128]{2,3,1,0:T(8,128)(2,1)S(1)}, u32[]{:S(2)}, u32[]{:S(2)}) async-start(bf16[8,2,512,128]{2,3,1,0:T(8,128)(2,1)} %bitcast.77), calls=%async_computation | async-start | bytes 4194304 | tf_op jit(solution)/shard_map/all_to_all | solution.py:87
  1254.9 87.8 %all-gather.2.cloned.1.call-start = ((), (), s32[]{:S(2)}) async-start(), calls=%async_computation.4 | async-start | bytes 9437184 | tf_op jit(solution)/shard_map/all_gather | solution.py:119
  1281.5 6.2 copy-start.6
  1281.5 6.2 copy-start.7
  1285.6 2.2 copy-start.3
  1285.6 2.9 copy-start.5
  1285.6 2.9 copy-start.8
  1290.4 172.6 %reduce-scatter.2.cloned.1.call-start = ((), (), s32[]{:S(2)}) async-start(), calls=%async_computation.5 | async-start | bytes 2621440 | tf_op jit(solution)/shard_map/reduce_scatter | solution.py:134
  1363.1 1.2 copy-start.2
  1365.4 95.4 %all-to-all-start.2 = ((bf16[512,4,256]{2,0,1:T(8,128)(2,1)}), bf16[512,4,256]{2,0,1:T(8,128)(2,1)}, u32[]{:S(2)}, u32[]{:S(2)}) async-start(bf16[512,4,256]{2,0,1:T(8,128)(2,1)} %bitcast.76), calls=%async_computation.2 | async-start | bytes 2097152 | tf_op jit(solution)/shard_map/all_to_all | solution.py:136
  1432.4 32.8 %copy-start.1 = (bf16[8,4,128,128]{3,2,1,0:T(8,128)(2,1)S(1)}, bf16[8,4,128,128]{3,2,1,0:T(8,128)(2,1)}, u32[]{:S(2)}) copy-start(bf16[8,4,128,128]{3,2,1,0:T(8,128)(2,1)} %param.15) | copy-start | bytes 3145732
Sparse Core Ops, SparseCore 0:
  1290.5 52.0 all-gather.1
  1363.3 63.8 reduce-scatter.1
where the time goes:
time: 1470 us
  local copies, waits for them, and re-layouts  1220 us (83%)
  blocking collectives  81 us (6%)
  waiting for transfers between devices  77.6 us (5%)
  matrix products  42.4 us (3%)
  starting transfers between devices  18.4 us (1%)
  other arithmetic  17.5 us (1%)
    gather x2, local copies, waits for them, and re-layouts, shards(): basis[:, jnp.clip(lag_index - 1, 0, LAG - 1)]  1200 us
    all_gather x1, blocking collectives, shards(): lax.all_gather(stimulus, 'tm', axis=0, tiled=True)  62.4 us
    all_gather x1, waiting for transfers between devices, shards(): everyone = lax.all_gather(resid_bf, 'unit', axis=1, tiled=True)  52.2 us
  transfers between devices with their start and end apart: 6, of which 2 were waited for; matrix products, arithmetic and copies ran while one was open for 85% of the time, Pallas kernels for 0%

commit v1 on v0

v1 whole, which is shorter than its diff:
```python
import functools
import math

import jax
import jax.numpy as jnp
import numpy as np
from jax import lax
from jax.experimental import pallas as pl
from jax.experimental.pallas import tpu as pltpu
from jax.sharding import PartitionSpec as P

TILE = 128
FAN = 4
CAP = 2
NB = 10
LAG = 128
HALVES = (64, 64)
BF = jnp.bfloat16
F32 = jnp.float32
SMEM = pltpu.SMEM


def raised_cosine(count, lag):
    low = math.log(2.0)
    high = math.log(lag + 1.0)
    spacing = (high - low) / (count - 1)
    stretched = np.log(np.arange(1, lag + 1).astype(np.float64) + 1.0)
    centers = low + spacing * np.arange(count).astype(np.float64)
    phases = np.clip(
        (stretched[None, :] - centers[:, None]) * (math.pi / (2.0 * spacing)), -math.pi, math.pi
    )
    shapes = 0.5 * (1.0 + np.cos(phases))
    return (shapes / np.sum(shapes, axis=1, keepdims=True)).astype(np.float32).astype(BF)


def toeplitz():
    basis = raised_cosine(NB, LAG)
    lag = LAG + np.arange(LAG)[None, :] - np.arange(2 * LAG)[:, None]
    inside = (lag >= 1) & (lag <= LAG)
    blocks = np.where(inside[None], basis[:, np.clip(lag - 1, 0, LAG - 1)], np.zeros((), BF))
    return np.ascontiguousarray(blocks.transpose(1, 0, 2).reshape(2 * LAG, NB * LAG))


def contract(a, b, dims):
    return lax.dot_general(a, b, ((dims[:1], dims[1:]), ((), ())), preferred_element_type=F32)


def find_lowest(target, lowest, tiles_dev):
    for o in range(lowest.shape[0]):
        lowest[o] = 1 << 30
    for s in range(target.shape[0]):
        for f in range(FAN):
            t = target[s, f]
            o = lax.div(t, tiles_dev)
            lowest[o] = jnp.minimum(lowest[o], t)


def slot_of(target, lowest, s, f, tiles_dev):
    t = target[s, f]
    o = lax.div(t, tiles_dev)
    return o * CAP + (t != lowest[o]).astype(jnp.int32)


def mixing_filter(mix, toep, filt):
    total = jnp.zeros((2 * LAG, LAG), F32)
    for b in range(NB):
        total += mix[b] * toep[:, b * LAG : (b + 1) * LAG].astype(F32)
    high = total.astype(BF)
    filt[:, :LAG] = high
    filt[:, LAG:] = (total - high.astype(F32)).astype(BF)


def mix_window(window, filt):
    both = jnp.dot(window, filt, preferred_element_type=F32)
    return (both[:, :LAG] + both[:, LAG:]).astype(BF)


def add_partials(target, lowest, weight, mixed, total, out, tiles_dev):
    s = pl.program_id(0)
    for f in range(FAN):
        slot = slot_of(target, lowest, s, f, tiles_dev)
        total[slot] += contract(weight[0, f], mixed, (0, 0))

    @pl.when(s == pl.num_programs(0) - 1)
    def _():
        out[...] = total[...].astype(BF)


def late_kernel(target, mix, spikes, toep, weight, x_out, mixed_out, part, filt, total, lowest):
    tiles_dev = target.shape[0]

    @pl.when(pl.program_id(0) == 0)
    def _():
        find_lowest(target, lowest, tiles_dev)
        mixing_filter(mix, toep, filt)
        total[...] = jnp.zeros_like(total)

    x = spikes[...].astype(F32).T.astype(BF)
    x_out[0] = x
    filter_now = filt[...]
    blocks = [
        mix_window(x[:, k - LAG : k + LAG], filter_now) for k in range(LAG, x.shape[1], LAG)
    ]
    mixed = jnp.concatenate(blocks, axis=1)
    mixed_out[0] = mixed
    add_partials(target, lowest, weight, mixed, total, part, tiles_dev)


def early_kernel(
    target, mix, halo, x, toep, weight, halo_out, mixed_out, part, filt, total, lowest
):
    tiles_dev = target.shape[0]

    @pl.when(pl.program_id(0) == 0)
    def _():
        find_lowest(target, lowest, tiles_dev)
        mixing_filter(mix, toep, filt)
        total[...] = jnp.zeros_like(total)

    before = halo[...].astype(F32).T.astype(BF)
    halo_out[0] = before
    mixed = mix_window(jnp.concatenate([before, x[0]], axis=1), filt[...])
    mixed_out[0] = mixed
    add_partials(target, lowest, weight, mixed, total, part, tiles_dev)


def logit_kernel(x, halo, toep, hist_weight, bias, stim_filter, stimulus, out, rows):
    rows[...] = jnp.zeros_like(rows)
    rows[:NB] = hist_weight[...]
    rows[NB : NB + 1] = bias[...]
    columns = rows[...].T
    drive = contract(stim_filter[...], stimulus[...], (1, 1))
    start = drive + columns[:, NB : NB + 1]
    extended = jnp.concatenate([halo[0], x[0]], axis=1)
    for k in range(0, x.shape[2], LAG):
        history = jnp.dot(extended[:, k : k + 2 * LAG], toep[...], preferred_element_type=F32)
        total = start[:, k : k + LAG]
        for b in range(NB):
            total += columns[:, b : b + 1] * history[:, b * LAG : (b + 1) * LAG]
        out[0, :, k : k + LAG] = total


def resid_kernel(ids, late, early, logit, x, resid, send, total, rounded):
    total[...] = logit[...]
    for src in range(ids.shape[0]):
        for q in range(CAP):
            tile = ids[src, q]

            @pl.when(tile >= 0)
            def _():
                total[tile, :, :LAG] += early[src * CAP + q].astype(F32)
                total[tile, :, LAG:] += late[src * CAP + q].astype(F32)

    for j in range(logit.shape[0]):
        r = x[j].astype(F32) - jnp.exp(total[j])
        resid[j] = r
        rounded[j] = r.astype(BF)
    for dst in range(ids.shape[0]):
        for q in range(CAP):
            tile = ids[dst, q]

            @pl.when(tile >= 0)
            def _():
                send[dst * CAP + q] = rounded[tile]

            @pl.when(tile < 0)
            def _():
                send[dst * CAP + q] = jnp.zeros(send.shape[1:], BF)


def own_kernel(x, halo, toep, stimulus, resid_a, resid_b, stim_out, rows_out, rows):
    resid = jnp.concatenate([resid_a[0], resid_b[0]], axis=0)
    stim_out[...] = jnp.dot(resid.astype(BF), stimulus[...], preferred_element_type=F32)
    extended = jnp.concatenate([halo[0], x[0]], axis=1)
    totals = [jnp.zeros((TILE, LAG), F32) for _ in range(NB + 1)]
    for k in range(0, x.shape[2], LAG):
        history = jnp.dot(extended[:, k : k + 2 * LAG], toep[...], preferred_element_type=F32)
        piece = resid[:, k : k + LAG]
        for b in range(NB):
            totals[b] += piece * history[:, b * LAG : (b + 1) * LAG]
        totals[NB] += piece
    rows[...] = jnp.zeros_like(rows)
    for b in range(NB + 1):
        rows[b : b + 1] = jnp.sum(totals[b].T, axis=0, keepdims=True)
    rows_out[...] = rows[...]


def grad_kernel(target, recv, mixed_early, mixed_late, out, chosen, lowest):
    tiles_dev = target.shape[0]
    s = pl.program_id(0)

    @pl.when(s == 0)
    def _():
        find_lowest(target, lowest, tiles_dev)

    part = recv.shape[1]
    for f in range(FAN):
        chosen[f * part : (f + 1) * part] = recv[slot_of(target, lowest, s, f, tiles_dev)]
    mixed = jnp.concatenate([mixed_early[0], mixed_late[0]], axis=1)
    grads = contract(mixed, chosen[...], (1, 1)).astype(BF)
    out[...] = grads.reshape(out.shape)


def final_kernel(scale, *refs):
    parts, out = refs[:-1], refs[-1]
    sums = [jnp.sum(part[:, 0].astype(F32), axis=0) * scale for part in parts]
    for f in range(FAN):
        pieces = []
        for total in sums:
            wide = total.shape[1] // FAN
            pieces.append(total[:, f * wide : (f + 1) * wide])
        out[0, f] = jnp.concatenate(pieces, axis=1)


def call(kernel, name, **kw):
    limit = pltpu.CompilerParams(vmem_limit_bytes=40 << 20)
    return pl.pallas_call(kernel, name=name, compiler_params=limit, **kw)


def smem():
    return pl.BlockSpec(memory_space=SMEM)


def whole(shape, at=None):
    spot = at or (0,) * len(shape)
    return pl.BlockSpec(shape, lambda *_: spot)


def per_tile(shape, axis=0):
    return pl.BlockSpec(shape, lambda s: tuple(s if a == axis else 0 for a in range(len(shape))))


def struct(shape, dtype):
    return jax.ShapeDtypeStruct(shape, dtype)


def shards(
    spikes, stimulus, bias, hist_weight, stim_filter, coupling_mix, coupling_target, coupling_weight
):
    time_dev, units_dev = spikes.shape
    tiles_dev = units_dev // TILE
    unit_count = lax.axis_size("unit")
    time_count = lax.axis_size("tm")
    time_total = time_dev * time_count
    slots = unit_count * CAP
    late = time_dev - LAG
    toep = jnp.asarray(toeplitz())
    toep_spec = whole((2 * LAG, NB * LAG))

    tail = spikes[time_dev - LAG :].astype(BF)
    halo = lax.ppermute(tail, "tm", [(i, i + 1) for i in range(time_count - 1)])
    all_targets = lax.all_gather(coupling_target.reshape(-1), "unit", axis=0)

    part_scratch = lambda width: [
        pltpu.VMEM((2 * LAG, 2 * LAG), BF),
        pltpu.VMEM((slots, TILE, width), F32),
        SMEM((unit_count,), jnp.int32),
    ]
    weight_spec = per_tile((1, FAN, TILE, TILE))
    x, mixed_late, part_late = call(
        late_kernel,
        "late",
        grid=(tiles_dev,),
        in_specs=[smem(), smem(), per_tile((time_dev, TILE), 1), toep_spec, weight_spec],
        out_specs=[
            per_tile((1, TILE, time_dev)),
            per_tile((1, TILE, late)),
            whole((slots, TILE, late)),
        ],
        out_shape=[
            struct((tiles_dev, TILE, time_dev), BF),
            struct((tiles_dev, TILE, late), BF),
            struct((slots, TILE, late), BF),
        ],
        scratch_shapes=part_scratch(late),
    )(coupling_target, coupling_mix, spikes, toep, coupling_weight)
    got_late = lax.all_to_all(part_late, "unit", 0, 0, tiled=True)

    halo_t, mixed_early, part_early = call(
        early_kernel,
        "early",
        grid=(tiles_dev,),
        in_specs=[
            smem(),
            smem(),
            per_tile((LAG, TILE), 1),
            per_tile((1, TILE, LAG)),
            toep_spec,
            weight_spec,
        ],
        out_specs=[
            per_tile((1, TILE, LAG)),
            per_tile((1, TILE, LAG)),
            whole((slots, TILE, LAG)),
        ],
        out_shape=[
            struct((tiles_dev, TILE, LAG), BF),
            struct((tiles_dev, TILE, LAG), BF),
            struct((slots, TILE, LAG), BF),
        ],
        scratch_shapes=part_scratch(LAG),
    )(coupling_target, coupling_mix, halo, x, toep, coupling_weight)
    got_early = lax.all_to_all(part_early, "unit", 0, 0, tiled=True)

    x_spec = per_tile((1, TILE, time_dev))
    halo_spec = per_tile((1, TILE, LAG))
    stim_spec = whole(stimulus.shape)
    logit = call(
        logit_kernel,
        "logit",
        grid=(tiles_dev,),
        in_specs=[
            x_spec,
            halo_spec,
            toep_spec,
            per_tile((NB, TILE), 1),
            per_tile((1, TILE), 1),
            per_tile((TILE, stim_filter.shape[1])),
            stim_spec,
        ],
        out_specs=x_spec,
        out_shape=struct((tiles_dev, TILE, time_dev), F32),
        scratch_shapes=[pltpu.VMEM((TILE, TILE), F32)],
    )(x, halo_t, toep, hist_weight, bias.reshape(1, -1), stim_filter, stimulus)

    mine = lax.div(all_targets, tiles_dev) == lax.axis_index("unit")
    local = lax.rem(all_targets, tiles_dev)
    highest = jnp.max(jnp.where(mine, local, -1), axis=1)
    lowest = jnp.min(jnp.where(mine, local, tiles_dev), axis=1)
    ids = jnp.stack([jnp.where(highest < 0, -1, lowest), highest], axis=1)

    resids, grads = [], []
    first = 0
    for part in HALVES:
        at = (0, first // part, 0)
        resid, send = call(
            resid_kernel,
            "resid",
            grid=(1,),
            in_specs=[
                smem(),
                whole((slots, part, late), at),
                whole((slots, part, LAG), at),
                whole((tiles_dev, part, time_dev), at),
                whole((tiles_dev, part, time_dev), at),
            ],
            out_specs=[
                whole((tiles_dev, part, time_dev)),
                whole((slots, part, time_dev)),
            ],
            out_shape=[
                struct((tiles_dev, part, time_dev), F32),
                struct((slots, part, time_dev), BF),
            ],
            scratch_shapes=[
                pltpu.VMEM((tiles_dev, part, time_dev), F32),
                pltpu.VMEM((tiles_dev, part, time_dev), BF),
            ],
        )(ids, got_late, got_early, logit, x)
        resids.append(resid)
        got = lax.all_to_all(send, "unit", 0, 0, tiled=True)
        rows = TILE // time_count
        grad = call(
            grad_kernel,
            "grad",
            grid=(tiles_dev,),
            in_specs=[
                smem(),
                whole((slots, part, time_dev)),
                halo_spec,
                per_tile((1, TILE, late)),
            ],
            out_specs=per_tile((time_count, 1, rows, FAN * part), 1),
            out_shape=struct((time_count, tiles_dev, rows, FAN * part), BF),
            scratch_shapes=[
                pltpu.VMEM((FAN * part, time_dev), BF),
                SMEM((unit_count,), jnp.int32),
            ],
        )(coupling_target, got, mixed_early, mixed_late)
        grads.append(lax.all_to_all(grad, "tm", 0, 0, tiled=True))
        first += part

    stim_part, rows_part = call(
        own_kernel,
        "own",
        grid=(tiles_dev,),
        in_specs=[x_spec, halo_spec, toep_spec, stim_spec]
        + [per_tile((1, part, time_dev)) for part in HALVES],
        out_specs=[per_tile((TILE, stimulus.shape[1])), per_tile((16, TILE), 1)],
        out_shape=[
            struct((units_dev, stimulus.shape[1]), F32),
            struct((16, units_dev), F32),
        ],
        scratch_shapes=[pltpu.VMEM((16, TILE), F32)],
    )(x, halo_t, toep, stimulus, *resids)
    rows_total = lax.psum(rows_part, "tm")
    stim_got = lax.all_to_all(
        stim_part.reshape(time_count, units_dev // time_count, -1), "tm", 0, 0, tiled=True
    )
    grad_stim = jnp.sum(stim_got, axis=0) / time_total
    grad_bias = rows_total[NB] / time_total
    grad_hist = rows_total[:NB] / time_total

    rows = TILE // time_count
    grad_coupling = call(
        functools.partial(final_kernel, 1.0 / time_total),
        "final",
        grid=(tiles_dev,),
        in_specs=[per_tile((time_count, 1, rows, FAN * part), 1) for part in HALVES],
        out_specs=per_tile((1, FAN, rows, TILE)),
        out_shape=struct((tiles_dev, FAN, rows, TILE), F32),
    )(*grads)
    return (grad_bias, grad_hist, grad_stim, grad_coupling)


def solution(mesh):
    return jax.shard_map(
        shards,
        mesh=mesh,
        in_specs=(
            P("tm", "unit"),
            P("tm", None),
            P("unit"),
            P(None, "unit"),
            P("unit", None),
            P(),
            P("unit", None),
            P("unit", None, None, None),
        ),
        out_specs=(
            P("unit"),
            P(None, "unit"),
            P(("unit", "tm"), None),
            P("unit", None, "tm", None),
        ),
        check_vma=False,
    )
```

time: 1470 us -> 220 us (0.15)
  local copies, waits for them, and re-layouts: 1220 us -> 14.9 us
  matrix products: 42.4 us -> 0 us
  Pallas kernels: 0 us -> 38.9 us
  waiting for transfers between devices: 77.6 us -> 58.4 us
    gather x2 -> x0, local copies, waits for them, and re-layouts: 1200 us -> none  [shards(): basis[:, jnp.clip(lag_index - 1, 0, LAG - 1)]]
    all_gather x1 -> x0, waiting for transfers between devices: 52.2 us -> none  [shards(): everyone = lax.all_gather(resid_bf, 'unit', axis=1, tiled=True)]
    all_to_all x0 -> x3, blocking collectives: none -> 45.5 us  [the longest x1 19 us: shards(): got = lax.all_to_all(send, 'unit', 0, 0, tiled=True)]
    dot_general x8 -> x0, matrix products: 42.4 us -> none  [the longest x1 18.5 us: shards(): jnp.einsum('bkw,wu->bku', toeplitz, extended, preferred_element_type=jnp....]
    psum x0 -> x1, waiting for transfers between devices: none -> 39.7 us  [shards(): rows_total = lax.psum(rows_part, 'tm')]
    all_gather x1, blocking collectives: 62.4 us -> 22.9 us  [shards(): all_targets = lax.all_gather(coupling_target.reshape(-1), 'unit', axis=0)]
    pallas_call x0 -> x9, Pallas kernels: none -> 38.9 us  [the longest x2 9.17 us: shards(): call(grad_kernel, 'grad', grid=(tiles_dev,), in_specs=[smem(), whole((slo...]
    psum x1 -> x0, blocking collectives: 18.6 us -> none  [shards(): lax.psum((jnp.sum(resid, axis=0), jnp.sum(history_blocks * resid[None, :,...]
  transfers between devices with their start and end apart: 6 -> 6, of which waited for: 2 -> 3; matrix products, arithmetic and copies ran while one was open for 85% -> 3% of each run, Pallas kernels for 0% -> 10%
where the time goes in v1:
time: 220 us; the launch traced here: 219 us
  blocking collectives  68.4 us (31%)
  waiting for transfers between devices  58.4 us (27%)
  Pallas kernels  38.9 us (18%)
  starting transfers between devices  19.9 us (9%)
  local copies, waits for them, and re-layouts  14.9 us (7%)
  between operations  14.2 us (6%)
  other arithmetic  4.1 us (2%)
    psum x1, waiting for transfers between devices, shards(): rows_total = lax.psum(rows_part, 'tm')  39.7 us
    all_gather x1, blocking collectives, shards(): all_targets = lax.all_gather(coupling_target.reshape(-1), 'unit', axis=0)  22.9 us
    all_to_all x1, blocking collectives, shards(): got = lax.all_to_all(send, 'unit', 0, 0, tiled=True)  19 us
    unnamed x46, local copies, waits for them, and re-layouts  14.6 us
    all_to_all x1, blocking collectives, shards(): got_early = lax.all_to_all(part_early, 'unit', 0, 0, tiled=True)  13.5 us
    all_to_all x1, blocking collectives, shards(): lax.all_to_all(stim_part.reshape(time_count, units_dev // time_count, -1)...  13 us
    all_to_all x1, waiting for transfers between devices, shards(): got = lax.all_to_all(send, 'unit', 0, 0, tiled=True)  10.7 us
    pallas_call x2, Pallas kernels, shards(): call(grad_kernel, 'grad', grid=(tiles_dev,), in_specs=[smem(), whole((slo...  9.17 us
  transfers between devices with their start and end apart: 6, of which 3 were waited for; matrix products, arithmetic and copies ran while one was open for 3% of the time, Pallas kernels for 10%

profile of v1, /device:TPU:0, one launch (start us, length us, event | category | flops | bytes accessed | tf_op | source)
XLA Modules:
  0.0 218.8 jit_solution(9001990678781504388)
XLA Ops:
  8.2 4.9 %collective-permute-start = (bf16[128,1024]{1,0:T(8,128)(2,1)S(1)}, bf16[128,1024]{1,0:T(8,128)(2,1)S(1)}, u32[]{:S(2)}, u32[]{:S(2)}) collective-permute-start(bf16[128,1024]{1,0:T(8,128)(2,1)S(1)} %slice_convert_fusion), channel_id=1, source_target_pairs={{0,1},{1,2},{2,3},{4,5},{5,6},{6,7},{8,9},{9,10},{10,11},{12,13},{... | collective-permute-start | bytes 786440 | tf_op jit(solution)/shard_map/ppermute | solution.py:251
  16.3 1.6 copy-done.6
  18.5 6.8 %late.1 = (bf16[8,128,512]{2,1,0:T(8,128)(2,1)S(1)}, bf16[8,128,384]{2,1,0:T(8,128)(2,1)S(1)}, bf16[16,128,384]{2,1,0:T(8,128)(2,1)}) custom-call(s32[8,4]{1,0:T(8,128)S(1)} %copy.35.target, f32[10]{0:T(128)S(1)} %copy-done.17, s32[512,1024]{1,0:T(8,128)S(1)} %copy-done.6, bf16[256,1280]{1,0:T(8,128)(2,1)S(1)} %copy-done, bf16[8,4,128,128]{3,2,1,0:T(8,128)(2,1)S(1)} %copy-done.4), custom_call_target="tpu_custom_call" | custom-call | tf_op jit(solution)/shard_map/late/pallas_call | solution.py:260
  26.2 4.6 %early.1 = (bf16[8,128,128]{2,1,0:T(8,128)(2,1)S(1)}, bf16[8,128,128]{2,1,0:T(8,128)(2,1)S(1)}, bf16[16,128,128]{2,1,0:T(8,128)(2,1)S(1)}) custom-call(s32[8,4]{1,0:T(8,128)S(1)} %copy.35.target, f32[10]{0:T(128)S(1)} %copy-done.17, bf16[128,1024]{1,0:T(8,128)(2,1)S(1)} %collective-permute-done.halo, bf16[8,128,512]{2,1,0:T(8,128)(2,1)S(1)} %get-tuple-element.16.x, ...), custom_call_target="tpu_custom_call" | custom-call | tf_op jit(solution)/shard_map/early/pallas_call | solution.py:279
  31.5 13.5 %all_to_all.35.early = bf16[16,128,128]{2,1,0:T(8,128)(2,1)} all-to-all(bf16[16,128,128]{2,1,0:T(8,128)(2,1)S(1)} %get-tuple-element.19), channel_id=1, replica_groups=mesh['unit'=8,'tm'=4] {'unit'}, dimensions={0} | all-to-all | bytes 1048576 | tf_op jit(solution)/shard_map/all_to_all | solution.py:303
  45.0 4.4 %all-to-all-start = ((bf16[16,128,384]{2,1,0:T(8,128)(2,1)}), bf16[16,128,384]{2,1,0:T(8,128)(2,1)}, u32[]{:S(2)}, u32[]{:S(2)}) async-start(bf16[16,128,384]{2,1,0:T(8,128)(2,1)} %get-tuple-element.18), calls=%async_computation | async-start | bytes 3145728 | tf_op jit(solution)/shard_map/all_to_all | solution.py:277
  50.6 22.9 %all-gather = s32[8,1,32]{2,1,0:T(1,128)S(1)} all-gather(s32[1,1,32]{2,1,0:T(1,128)S(1)} %reshape.32), channel_id=1, replica_groups=mesh['unit'=8,'tm'=4] {'unit'}, dimensions={0}, use_global_device_ids=true | all-gather | bytes 1152 | tf_op jit(solution)/shard_map/all_gather | solution.py:252
  77.5 4.9 %logit.1 = f32[8,128,512]{2,1,0:T(8,128)S(1)} custom-call(bf16[8,128,512]{2,1,0:T(8,128)(2,1)S(1)} %get-tuple-element.16.x, bf16[8,128,128]{2,1,0:T(8,128)(2,1)S(1)} %copy-done.10, bf16[256,1280]{1,0:T(8,128)(2,1)S(1)} %copy-done.1, f32[10,1024]{1,0:T(8,128)S(1)} %copy-done.15, f32[1,1024]{1,0:T(1,128)S(1)} %bitcast.9, bf16[1024,64]{1,0:T(8,128)(2,1)S(1)} %copy-done.12, ...), custom_call_target="tpu_custom_call" | custom-call | tf_op jit(solution)/shard_map/logit/pallas_call | solution.py:308
  83.4 1.8 resid.3
  86.3 1.9 resid.2
  88.2 6.7 %own.1 = (f32[1024,64]{1,0:T(8,128)S(1)}, f32[16,1024]{1,0:T(8,128)}) custom-call(bf16[8,128,512]{2,1,0:T(8,128)(2,1)S(1)} %get-tuple-element.16.x, bf16[8,128,128]{2,1,0:T(8,128)(2,1)S(1)} %copy-done.11, bf16[256,1280]{1,0:T(8,128)(2,1)S(1)} %copy-done.2, bf16[512,64]{1,0:T(8,128)(2,1)S(1)} %copy.42.stimulus, f32[8,64,512]{2,1,0:T(8,128)S(1)} %get-tuple-element.20.resid_a, ...), custom_call_target="tpu_custom_call" | custom-call | tf_op jit(solution)/shard_map/own/pallas_call | solution.py:383
  95.1 13.0 %all_to_all.36 = f32[4,256,64]{1,2,0:T(8,128)S(1)} all-to-all(f32[4,256,64]{1,2,0:T(8,128)S(1)} %copy.43), channel_id=1, replica_groups=mesh['unit'=8,'tm'=4] {'tm'}, dimensions={0} | all-to-all | bytes 524288 | tf_op jit(solution)/shard_map/all_to_all | solution.py:397
  108.1 19.0 %all_to_all.37.recv = bf16[16,64,512]{2,1,0:T(8,128)(2,1)S(1)} all-to-all(bf16[16,64,512]{2,1,0:T(8,128)(2,1)} %copy-done.14), channel_id=1, replica_groups=mesh['unit'=8,'tm'=4] {'unit'}, dimensions={0} | all-to-all | bytes 2097152 | tf_op jit(solution)/shard_map/all_to_all | solution.py:361
  127.1 3.6 %all-to-all-start.3 = ((bf16[16,64,512]{2,1,0:T(8,128)(2,1)}), bf16[16,64,512]{2,1,0:T(8,128)(2,1)S(1)}, u32[]{:S(2)}, u32[]{:S(2)}) async-start(bf16[16,64,512]{2,1,0:T(8,128)(2,1)} %copy-done.13), calls=%async_computation.3 | async-start | bytes 2097152 | tf_op jit(solution)/shard_map/all_to_all | solution.py:361
  130.6 4.6 %grad.3 = bf16[4,8,32,256]{3,2,1,0:T(8,128)(2,1)} custom-call(s32[8,4]{1,0:T(8,128)S(1)} %copy.35.target, bf16[16,64,512]{2,1,0:T(8,128)(2,1)S(1)} %all_to_all.37.recv, bf16[8,128,128]{2,1,0:T(8,128)(2,1)S(1)} %get-tuple-element.25.mixed_early, bf16[8,128,384]{2,1,0:T(8,128)(2,1)S(1)} %copy-done.8), custom_call_target="tpu_custom_call" | custom-call | tf_op jit(solution)/shard_map/grad/pallas_call | solution.py:363
  135.2 10.7 %all-to-all-done.3.recv = bf16[16,64,512]{2,1,0:T(8,128)(2,1)S(1)} async-done(((bf16[16,64,512]{2,1,0:T(8,128)(2,1)}), bf16[16,64,512]{2,1,0:T(8,128)(2,1)S(1)}, u32[]{:S(2)}, u32[]{:S(2)}) %all-to-all-start.3) | async-done | bytes 1048608 | tf_op jit(solution)/shard_map/all_to_all | solution.py:361
  146.0 3.5 %all-to-all-start.6 = ((bf16[4,8,32,256]{3,2,1,0:T(8,128)(2,1)}), bf16[4,8,32,256]{3,2,1,0:T(8,128)(2,1)S(1)}, u32[]{:S(2)}, u32[]{:S(2)}) async-start(bf16[4,8,32,256]{3,2,1,0:T(8,128)(2,1)} %grad.3), calls=%async_computation.6 | async-start | bytes 1048576 | tf_op jit(solution)/shard_map/all_to_all | solution.py:380
  149.5 4.6 %grad.2 = bf16[4,8,32,256]{3,2,1,0:T(8,128)(2,1)} custom-call(s32[8,4]{1,0:T(8,128)S(1)} %copy.35.target, bf16[16,64,512]{2,1,0:T(8,128)(2,1)S(1)} %all-to-all-done.3.recv, bf16[8,128,128]{2,1,0:T(8,128)(2,1)S(1)} %get-tuple-element.25.mixed_early, bf16[8,128,384]{2,1,0:T(8,128)(2,1)S(1)} %copy-done.8), custom_call_target="tpu_custom_call" | custom-call | tf_op jit(solution)/shard_map/grad/pallas_call | solution.py:363
  154.0 7.3 %all-to-all-done.6.refs_1_ = bf16[4,8,32,256]{3,2,1,0:T(8,128)(2,1)S(1)} async-done(((bf16[4,8,32,256]{3,2,1,0:T(8,128)(2,1)}), bf16[4,8,32,256]{3,2,1,0:T(8,128)(2,1)S(1)}, u32[]{:S(2)}, u32[]{:S(2)}) %all-to-all-start.6) | async-done | bytes 524320 | tf_op jit(solution)/shard_map/all_to_all | solution.py:380
  161.3 3.5 %all-to-all-start.4 = ((bf16[4,8,32,256]{3,2,1,0:T(8,128)(2,1)}), bf16[4,8,32,256]{3,2,1,0:T(8,128)(2,1)S(1)}, u32[]{:S(2)}, u32[]{:S(2)}) async-start(bf16[4,8,32,256]{3,2,1,0:T(8,128)(2,1)} %grad.2), calls=%async_computation.4 | async-start | bytes 1048576 | tf_op jit(solution)/shard_map/all_to_all | solution.py:380
  165.5 39.7 %all-reduce.2.cloned.1.call-done = f32[16,1024]{1,0:T(8,128)} async-done(((f32[16,1024]{1,0:T(8,128)}), f32[16,1024]{1,0:T(8,128)}) %all-reduce.2.cloned.1.call-update) | async-done | bytes 65552 | tf_op jit(solution)/shard_map/psum | solution.py:396
  205.3 1.4 slice_multiply_fusion.1
  206.6 1.5 slice_multiply_fusion
  208.9 3.0 %final.1 = f32[8,4,32,128]{3,2,1,0:T(8,128)} custom-call(bf16[4,8,32,256]{3,2,1,0:T(8,128)(2,1)S(1)} %all-to-all-done.4.refs_0_, bf16[4,8,32,256]{3,2,1,0:T(8,128)(2,1)S(1)} %all-to-all-done.6.refs_1_), custom_call_target="tpu_custom_call" | custom-call | tf_op jit(solution)/shard_map/final/pallas_call | solution.py:405
  (58 shorter events, 15.3 us)
Async XLA Ops:
  8.2 18.0 %collective-permute-start = (bf16[128,1024]{1,0:T(8,128)(2,1)S(1)}, bf16[128,1024]{1,0:T(8,128)(2,1)S(1)}, u32[]{:S(2)}, u32[]{:S(2)}) collective-permute-start(bf16[128,1024]{1,0:T(8,128)(2,1)S(1)} %slice_convert_fusion), channel_id=1, source_target_pairs={{0,1},{1,2},{2,3},{4,5},{5,6},{6,7},{8,9},{9,10},{10,11},{12,13},{... | collective-permute-start | bytes 786440 | tf_op jit(solution)/shard_map/ppermute | solution.py:251
  14.0 1.1 copy-start
  15.0 1.2 copy-start.4
  16.3 1.6 copy-start.6
  18.5 7.7 %copy-start.5 = (bf16[8,4,128,128]{3,2,1,0:T(8,128)(2,1)S(1)}, bf16[8,4,128,128]{3,2,1,0:T(8,128)(2,1)}, u32[]{:S(2)}) copy-start(bf16[8,4,128,128]{3,2,1,0:T(8,128)(2,1)} %weight.3) | copy-start | bytes 3145732
  25.3 0.9 copy-start.7
  31.5 18.0 %copy-start.19 = (bf16[512,64]{0,1:T(8,128)(2,1)S(1)}, bf16[512,64]{0,1:T(8,128)(2,1)}, u32[]{:S(2)}) copy-start(bf16[512,64]{0,1:T(8,128)(2,1)} %param.10) | copy-start | bytes 196612
  31.5 18.2 %copy-start.18 = (bf16[1024,64]{0,1:T(8,128)(2,1)S(1)}, bf16[1024,64]{0,1:T(8,128)(2,1)}, u32[]{:S(2)}) copy-start(bf16[1024,64]{0,1:T(8,128)(2,1)} %param.13) | copy-start | bytes 393220
  45.0 28.6 %copy-start.16 = (f32[1024]{0:T(1024)S(1)}, f32[1024]{0:T(1024)}, u32[]{:S(2)}) copy-start(f32[1024]{0:T(1024)} %param.11) | copy-start | bytes 12292
  45.0 37.3 %all-to-all-start = ((bf16[16,128,384]{2,1,0:T(8,128)(2,1)}), bf16[16,128,384]{2,1,0:T(8,128)(2,1)}, u32[]{:S(2)}, u32[]{:S(2)}) async-start(bf16[16,128,384]{2,1,0:T(8,128)(2,1)} %get-tuple-element.18), calls=%async_computation | async-start | bytes 3145728 | tf_op jit(solution)/shard_map/all_to_all | solution.py:277
  73.7 1.1 copy-start.1
  74.8 0.9 copy-start.10
  75.7 0.9 copy-start.12
  76.7 0.8 copy-start.15
  82.4 1.0 copy-start.3
  85.3 1.0 copy-start.14
  86.3 2.0 copy-start.2
  86.3 2.0 copy-start.11
  88.2 6.7 %copy-start.13 = (bf16[16,64,512]{2,1,0:T(8,128)(2,1)}, bf16[16,64,512]{2,1,0:T(8,128)(2,1)S(1)}, u32[]{:S(2)}) copy-start(bf16[16,64,512]{2,1,0:T(8,128)(2,1)S(1)} %get-tuple-element.24) | copy-start | bytes 3145732
  108.1 22.5 %copy-start.8 = (bf16[8,128,384]{2,1,0:T(8,128)(2,1)S(1)}, bf16[8,128,384]{2,1,0:T(8,128)(2,1)}, u32[]{:S(2)}) copy-start(bf16[8,128,384]{2,1,0:T(8,128)(2,1)} %copy-done.7) | copy-start | bytes 2359300
  127.1 18.9 %all-to-all-start.3 = ((bf16[16,64,512]{2,1,0:T(8,128)(2,1)}), bf16[16,64,512]{2,1,0:T(8,128)(2,1)S(1)}, u32[]{:S(2)}, u32[]{:S(2)}) async-start(bf16[16,64,512]{2,1,0:T(8,128)(2,1)} %copy-done.13), calls=%async_computation.3 | async-start | bytes 2097152 | tf_op jit(solution)/shard_map/all_to_all | solution.py:361
  146.0 15.3 %all-to-all-start.6 = ((bf16[4,8,32,256]{3,2,1,0:T(8,128)(2,1)}), bf16[4,8,32,256]{3,2,1,0:T(8,128)(2,1)S(1)}, u32[]{:S(2)}, u32[]{:S(2)}) async-start(bf16[4,8,32,256]{3,2,1,0:T(8,128)(2,1)} %grad.3), calls=%async_computation.6 | async-start | bytes 1048576 | tf_op jit(solution)/shard_map/all_to_all | solution.py:380
  161.3 47.6 %all-to-all-start.4 = ((bf16[4,8,32,256]{3,2,1,0:T(8,128)(2,1)}), bf16[4,8,32,256]{3,2,1,0:T(8,128)(2,1)S(1)}, u32[]{:S(2)}, u32[]{:S(2)}) async-start(bf16[4,8,32,256]{3,2,1,0:T(8,128)(2,1)} %grad.2), calls=%async_computation.4 | async-start | bytes 1048576 | tf_op jit(solution)/shard_map/all_to_all | solution.py:380
  164.8 40.5 %all-reduce.2.cloned.1.call-start = ((), (), s32[]{:S(2)}) async-start(), calls=%async_computation.7 | async-start | bytes 131072 | tf_op jit(solution)/shard_map/psum | solution.py:396
  (2 other events, 1.4 us)
Sparse Core Ops, SparseCore 0:
  168.5 36.6 all-reduce.1

commit v2 on v1

--- a/solution.py
+++ b/solution.py
@@ -18,6 +18,9 @@
 BF = jnp.bfloat16
 F32 = jnp.float32
 SMEM = pltpu.SMEM
+VMEM_LIMIT = 40 << 20
+FLOPS_A_MICRO = 1.1e9
+HIST_ROWS = 16
 
 
 def raised_cosine(count, lag):
@@ -107,15 +110,24 @@
 
 
 def early_kernel(
-    target, mix, halo, x, toep, weight, halo_out, mixed_out, part, filt, total, lowest
+    target, mix, halo, x, toep, weight, kept, halo_out, mixed_out, part, named, filt, total, lowest
 ):
     tiles_dev = target.shape[0]
+    del kept
 
     @pl.when(pl.program_id(0) == 0)
     def _():
         find_lowest(target, lowest, tiles_dev)
         mixing_filter(mix, toep, filt)
         total[...] = jnp.zeros_like(total)
+
+        for o in range(lowest.shape[0]):
+            for q in range(CAP):
+                named[o * CAP + q] = -1
+        for s in range(tiles_dev):
+            for f in range(FAN):
+                slot = slot_of(target, lowest, s, f, tiles_dev)
+                named[slot] = lax.rem(target[s, f], tiles_dev)
 
     before = halo[...].astype(F32).T.astype(BF)
     halo_out[0] = before
@@ -140,24 +152,31 @@
         out[0, :, k : k + LAG] = total
 
 
-def resid_kernel(ids, late, early, logit, x, resid, send, total, rounded):
+def tile_at(ids, other, q, count):
+    me = lax.axis_index("unit")
+    return ids[jnp.bitwise_xor(me, other) * count * CAP + me * CAP + q]
+
+
+def resid_kernel(ids, got, logit, x, resid, send, total, rounded):
     total[...] = logit[...]
-    for src in range(ids.shape[0]):
+    count = got.shape[0] // CAP
+    late = got.shape[2] - LAG
+    for src in range(count):
         for q in range(CAP):
-            tile = ids[src, q]
+            tile = tile_at(ids, src, q, count)
 
             @pl.when(tile >= 0)
             def _():
-                total[tile, :, :LAG] += early[src * CAP + q].astype(F32)
-                total[tile, :, LAG:] += late[src * CAP + q].astype(F32)
+                total[tile, :, LAG:] += got[src * CAP + q, :, :late].astype(F32)
+                total[tile, :, :LAG] += got[src * CAP + q, :, late:].astype(F32)
 
     for j in range(logit.shape[0]):
         r = x[j].astype(F32) - jnp.exp(total[j])
         resid[j] = r
         rounded[j] = r.astype(BF)
-    for dst in range(ids.shape[0]):
+    for dst in range(count):
         for q in range(CAP):
-            tile = ids[dst, q]
+            tile = tile_at(ids, dst, q, count)
 
             @pl.when(tile >= 0)
             def _():
@@ -168,9 +187,26 @@
                 send[dst * CAP + q] = jnp.zeros(send.shape[1:], BF)
 
 
-def own_kernel(x, halo, toep, stimulus, resid_a, resid_b, stim_out, rows_out, rows):
+def peer(shift, count):
+    return lax.rem(lax.axis_index("tm") + shift, count)
+
+
+def own_kernel(x, halo, toep, stimulus, resid_a, resid_b, *refs):
+    outs, (wide, stim, sums) = refs[:-3], refs[-3:]
+    s = pl.program_id(0)
+    channels = stimulus.shape[1]
+    rows = sums.shape[0]
+
+    @pl.when(s == 0)
+    def _():
+        wide[...] = jnp.zeros_like(wide)
+        wide[:, :channels] = stimulus[...]
+        sums[...] = jnp.zeros_like(sums)
+
     resid = jnp.concatenate([resid_a[0], resid_b[0]], axis=0)
-    stim_out[...] = jnp.dot(resid.astype(BF), stimulus[...], preferred_element_type=F32)
+    stim[pl.ds(s * TILE, TILE)] = jnp.dot(
+        resid.astype(BF), wide[...], preferred_element_type=F32
+    )
     extended = jnp.concatenate([halo[0], x[0]], axis=1)
     totals = [jnp.zeros((TILE, LAG), F32) for _ in range(NB + 1)]
     for k in range(0, x.shape[2], LAG):
@@ -179,13 +215,41 @@
         for b in range(NB):
             totals[b] += piece * history[:, b * LAG : (b + 1) * LAG]
         totals[NB] += piece
-    rows[...] = jnp.zeros_like(rows)
+    lane = lax.broadcasted_iota(jnp.int32, (TILE, sums.shape[1]), 1)
+    first = channels + HIST_ROWS * lax.div(s * TILE, rows)
+    block = jnp.zeros((TILE, sums.shape[1]), F32)
     for b in range(NB + 1):
-        rows[b : b + 1] = jnp.sum(totals[b].T, axis=0, keepdims=True)
-    rows_out[...] = rows[...]
-
-
-def grad_kernel(target, recv, mixed_early, mixed_late, out, chosen, lowest):
+        column = jnp.sum(totals[b], axis=1, keepdims=True)
+        block = jnp.where(lane == first + b, column, block)
+    at = pl.ds(pl.multiple_of(lax.rem(s * TILE, rows), TILE), TILE)
+    sums[at] += block
+
+    @pl.when(s == pl.num_programs(0) - 1)
+    def _():
+        for shift, out in enumerate(outs):
+            first = pl.multiple_of(peer(shift, len(outs)) * rows, TILE)
+            out[...] = stim[pl.ds(first, rows)] + sums[...]
+
+
+def finish_kernel(scale, *refs):
+    parts, (bias_out, hist_out, stim_out) = refs[:-3], refs[-3:]
+    total = parts[0][...]
+    for part in parts[1:]:
+        total += part[...]
+    total *= scale
+    channels = stim_out.shape[1]
+    rows = total.shape[0]
+    stim_out[...] = total[:, :channels]
+    flat = total.T
+    for g in range(hist_out.shape[1] // rows):
+        first = channels + HIST_ROWS * g
+        at = slice(g * rows, (g + 1) * rows)
+        hist_out[:, at] = flat[first : first + NB]
+        bias_out[:, at] = flat[first + NB : first + NB + 1]
+
+
+def grad_kernel(target, recv, mixed_early, mixed_late, *refs):
+    outs, (chosen, grads, lowest) = refs[:-3], refs[-3:]
     tiles_dev = target.shape[0]
     s = pl.program_id(0)
 
@@ -197,13 +261,23 @@
     for f in range(FAN):
         chosen[f * part : (f + 1) * part] = recv[slot_of(target, lowest, s, f, tiles_dev)]
     mixed = jnp.concatenate([mixed_early[0], mixed_late[0]], axis=1)
-    grads = contract(mixed, chosen[...], (1, 1)).astype(BF)
-    out[...] = grads.reshape(out.shape)
-
-
-def final_kernel(scale, *refs):
+    grads[...] = contract(mixed, chosen[...], (1, 1))
+    rows = TILE // len(outs)
+    for shift, out in enumerate(outs):
+        first = pl.multiple_of(peer(shift, len(outs)) * rows, rows)
+        out[0] = grads[pl.ds(first, rows)].astype(out.dtype)
+
+
+def final_kernel(scale, halves, *refs):
     parts, out = refs[:-1], refs[-1]
-    sums = [jnp.sum(part[:, 0].astype(F32), axis=0) * scale for part in parts]
+    count = len(parts) // halves
+    sums = []
+    for half in range(halves):
+        mine = parts[half * count : (half + 1) * count]
+        total = mine[0][0].astype(F32)
+        for part in mine[1:]:
+            total += part[0].astype(F32)
+        sums.append(total * scale)
     for f in range(FAN):
         pieces = []
         for total in sums:
@@ -212,9 +286,30 @@
         out[0, f] = jnp.concatenate(pieces, axis=1)
 
 
-def call(kernel, name, **kw):
-    limit = pltpu.CompilerParams(vmem_limit_bytes=40 << 20)
-    return pl.pallas_call(kernel, name=name, compiler_params=limit, **kw)
+def to_peers(pieces):
+    count = len(pieces)
+    got = [pieces[0]]
+    for shift in range(1, count):
+        pairs = [(i, (i + shift) % count) for i in range(count)]
+        got.append(lax.ppermute(pieces[shift], "tm", pairs))
+    return got
+
+
+def gathered(value, axis):
+    step = 1
+    while step < lax.axis_size(axis):
+        pairs = [(i, i ^ step) for i in range(lax.axis_size(axis))]
+        value = jnp.concatenate([value, lax.ppermute(value, axis, pairs)])
+        step *= 2
+    return value
+
+
+def call(kernel, name, micros, **kw):
+    limit = pltpu.CompilerParams(vmem_limit_bytes=VMEM_LIMIT)
+    cost = pl.CostEstimate(
+        flops=int(micros * FLOPS_A_MICRO), bytes_accessed=1 << 20, transcendentals=0
+    )
+    return pl.pallas_call(kernel, name=name, compiler_params=limit, cost_estimate=cost, **kw)
 
 
 def smem():
@@ -239,6 +334,7 @@
 ):
     time_dev, units_dev = spikes.shape
     tiles_dev = units_dev // TILE
+    channels = stimulus.shape[1]
     unit_count = lax.axis_size("unit")
     time_count = lax.axis_size("tm")
     time_total = time_dev * time_count
@@ -249,7 +345,6 @@
 
     tail = spikes[time_dev - LAG :].astype(BF)
     halo = lax.ppermute(tail, "tm", [(i, i + 1) for i in range(time_count - 1)])
-    all_targets = lax.all_gather(coupling_target.reshape(-1), "unit", axis=0)
 
     part_scratch = lambda width: [
         pltpu.VMEM((2 * LAG, 2 * LAG), BF),
@@ -260,6 +355,7 @@
     x, mixed_late, part_late = call(
         late_kernel,
         "late",
+        5,
         grid=(tiles_dev,),
         in_specs=[smem(), smem(), per_tile((time_dev, TILE), 1), toep_spec, weight_spec],
         out_specs=[
@@ -270,15 +366,15 @@
         out_shape=[
             struct((tiles_dev, TILE, time_dev), BF),
             struct((tiles_dev, TILE, late), BF),
-            struct((slots, TILE, late), BF),
+            struct((slots, TILE, time_dev), BF),
         ],
         scratch_shapes=part_scratch(late),
     )(coupling_target, coupling_mix, spikes, toep, coupling_weight)
-    got_late = lax.all_to_all(part_late, "unit", 0, 0, tiled=True)
-
-    halo_t, mixed_early, part_early = call(
+
+    halo_t, mixed_early, partials, named = call(
         early_kernel,
         "early",
+        4,
         grid=(tiles_dev,),
         in_specs=[
             smem(),
@@ -287,20 +383,25 @@
             per_tile((1, TILE, LAG)),
             toep_spec,
             weight_spec,
+            pl.BlockSpec(memory_space=pl.ANY),
         ],
         out_specs=[
             per_tile((1, TILE, LAG)),
             per_tile((1, TILE, LAG)),
-            whole((slots, TILE, LAG)),
+            whole((slots, TILE, LAG), (0, 0, late // LAG)),
+            smem(),
         ],
         out_shape=[
             struct((tiles_dev, TILE, LAG), BF),
             struct((tiles_dev, TILE, LAG), BF),
-            struct((slots, TILE, LAG), BF),
+            struct((slots, TILE, time_dev), BF),
+            struct((slots,), jnp.int32),
         ],
         scratch_shapes=part_scratch(LAG),
-    )(coupling_target, coupling_mix, halo, x, toep, coupling_weight)
-    got_early = lax.all_to_all(part_early, "unit", 0, 0, tiled=True)
+        input_output_aliases={6: 2},
+    )(coupling_target, coupling_mix, halo, x, toep, coupling_weight, part_late)
+    got_partials = lax.all_to_all(partials, "unit", 0, 0, tiled=True)
+    ids = gathered(named, "unit")
 
     x_spec = per_tile((1, TILE, time_dev))
     halo_spec = per_tile((1, TILE, LAG))
@@ -308,6 +409,7 @@
     logit = call(
         logit_kernel,
         "logit",
+        5,
         grid=(tiles_dev,),
         in_specs=[
             x_spec,
@@ -315,7 +417,7 @@
             toep_spec,
             per_tile((NB, TILE), 1),
             per_tile((1, TILE), 1),
-            per_tile((TILE, stim_filter.shape[1])),
+            per_tile((TILE, channels)),
             stim_spec,
         ],
         out_specs=x_spec,
@@ -323,12 +425,7 @@
         scratch_shapes=[pltpu.VMEM((TILE, TILE), F32)],
     )(x, halo_t, toep, hist_weight, bias.reshape(1, -1), stim_filter, stimulus)
 
-    mine = lax.div(all_targets, tiles_dev) == lax.axis_index("unit")
-    local = lax.rem(all_targets, tiles_dev)
-    highest = jnp.max(jnp.where(mine, local, -1), axis=1)
-    lowest = jnp.min(jnp.where(mine, local, tiles_dev), axis=1)
-    ids = jnp.stack([jnp.where(highest < 0, -1, lowest), highest], axis=1)
-
+    rows = TILE // time_count
     resids, grads = [], []
     first = 0
     for part in HALVES:
@@ -336,11 +433,11 @@
         resid, send = call(
             resid_kernel,
             "resid",
+            2,
             grid=(1,),
             in_specs=[
                 smem(),
-                whole((slots, part, late), at),
-                whole((slots, part, LAG), at),
+                whole((slots, part, time_dev), at),
                 whole((tiles_dev, part, time_dev), at),
                 whole((tiles_dev, part, time_dev), at),
             ],
@@ -356,13 +453,13 @@
                 pltpu.VMEM((tiles_dev, part, time_dev), F32),
                 pltpu.VMEM((tiles_dev, part, time_dev), BF),
             ],
-        )(ids, got_late, got_early, logit, x)
+        )(ids, got_partials, logit, x)
         resids.append(resid)
         got = lax.all_to_all(send, "unit", 0, 0, tiled=True)
-        rows = TILE // time_count
-        grad = call(
+        pieces = call(
             grad_kernel,
             "grad",
+            4,
             grid=(tiles_dev,),
             in_specs=[
                 smem(),
@@ -370,47 +467,57 @@
                 halo_spec,
                 per_tile((1, TILE, late)),
             ],
-            out_specs=per_tile((time_count, 1, rows, FAN * part), 1),
-            out_shape=struct((time_count, tiles_dev, rows, FAN * part), BF),
+            out_specs=[per_tile((1, rows, FAN * part))] * time_count,
+            out_shape=[struct((tiles_dev, rows, FAN * part), BF)] * time_count,
             scratch_shapes=[
                 pltpu.VMEM((FAN * part, time_dev), BF),
+                pltpu.VMEM((TILE, FAN * part), F32),
                 SMEM((unit_count,), jnp.int32),
             ],
         )(coupling_target, got, mixed_early, mixed_late)
-        grads.append(lax.all_to_all(grad, "tm", 0, 0, tiled=True))
+        grads += to_peers(pieces)
         first += part
 
-    stim_part, rows_part = call(
+    own_rows = units_dev // time_count
+    wide = -(-(channels + HIST_ROWS * time_count) // TILE) * TILE
+    pieces = call(
         own_kernel,
         "own",
+        6,
         grid=(tiles_dev,),
         in_specs=[x_spec, halo_spec, toep_spec, stim_spec]
         + [per_tile((1, part, time_dev)) for part in HALVES],
-        out_specs=[per_tile((TILE, stimulus.shape[1])), per_tile((16, TILE), 1)],
+        out_specs=[whole((own_rows, wide))] * time_count,
+        out_shape=[struct((own_rows, wide), F32)] * time_count,
+        scratch_shapes=[
+            pltpu.VMEM((time_dev, wide), BF),
+            pltpu.VMEM((units_dev, wide), F32),
+            pltpu.VMEM((own_rows, wide), F32),
+        ],
+    )(x, halo_t, toep, stimulus, *resids)
+    grad_bias, grad_hist, grad_stim = call(
+        functools.partial(finish_kernel, 1.0 / time_total),
+        "finish",
+        1,
         out_shape=[
-            struct((units_dev, stimulus.shape[1]), F32),
-            struct((16, units_dev), F32),
-        ],
-        scratch_shapes=[pltpu.VMEM((16, TILE), F32)],
-    )(x, halo_t, toep, stimulus, *resids)
-    rows_total = lax.psum(rows_part, "tm")
-    stim_got = lax.all_to_all(
-        stim_part.reshape(time_count, units_dev // time_count, -1), "tm", 0, 0, tiled=True
-    )
-    grad_stim = jnp.sum(stim_got, axis=0) / time_total
-    grad_bias = rows_total[NB] / time_total
-    grad_hist = rows_total[:NB] / time_total
-
-    rows = TILE // time_count
+            struct((1, units_dev), F32),
+            struct((NB, units_dev), F32),
+            struct((own_rows, channels), F32),
+        ],
+    )(*to_peers(pieces))
+
     grad_coupling = call(
-        functools.partial(final_kernel, 1.0 / time_total),
+        functools.partial(final_kernel, 1.0 / time_total, len(HALVES)),
         "final",
+        2,
         grid=(tiles_dev,),
-        in_specs=[per_tile((time_count, 1, rows, FAN * part), 1) for part in HALVES],
+        in_specs=[
+            per_tile((1, rows, FAN * part)) for part in HALVES for _ in range(time_count)
+        ],
         out_specs=per_tile((1, FAN, rows, TILE)),
         out_shape=struct((tiles_dev, FAN, rows, TILE), F32),
     )(*grads)
-    return (grad_bias, grad_hist, grad_stim, grad_coupling)
+    return (grad_bias.reshape(-1), grad_hist, grad_stim, grad_coupling)
 
 
 def solution(mesh):

time: 220 us -> 145 us (0.66)
  blocking collectives: 68.4 us -> 0 us
  waiting for transfers between devices: 58.4 us -> 40 us
  starting transfers between devices: 19.9 us -> 34.5 us
  between operations: 14.2 us -> 0.84 us
  local copies, waits for them, and re-layouts: 14.9 us -> 27.6 us
  other arithmetic: 4.1 us -> 1.3 us
    all_to_all x3 -> x0, blocking collectives: 45.5 us -> none  [the longest x1 19 us: shards(): got = lax.all_to_all(send, 'unit', 0, 0, tiled=True)]
    psum x1 -> x0, waiting for transfers between devices: 39.7 us -> none  [shards(): rows_total = lax.psum(rows_part, 'tm')]
    ppermute x0 -> x12, waiting for transfers between devices: none -> 30.7 us  [the longest x3 22.1 us: gathered(): value = jnp.concatenate([value, lax.ppermute(value, axis, pairs)])]
    all_gather x1 -> x0, blocking collectives: 22.9 us -> none  [shards(): all_targets = lax.all_gather(coupling_target.reshape(-1), 'unit', axis=0)]
    ppermute x0 -> x12, starting transfers between devices: none -> 18.5 us  [the longest x9 14.7 us: to_peers(): got.append(lax.ppermute(pieces[shift], 'tm', pairs))]
    unnamed x46 -> x72, local copies, waits for them, and re-layouts: 14.6 us -> 27.6 us
    all_to_all x3 -> x1, starting transfers between devices: 11.4 us -> 3.85 us  [shards(): got_partials = lax.all_to_all(partials, 'unit', 0, 0, tiled=True)]
    all_to_all x3 -> x1, waiting for transfers between devices: 7.3 us -> 0.01 us  [shards(): got_partials = lax.all_to_all(partials, 'unit', 0, 0, tiled=True)]
  transfers between devices with their start and end apart: 6 -> 16, of which waited for: 3 -> 5; matrix products, arithmetic and copies ran while one was open for 3% -> 2% of each run, Pallas kernels for 10% -> 21%
where the time goes in v2:
time: 145 us; the launch traced here: 143 us
  waiting for transfers between devices  40 us (28%)
  Pallas kernels  39.2 us (27%)
  starting transfers between devices  34.5 us (24%)
  local copies, waits for them, and re-layouts  27.6 us (19%)
    unnamed x72, local copies, waits for them, and re-layouts  27.6 us
    ppermute x3, waiting for transfers between devices, gathered(): value = jnp.concatenate([value, lax.ppermute(value, axis, pairs)])  22.1 us
    ppermute x9, starting transfers between devices, to_peers(): got.append(lax.ppermute(pieces[shift], 'tm', pairs))  14.7 us
    all_to_all x2, waiting for transfers between devices, shards(): got = lax.all_to_all(send, 'unit', 0, 0, tiled=True)  9.23 us
    ppermute x9, waiting for transfers between devices, to_peers(): got.append(lax.ppermute(pieces[shift], 'tm', pairs))  8.66 us
    pallas_call x2, Pallas kernels, shards(): call(grad_kernel, 'grad', 4, grid=(tiles_dev,), in_specs=[smem(), whole((...  7.51 us
    all_to_all x2, starting transfers between devices, shards(): got = lax.all_to_all(send, 'unit', 0, 0, tiled=True)  7.11 us
    pallas_call x1, Pallas kernels, shards(): call(own_kernel, 'own', 6, grid=(tiles_dev,), in_specs=[x_spec, halo_spec...  6.53 us
  transfers between devices with their start and end apart: 16, of which 5 were waited for; matrix products, arithmetic and copies ran while one was open for 2% of the time, Pallas kernels for 21%

profile of v2, /device:TPU:0, one launch (start us, length us, event | category | flops | bytes accessed | tf_op | source)
XLA Modules:
  0.0 143.4 jit_solution(14029018364815925262)
XLA Ops:
  1.7 4.9 %collective-permute-start = (bf16[128,1024]{1,0:T(8,128)(2,1)S(1)}, bf16[128,1024]{1,0:T(8,128)(2,1)S(1)}, u32[]{:S(2)}, u32[]{:S(2)}) collective-permute-start(bf16[128,1024]{1,0:T(8,128)(2,1)S(1)} %slice_convert_fusion), channel_id=1, source_target_pairs={{0,1},{1,2},{2,3},{4,5},{5,6},{6,7},{8,9},{9,10},{10,11},{12,13},{... | collective-permute-start | bytes 786440 | tf_op jit(solution)/shard_map/ppermute | solution.py:347
  7.4 1.6 %copy-done.2 = s32[512,1024]{1,0:T(8,128)S(1)} copy-done((s32[512,1024]{1,0:T(8,128)S(1)}, s32[512,1024]{1,0:T(8,128)}, u32[]{:S(2)}) %copy-start.2) | copy-done | bytes 2097176
  12.0 5.9 %late.1 = (bf16[8,128,512]{2,1,0:T(8,128)(2,1)S(1)}, bf16[8,128,384]{2,1,0:T(8,128)(2,1)S(1)}, bf16[16,128,512]{2,1,0:T(8,128)(2,1)S(1)}) custom-call(s32[8,4]{1,0:T(8,128)S(1)} %copy.14.target, f32[10]{0:T(128)S(1)} %copy-done.7, s32[512,1024]{1,0:T(8,128)S(1)} %copy-done.2, bf16[256,1280]{1,0:T(8,128)(2,1)S(1)} %copy-done.8, ...), custom_call_target="tpu_custom_call" | custom-call | flops 5500000256 | bytes 1048576 | tf_op jit(solution)/shard_map/late/pallas_call | solution.py:355
  18.7 5.5 %early.1 = (bf16[8,128,128]{2,1,0:T(8,128)(2,1)S(1)}, bf16[8,128,128]{2,1,0:T(8,128)(2,1)S(1)}, bf16[16,128,512]{2,1,0:T(8,128)(2,1)S(1)}, s32[16]{0:T(128)S(1)}) custom-call(s32[8,4]{1,0:T(8,128)S(1)} %copy.14.target, f32[10]{0:T(128)S(1)} %copy-done.7, bf16[128,1024]{1,0:T(8,128)(2,1)S(1)} %collective-permute-done.halo, ...), custom_call_target="tpu_custom_call", output_to_operand_aliasing={{2}: (6, {})} | custom-call | flops 4400000000 | bytes 1048576 | tf_op jit(solution)/shard_map/early/pallas_call | solution.py:374
  26.4 3.9 %all-to-all-start = ((bf16[16,128,512]{2,1,0:T(8,128)(2,1)}), bf16[16,128,512]{2,1,0:T(8,128)(2,1)S(1)}, u32[]{:S(2)}, u32[]{:S(2)}) async-start(bf16[16,128,512]{2,1,0:T(8,128)(2,1)} %copy-done), calls=%async_computation | async-start | bytes 4194304 | tf_op jit(solution)/shard_map/all_to_all | solution.py:403
  31.6 1.9 %collective-permute-start.2 = (s32[32]{0:T(128)S(1)}, s32[32]{0:T(128)S(1)}, u32[]{:S(2)}, u32[]{:S(2)}) collective-permute-start(s32[32]{0:T(128)S(1)} %pad_add_fusion), channel_id=1, source_target_pairs={{0,8},{4,12},{8,0},{12,4},{16,24},{20,28},{24,16},{28,20},{1,9},{5... | collective-permute-start | bytes 392 | tf_op jit(solution)/shard_map/ppermute | solution.py:302
  34.5 21.4 %collective-permute-done.2 = s32[32]{0:T(128)S(1)} collective-permute-done((s32[32]{0:T(128)S(1)}, s32[32]{0:T(128)S(1)}, u32[]{:S(2)}, u32[]{:S(2)}) %collective-permute-start.2) | collective-permute-done | bytes 160 | tf_op jit(solution)/shard_map/ppermute | solution.py:302
  58.7 5.5 %logit.1 = f32[8,128,512]{2,1,0:T(8,128)S(1)} custom-call(bf16[8,128,512]{2,1,0:T(8,128)(2,1)S(1)} %copy-done.15, bf16[8,128,128]{2,1,0:T(8,128)(2,1)S(1)} %get-tuple-element.32.halo, bf16[256,1280]{1,0:T(8,128)(2,1)S(1)} %copy-done.9, f32[10,1024]{1,0:T(8,128)S(1)} %copy-done.5, f32[1,1024]{1,0:T(1,128)S(1)} %bitcast.2, ...), custom_call_target="tpu_custom_call" | custom-call | flops 5500000256 | bytes 1048576 | tf_op jit(solution)/shard_map/logit/pallas_call | solution.py:409
  65.7 1.6 %copy-done.12 = f32[8,128,512]{2,1,0:T(8,128)S(1)} copy-done((f32[8,128,512]{2,1,0:T(8,128)S(1)}, f32[8,128,512]{2,1,0:T(8,128)}, u32[]{:S(2)}) %copy-start.12) | copy-done | bytes 2097176
  71.8 3.6 %all-to-all-start.2 = ((bf16[16,64,512]{2,1,0:T(8,128)(2,1)}), bf16[16,64,512]{2,1,0:T(8,128)(2,1)S(1)}, u32[]{:S(2)}, u32[]{:S(2)}) async-start(bf16[16,64,512]{2,1,0:T(8,128)(2,1)} %copy-done.1), calls=%async_computation.2 | async-start | bytes 2097152 | tf_op jit(solution)/shard_map/all_to_all | solution.py:458
  78.2 2.3 %resid.2 = (f32[8,64,512]{2,1,0:T(8,128)S(1)}, bf16[16,64,512]{2,1,0:T(8,128)(2,1)}) custom-call(s32[128]{0:T(128)S(1)} %pad_add_fusion.2.ids, bf16[16,128,512]{2,1,0:T(8,128)(2,1)S(1)} %all-to-all-done.got, f32[8,128,512]{2,1,0:T(8,128)S(1)} %copy-done.13, bf16[8,128,512]{2,1,0:T(8,128)(2,1)S(1)} %copy-done.17), custom_call_target="tpu_custom_call" | custom-call | flops 2200000000 | bytes 1048576 | tf_op jit(solution)/shard_map/resid/pallas_call | solution.py:433
  81.4 9.2 %all-to-all-done.2.recv = bf16[16,64,512]{2,1,0:T(8,128)(2,1)S(1)} async-done(((bf16[16,64,512]{2,1,0:T(8,128)(2,1)}), bf16[16,64,512]{2,1,0:T(8,128)(2,1)S(1)}, u32[]{:S(2)}, u32[]{:S(2)}) %all-to-all-start.2) | async-done | bytes 1048608 | tf_op jit(solution)/shard_map/all_to_all | solution.py:458
  90.7 3.6 %all-to-all-start.1 = ((bf16[16,64,512]{2,1,0:T(8,128)(2,1)}), bf16[16,64,512]{2,1,0:T(8,128)(2,1)S(1)}, u32[]{:S(2)}, u32[]{:S(2)}) async-start(bf16[16,64,512]{2,1,0:T(8,128)(2,1)} %get-tuple-element.44), calls=%async_computation.1 | async-start | bytes 2097152 | tf_op jit(solution)/shard_map/all_to_all | solution.py:458
  97.8 6.5 %own.1 = (f32[256,128]{1,0:T(8,128)S(1)}, f32[256,128]{1,0:T(8,128)}, f32[256,128]{1,0:T(8,128)}, f32[256,128]{1,0:T(8,128)}) custom-call(bf16[8,128,512]{2,1,0:T(8,128)(2,1)S(1)} %copy-done.18, bf16[8,128,128]{2,1,0:T(8,128)(2,1)S(1)} %get-tuple-element.32.halo, bf16[256,1280]{1,0:T(8,128)(2,1)S(1)} %copy-done.10, bf16[512,64]{1,0:T(8,128)(2,1)S(1)} %copy.18.stimulus, ...), custom_call_target="tpu_custom_call" | custom-call | flops 6600000000 | bytes 1048576 | tf_op jit(solution)/shard_map/own/pallas_call | solution.py:483
  104.3 1.6 %collective-permute-start.4 = (f32[256,128]{1,0:T(8,128)}, f32[256,128]{1,0:T(8,128)S(1)}, u32[]{:S(2)}, u32[]{:S(2)}) collective-permute-start(f32[256,128]{1,0:T(8,128)} %get-tuple-element.38), channel_id=1, source_target_pairs={{0,1},{1,2},{2,3},{3,0},{4,5},{5,6},{6,7},{7,4},{8,9},{9,10},{10,1... | collective-permute-start | bytes 393224 | tf_op jit(solution)/shard_map/ppermute | solution.py:294
  107.0 2.9 %collective-permute-start.6 = (f32[256,128]{1,0:T(8,128)}, f32[256,128]{1,0:T(8,128)}, u32[]{:S(2)}, u32[]{:S(2)}) collective-permute-start(f32[256,128]{1,0:T(8,128)} %get-tuple-element.40), channel_id=1, source_target_pairs={{0,3},{1,0},{2,1},{3,2},{4,7},{5,4},{6,5},{7,6},{8,11},{9,8},{10,9... | collective-permute-start | bytes 393224 | tf_op jit(solution)/shard_map/ppermute | solution.py:294
  109.9 4.6 %grad.3 = (bf16[8,32,256]{2,1,0:T(8,128)(2,1)S(1)}, bf16[8,32,256]{2,1,0:T(8,128)(2,1)}, bf16[8,32,256]{2,1,0:T(8,128)(2,1)}, bf16[8,32,256]{2,1,0:T(8,128)(2,1)S(1)}) custom-call(s32[8,4]{1,0:T(8,128)S(1)} %copy.14.target, bf16[16,64,512]{2,1,0:T(8,128)(2,1)S(1)} %all-to-all-done.2.recv, bf16[8,128,128]{2,1,0:T(8,128)(2,1)S(1)} %copy-done.31, ...), custom_call_target="tpu_custom_call" | custom-call | flops 4400000000 | bytes 1048576 | tf_op jit(solution)/shard_map/grad/pallas_call | solution.py:459
  118.2 2.9 %grad.2 = (bf16[8,32,256]{2,1,0:T(8,128)(2,1)S(1)}, bf16[8,32,256]{2,1,0:T(8,128)(2,1)S(1)}, bf16[8,32,256]{2,1,0:T(8,128)(2,1)S(1)}, bf16[8,32,256]{2,1,0:T(8,128)(2,1)S(1)}) custom-call(s32[8,4]{1,0:T(8,128)S(1)} %copy.14.target, bf16[16,64,512]{2,1,0:T(8,128)(2,1)S(1)} %all-to-all-done.1.recv, bf16[8,128,128]{2,1,0:T(8,128)(2,1)S(1)} %copy-done.32, ...), custom_call_target="tpu_custom_call" | custom-call | flops 4400000000 | bytes 1048576 | tf_op jit(solution)/shard_map/grad/pallas_call | solution.py:459
  121.2 2.9 %collective-permute-start.12 = (bf16[8,32,256]{2,1,0:T(8,128)(2,1)S(1)}, bf16[8,32,256]{2,1,0:T(8,128)(2,1)S(1)}, u32[]{:S(2)}, u32[]{:S(2)}) collective-permute-start(bf16[8,32,256]{2,1,0:T(8,128)(2,1)S(1)} %get-tuple-element.55), channel_id=1, source_target_pairs={{0,3},{1,0},{2,1},{3,2},{4,7},{5,4},{6,5},{7,6},{8,11},{9,8},{10,9... | collective-permute-start | bytes 393224 | tf_op jit(solution)/shard_map/ppermute | solution.py:294
  126.2 3.2 %collective-permute-start.9 = (bf16[8,32,256]{2,1,0:T(8,128)(2,1)S(1)}, bf16[8,32,256]{2,1,0:T(8,128)(2,1)S(1)}, u32[]{:S(2)}, u32[]{:S(2)}) collective-permute-start(bf16[8,32,256]{2,1,0:T(8,128)(2,1)S(1)} %get-tuple-element.50), channel_id=1, source_target_pairs={{0,3},{1,0},{2,1},{3,2},{4,7},{5,4},{6,5},{7,6},{8,11},{9,8},{10,9... | collective-permute-start | bytes 393224 | tf_op jit(solution)/shard_map/ppermute | solution.py:294
  129.3 1.7 %finish.1 = (f32[1,1024]{1,0:T(1,128)}, f32[10,1024]{1,0:T(8,128)}, f32[256,64]{1,0:T(8,128)S(1)}) custom-call(f32[256,128]{1,0:T(8,128)S(1)} %copy-done.24, f32[256,128]{1,0:T(8,128)S(1)} %collective-permute-done.4.refs_1_, f32[256,128]{1,0:T(8,128)S(1)} %collective-permute-done.5.refs_2_, f32[256,128]{1,0:T(8,128)} %collective-permute-done.6.refs_3_), custom_call_target="tpu_custom_call" | custom-call | flops 1100000000 | bytes 1048576 | tf_op jit(solution)/shard_map/finish/pallas_call | solution.py:498
  131.7 3.0 %collective-permute-done.11.refs_6_ = bf16[8,32,256]{2,1,0:T(8,128)(2,1)S(1)} collective-permute-done((bf16[8,32,256]{2,1,0:T(8,128)(2,1)}, bf16[8,32,256]{2,1,0:T(8,128)(2,1)S(1)}, u32[]{:S(2)}, u32[]{:S(2)}) %collective-permute-start.11) | collective-permute-done | bytes 131104 | tf_op jit(solution)/shard_map/ppermute | solution.py:294
  134.8 5.6 %collective-permute-done.8.refs_2_ = bf16[8,32,256]{2,1,0:T(8,128)(2,1)S(1)} collective-permute-done((bf16[8,32,256]{2,1,0:T(8,128)(2,1)S(1)}, bf16[8,32,256]{2,1,0:T(8,128)(2,1)S(1)}, u32[]{:S(2)}, u32[]{:S(2)}) %collective-permute-start.8) | collective-permute-done | bytes 131104 | tf_op jit(solution)/shard_map/ppermute | solution.py:294
  140.4 3.0 %final.1 = f32[8,4,32,128]{3,2,1,0:T(8,128)} custom-call(bf16[8,32,256]{2,1,0:T(8,128)(2,1)S(1)} %get-tuple-element.47.refs_0_, bf16[8,32,256]{2,1,0:T(8,128)(2,1)S(1)} %collective-permute-done.7.refs_1_, bf16[8,32,256]{2,1,0:T(8,128)(2,1)S(1)} %collective-permute-done.8.refs_2_, bf16[8,32,256]{2,1,0:T(8,128)(2,1)S(1)} %collective-permute-done.9.refs_3_, ...), custom_call_target="tpu_custom_call" | custom-call | flops 2200000000 | bytes 1048576 | tf_op jit(solution)/shard_map/final/pallas_call | solution.py:509
  (94 shorter events, 33.8 us)
Async XLA Ops:
  1.7 17.0 %collective-permute-start = (bf16[128,1024]{1,0:T(8,128)(2,1)S(1)}, bf16[128,1024]{1,0:T(8,128)(2,1)S(1)}, u32[]{:S(2)}, u32[]{:S(2)}) collective-permute-start(bf16[128,1024]{1,0:T(8,128)(2,1)S(1)} %slice_convert_fusion), channel_id=1, source_target_pairs={{0,1},{1,2},{2,3},{4,5},{5,6},{6,7},{8,9},{9,10},{10,11},{12,13},{... | collective-permute-start | bytes 786440 | tf_op jit(solution)/shard_map/ppermute | solution.py:347
  26.3 31.1 %copy-start.5 = (f32[10,1024]{1,0:T(8,128)S(1)}, f32[10,1024]{1,0:T(8,128)}, u32[]{:S(2)}) copy-start(f32[10,1024]{1,0:T(8,128)} %hist_weight.1) | copy-start | bytes 122884
  26.3 31.1 %copy-start.6 = (f32[1024]{0:T(1024)S(1)}, f32[1024]{0:T(1024)}, u32[]{:S(2)}) copy-start(f32[1024]{0:T(1024)} %param.11) | copy-start | bytes 12292
  26.3 31.1 %copy-start.9 = (bf16[256,1280]{1,0:T(8,128)(2,1)S(1)}, bf16[256,1280]{1,0:T(8,128)(2,1)}, u32[]{:S(2)}) copy-start(bf16[256,1280]{1,0:T(8,128)(2,1)} %constant.2.clone.toep) | copy-start | bytes 1966084
  26.4 39.3 %all-to-all-start = ((bf16[16,128,512]{2,1,0:T(8,128)(2,1)}), bf16[16,128,512]{2,1,0:T(8,128)(2,1)S(1)}, u32[]{:S(2)}, u32[]{:S(2)}) async-start(bf16[16,128,512]{2,1,0:T(8,128)(2,1)} %copy-done), calls=%async_computation | async-start | bytes 4194304 | tf_op jit(solution)/shard_map/all_to_all | solution.py:403
  30.2 1.3 collective-permute-start.1
  31.6 24.3 %collective-permute-start.2 = (s32[32]{0:T(128)S(1)}, s32[32]{0:T(128)S(1)}, u32[]{:S(2)}, u32[]{:S(2)}) collective-permute-start(s32[32]{0:T(128)S(1)} %pad_add_fusion), channel_id=1, source_target_pairs={{0,8},{4,12},{8,0},{12,4},{16,24},{20,28},{24,16},{28,20},{1,9},{5... | collective-permute-start | bytes 392 | tf_op jit(solution)/shard_map/ppermute | solution.py:302
  56.0 9.6 %collective-permute-start.3 = (s32[64]{0:T(128)S(1)}, s32[64]{0:T(128)S(1)}, u32[]{:S(2)}, u32[]{:S(2)}) collective-permute-start(s32[64]{0:T(128)S(1)} %pad_add_fusion.1), channel_id=1, source_target_pairs={{0,16},{4,20},{8,24},{12,28},{16,0},{20,4},{24,8},{28,12},{1,17},{... | collective-permute-start | bytes 776 | tf_op jit(solution)/shard_map/ppermute | solution.py:302
  71.8 18.9 %all-to-all-start.2 = ((bf16[16,64,512]{2,1,0:T(8,128)(2,1)}), bf16[16,64,512]{2,1,0:T(8,128)(2,1)S(1)}, u32[]{:S(2)}, u32[]{:S(2)}) async-start(bf16[16,64,512]{2,1,0:T(8,128)(2,1)} %copy-done.1), calls=%async_computation.2 | async-start | bytes 2097152 | tf_op jit(solution)/shard_map/all_to_all | solution.py:458
  81.4 12.8 %copy-start.18 = (bf16[8,128,512]{2,1,0:T(8,128)(2,1)S(1)}, bf16[8,128,512]{2,1,0:T(8,128)(2,1)}, u32[]{:S(2)}) copy-start(bf16[8,128,512]{2,1,0:T(8,128)(2,1)} %copy-done.14) | copy-start | bytes 3145732
  90.7 25.5 %all-to-all-start.1 = ((bf16[16,64,512]{2,1,0:T(8,128)(2,1)}), bf16[16,64,512]{2,1,0:T(8,128)(2,1)S(1)}, u32[]{:S(2)}, u32[]{:S(2)}) async-start(bf16[16,64,512]{2,1,0:T(8,128)(2,1)} %get-tuple-element.44), calls=%async_computation.1 | async-start | bytes 2097152 | tf_op jit(solution)/shard_map/all_to_all | solution.py:458
  97.8 12.1 %copy-start.26 = (bf16[8,128,384]{2,1,0:T(8,128)(2,1)S(1)}, bf16[8,128,384]{2,1,0:T(8,128)(2,1)}, u32[]{:S(2)}) copy-start(bf16[8,128,384]{2,1,0:T(8,128)(2,1)} %copy-done.25) | copy-start | bytes 2359300
  97.8 12.1 %copy-start.31 = (bf16[8,128,128]{2,1,0:T(8,128)(2,1)S(1)}, bf16[8,128,128]{2,1,0:T(8,128)(2,1)}, u32[]{:S(2)}) copy-start(bf16[8,128,128]{2,1,0:T(8,128)(2,1)} %copy-done.30) | copy-start | bytes 786436
  104.3 16.8 %collective-permute-start.4 = (f32[256,128]{1,0:T(8,128)}, f32[256,128]{1,0:T(8,128)S(1)}, u32[]{:S(2)}, u32[]{:S(2)}) collective-permute-start(f32[256,128]{1,0:T(8,128)} %get-tuple-element.38), channel_id=1, source_target_pairs={{0,1},{1,2},{2,3},{3,0},{4,5},{5,6},{6,7},{7,4},{8,9},{9,10},{10,1... | collective-permute-start | bytes 393224 | tf_op jit(solution)/shard_map/ppermute | solution.py:294
  105.9 18.1 %collective-permute-start.5 = (f32[256,128]{1,0:T(8,128)}, f32[256,128]{1,0:T(8,128)S(1)}, u32[]{:S(2)}, u32[]{:S(2)}) collective-permute-start(f32[256,128]{1,0:T(8,128)} %get-tuple-element.39), channel_id=1, source_target_pairs={{0,2},{1,3},{2,0},{3,1},{4,6},{5,7},{6,4},{7,5},{8,10},{9,11},{10,... | collective-permute-start | bytes 393224 | tf_op jit(solution)/shard_map/ppermute | solution.py:294
  107.0 17.7 %collective-permute-start.6 = (f32[256,128]{1,0:T(8,128)}, f32[256,128]{1,0:T(8,128)}, u32[]{:S(2)}, u32[]{:S(2)}) collective-permute-start(f32[256,128]{1,0:T(8,128)} %get-tuple-element.40), channel_id=1, source_target_pairs={{0,3},{1,0},{2,1},{3,2},{4,7},{5,4},{6,5},{7,6},{8,11},{9,8},{10,9... | collective-permute-start | bytes 393224 | tf_op jit(solution)/shard_map/ppermute | solution.py:294
  115.1 11.1 %collective-permute-start.10 = (bf16[8,32,256]{2,1,0:T(8,128)(2,1)}, bf16[8,32,256]{2,1,0:T(8,128)(2,1)S(1)}, u32[]{:S(2)}, u32[]{:S(2)}) collective-permute-start(bf16[8,32,256]{2,1,0:T(8,128)(2,1)} %get-tuple-element.53), channel_id=1, source_target_pairs={{0,1},{1,2},{2,3},{3,0},{4,5},{5,6},{6,7},{7,4},{8,9},{9,10},{10,1... | collective-permute-start | bytes 393224 | tf_op jit(solution)/shard_map/ppermute | solution.py:294
  115.1 14.2 %copy-start.24 = (f32[256,128]{1,0:T(8,128)S(1)}, f32[256,128]{1,0:T(8,128)}, u32[]{:S(2)}) copy-start(f32[256,128]{1,0:T(8,128)} %copy-done.23) | copy-start | bytes 393220
  115.1 19.7 %collective-permute-start.11 = (bf16[8,32,256]{2,1,0:T(8,128)(2,1)}, bf16[8,32,256]{2,1,0:T(8,128)(2,1)S(1)}, u32[]{:S(2)}, u32[]{:S(2)}) collective-permute-start(bf16[8,32,256]{2,1,0:T(8,128)(2,1)} %get-tuple-element.54), channel_id=1, source_target_pairs={{0,2},{1,3},{2,0},{3,1},{4,6},{5,7},{6,4},{7,5},{8,10},{9,11},{10,... | collective-permute-start | bytes 393224 | tf_op jit(solution)/shard_map/ppermute | solution.py:294
  121.2 13.6 %collective-permute-start.12 = (bf16[8,32,256]{2,1,0:T(8,128)(2,1)S(1)}, bf16[8,32,256]{2,1,0:T(8,128)(2,1)S(1)}, u32[]{:S(2)}, u32[]{:S(2)}) collective-permute-start(bf16[8,32,256]{2,1,0:T(8,128)(2,1)S(1)} %get-tuple-element.55), channel_id=1, source_target_pairs={{0,3},{1,0},{2,1},{3,2},{4,7},{5,4},{6,5},{7,6},{8,11},{9,8},{10,9... | collective-permute-start | bytes 393224 | tf_op jit(solution)/shard_map/ppermute | solution.py:294
  124.1 10.7 %collective-permute-start.7 = (bf16[8,32,256]{2,1,0:T(8,128)(2,1)S(1)}, bf16[8,32,256]{2,1,0:T(8,128)(2,1)S(1)}, u32[]{:S(2)}, u32[]{:S(2)}) collective-permute-start(bf16[8,32,256]{2,1,0:T(8,128)(2,1)S(1)} %get-tuple-element.48), channel_id=1, source_target_pairs={{0,1},{1,2},{2,3},{3,0},{4,5},{5,6},{6,7},{7,4},{8,9},{9,10},{10,1... | collective-permute-start | bytes 393224 | tf_op jit(solution)/shard_map/ppermute | solution.py:294
  124.7 15.7 %collective-permute-start.8 = (bf16[8,32,256]{2,1,0:T(8,128)(2,1)S(1)}, bf16[8,32,256]{2,1,0:T(8,128)(2,1)S(1)}, u32[]{:S(2)}, u32[]{:S(2)}) collective-permute-start(bf16[8,32,256]{2,1,0:T(8,128)(2,1)S(1)} %get-tuple-element.49), channel_id=1, source_target_pairs={{0,2},{1,3},{2,0},{3,1},{4,6},{5,7},{6,4},{7,5},{8,10},{9,11},{10,... | collective-permute-start | bytes 393224 | tf_op jit(solution)/shard_map/ppermute | solution.py:294
  126.2 14.2 %collective-permute-start.9 = (bf16[8,32,256]{2,1,0:T(8,128)(2,1)S(1)}, bf16[8,32,256]{2,1,0:T(8,128)(2,1)S(1)}, u32[]{:S(2)}, u32[]{:S(2)}) collective-permute-start(bf16[8,32,256]{2,1,0:T(8,128)(2,1)S(1)} %get-tuple-element.50), channel_id=1, source_target_pairs={{0,3},{1,0},{2,1},{3,2},{4,7},{5,4},{6,5},{7,6},{8,11},{9,8},{10,9... | collective-permute-start | bytes 393224 | tf_op jit(solution)/shard_map/ppermute | solution.py:294
  129.3 11.1 %copy-start.29 = (bf16[8,32,256]{2,1,0:T(8,128)(2,1)S(1)}, bf16[8,32,256]{2,1,0:T(8,128)(2,1)}, u32[]{:S(2)}) copy-start(bf16[8,32,256]{2,1,0:T(8,128)(2,1)} %copy-done.28) | copy-start | bytes 393220
  (26 other events, 51.7 us)

commit v3 on v2

v3 whole, which is shorter than its diff:
```python
import functools
import math

import jax
import jax.numpy as jnp
import numpy as np
from jax import lax
from jax.experimental import pallas as pl
from jax.experimental.pallas import tpu as pltpu
from jax.sharding import PartitionSpec as P

TILE = 128
FAN = 4
CAP = 2
NB = 10
LAG = 128
HALVES = (64, 64)
BF = jnp.bfloat16
F32 = jnp.float32
SMEM = pltpu.SMEM
VMEM_LIMIT = 20 << 20
FLOPS_A_MICRO = 1.1e9
HIST_ROWS = 16
NAME_ROWS = 16


def raised_cosine(count, lag):
    low = math.log(2.0)
    high = math.log(lag + 1.0)
    spacing = (high - low) / (count - 1)
    stretched = np.log(np.arange(1, lag + 1).astype(np.float64) + 1.0)
    centers = low + spacing * np.arange(count).astype(np.float64)
    phases = np.clip(
        (stretched[None, :] - centers[:, None]) * (math.pi / (2.0 * spacing)), -math.pi, math.pi
    )
    shapes = 0.5 * (1.0 + np.cos(phases))
    return (shapes / np.sum(shapes, axis=1, keepdims=True)).astype(np.float32).astype(BF)


def toeplitz():
    basis = raised_cosine(NB, LAG)
    lag = LAG + np.arange(LAG)[None, :] - np.arange(2 * LAG)[:, None]
    inside = (lag >= 1) & (lag <= LAG)
    blocks = np.where(inside[None], basis[:, np.clip(lag - 1, 0, LAG - 1)], np.zeros((), BF))
    return np.ascontiguousarray(blocks.transpose(1, 0, 2).reshape(2 * LAG, NB * LAG))


def contract(a, b, dims):
    return lax.dot_general(a, b, ((dims[:1], dims[1:]), ((), ())), preferred_element_type=F32)


def find_lowest(target, lowest, tiles_dev):
    for o in range(lowest.shape[0]):
        lowest[o] = 1 << 30
    for s in range(target.shape[0]):
        for f in range(FAN):
            t = target[s, f]
            o = lax.div(t, tiles_dev)
            lowest[o] = jnp.minimum(lowest[o], t)


def slot_of(target, lowest, s, f, tiles_dev):
    t = target[s, f]
    o = lax.div(t, tiles_dev)
    return o * CAP + (t != lowest[o]).astype(jnp.int32)


def mixing_filter(mix, toep, filt):
    total = jnp.zeros((2 * LAG, LAG), F32)
    for b in range(NB):
        total += mix[b] * toep[:, b * LAG : (b + 1) * LAG].astype(F32)
    high = total.astype(BF)
    filt[:, :LAG] = high
    filt[:, LAG:] = (total - high.astype(F32)).astype(BF)


def mix_window(window, filt):
    both = jnp.dot(window, filt, preferred_element_type=F32)
    return (both[:, :LAG] + both[:, LAG:]).astype(BF)


def add_partials(target, lowest, turned, mixed, total, tiles_dev):
    total[...] = jnp.zeros_like(total)
    for s in range(tiles_dev):
        products = jnp.dot(turned[s], mixed[s], preferred_element_type=F32)
        for f in range(FAN):
            slot = slot_of(target, lowest, s, f, tiles_dev)
            total[slot] += products[f * TILE : (f + 1) * TILE]


def late_kernel(target, mix, spikes, weight, toep, *refs):
    x, mixed, part, tail, filt, turned = refs[:6]
    counts, weights, bases, total, lowest, highest, sems = refs[6:]
    tiles_dev = target.shape[0]
    blocks = x.shape[2] // LAG
    pulls = [
        pltpu.make_async_copy(toep, bases, sems.at[0]),
        pltpu.make_async_copy(weight, weights, sems.at[1]),
    ]
    for k in range(blocks):
        at = pl.ds(k * LAG, LAG)
        pulls.append(pltpu.make_async_copy(spikes.at[at], counts.at[at], sems.at[2 + k]))
    for pull in pulls:
        pull.start()

    find_lowest(target, lowest, tiles_dev)
    for o in range(highest.shape[0]):
        highest[o] = -1
    for s in range(tiles_dev):
        for f in range(FAN):
            t = target[s, f]
            o = lax.div(t, tiles_dev)
            highest[o] = jnp.maximum(highest[o], lax.rem(t, tiles_dev))

    pulls[0].wait()
    mixing_filter(mix, bases, filt)
    before = None
    for k in range(blocks):
        pulls[2 + k].wait()
        now = counts[k * LAG : (k + 1) * LAG].astype(F32).T.astype(BF)
        x[:, :, k * LAG : (k + 1) * LAG] = now.reshape(tiles_dev, TILE, LAG)
        if k:
            got = mix_window(jnp.concatenate([before, now], axis=1), filt[...])
            mixed[:, :, (k - 1) * LAG : k * LAG] = got.reshape(tiles_dev, TILE, LAG)
        before = now
    tail[...] = before.reshape(tiles_dev, TILE, LAG)

    pulls[1].wait()
    for s in range(tiles_dev):
        for f in range(FAN):
            turned[s, f * TILE : (f + 1) * TILE] = weights[s, f].astype(F32).T.astype(BF)
    add_partials(target, lowest, turned, mixed, total, tiles_dev)

    row = lax.broadcasted_iota(jnp.int32, (NAME_ROWS, part.shape[2]), 0)
    for o in range(part.shape[0]):
        high = highest[o]
        low = jnp.where(high < 0, -1, lax.rem(lowest[o], tiles_dev))
        for q in range(CAP):
            part[o, q * TILE : (q + 1) * TILE] = total[o * CAP + q].astype(BF)
        names = jnp.where(row == 0, low, jnp.where(row == 1, high, 0))
        part[o, CAP * TILE :] = names.astype(F32).astype(BF)


def early_kernel(target, halo, x, filt, turned, mixed_out, *refs):
    outs, (total, lowest) = refs[:-2], refs[-2:]
    tiles_dev = target.shape[0]
    units = x.shape[0] * TILE
    find_lowest(target, lowest, tiles_dev)
    window = jnp.concatenate(
        [halo[...].reshape(units, LAG), x[:, :, :LAG].reshape(units, LAG)], axis=1
    )
    mixed_out[...] = mix_window(window, filt[...]).reshape(mixed_out.shape)
    add_partials(target, lowest, turned, mixed_out, total, tiles_dev)
    me = lax.axis_index("unit")
    for k, out in enumerate(outs):
        for q in range(CAP):
            out[q] = total[jnp.bitwise_xor(me, k) * CAP + q].astype(BF)


def names_kernel(got, ids):
    for src in range(got.shape[0]):
        block = got[src].astype(F32)
        for q in range(CAP):
            ids[src * CAP + q] = jnp.max(block[q : q + 1]).astype(jnp.int32)


def logit_kernel(x, halo, toep, hist_weight, bias, stim_filter, stimulus, out, rows):
    rows[...] = jnp.zeros_like(rows)
    rows[:NB] = hist_weight[...]
    rows[NB : NB + 1] = bias[...]
    columns = rows[...].T
    drive = contract(stim_filter[...], stimulus[...], (1, 1))
    start = drive + columns[:, NB : NB + 1]
    extended = jnp.concatenate([halo[0], x[0]], axis=1)
    for k in range(0, x.shape[2], LAG):
        history = jnp.dot(extended[:, k : k + 2 * LAG], toep[...], preferred_element_type=F32)
        total = start[:, k : k + LAG]
        for b in range(NB):
            total += columns[:, b : b + 1] * history[:, b * LAG : (b + 1) * LAG]
        out[0, :, k : k + LAG] = total


def resid_kernel(first, ids, late, logit, x, *refs):
    early, (resid, send, total, rounded) = refs[:-4], refs[-4:]
    part = resid.shape[1]
    mine = slice(first, first + part)
    me = lax.axis_index("unit")
    total[...] = logit[:, mine]
    count = late.shape[0]
    for k in range(count):
        for q in range(CAP):
            tile = ids[k * CAP + q]

            @pl.when(tile >= 0)
            def _():
                start = q * TILE + first
                total[tile, :, LAG:] += late[k, start : start + part].astype(F32)

            other = ids[jnp.bitwise_xor(me, k) * CAP + q]

            @pl.when(other >= 0)
            def _():
                total[other, :, :LAG] += early[k][q, mine].astype(F32)

    for j in range(logit.shape[0]):
        r = x[j, mine].astype(F32) - jnp.exp(total[j])
        resid[j] = r
        rounded[j] = r.astype(BF)
    for dst in range(count):
        for q in range(CAP):
            tile = ids[dst * CAP + q]

            @pl.when(tile >= 0)
            def _():
                send[dst * CAP + q] = rounded[tile]

            @pl.when(tile < 0)
            def _():
                send[dst * CAP + q] = jnp.zeros(send.shape[1:], BF)


def peer(shift, count):
    return lax.rem(lax.axis_index("tm") + shift, count)


def own_kernel(x, halo, toep, stimulus, resid_a, resid_b, kept, *refs):
    outs, (passed, wide, stim, sums) = refs[:-4], refs[-4:]
    del kept, passed
    s = pl.program_id(0)
    channels = stimulus.shape[1]
    rows = sums.shape[0]

    @pl.when(s == 0)
    def _():
        wide[...] = jnp.zeros_like(wide)
        wide[:, :channels] = stimulus[...]
        sums[...] = jnp.zeros_like(sums)

    resid = jnp.concatenate([resid_a[0], resid_b[0]], axis=0)
    stim[pl.ds(s * TILE, TILE)] = jnp.dot(
        resid.astype(BF), wide[...], preferred_element_type=F32
    )
    extended = jnp.concatenate([halo[0], x[0]], axis=1)
    totals = [jnp.zeros((TILE, LAG), F32) for _ in range(NB + 1)]
    for k in range(0, x.shape[2], LAG):
        history = jnp.dot(extended[:, k : k + 2 * LAG], toep[...], preferred_element_type=F32)
        piece = resid[:, k : k + LAG]
        for b in range(NB):
            totals[b] += piece * history[:, b * LAG : (b + 1) * LAG]
        totals[NB] += piece
    lane = lax.broadcasted_iota(jnp.int32, (TILE, sums.shape[1]), 1)
    first = channels + HIST_ROWS * lax.div(s * TILE, rows)
    block = jnp.zeros((TILE, sums.shape[1]), F32)
    for b in range(NB + 1):
        column = jnp.sum(totals[b], axis=1, keepdims=True)
        block = jnp.where(lane == first + b, column, block)
    at = pl.ds(pl.multiple_of(lax.rem(s * TILE, rows), TILE), TILE)
    sums[at] += block

    @pl.when(s == pl.num_programs(0) - 1)
    def _():
        for shift, out in enumerate(outs):
            first = pl.multiple_of(peer(shift, len(outs)) * rows, TILE)
            out[...] = stim[pl.ds(first, rows)] + sums[...]


def finish_kernel(scale, *refs):
    parts, (bias_out, hist_out, stim_out) = refs[:-3], refs[-3:]
    total = parts[0][...]
    for part in parts[1:]:
        total += part[...]
    total *= scale
    channels = stim_out.shape[1]
    rows = total.shape[0]
    stim_out[...] = total[:, :channels]
    flat = total.T
    for g in range(hist_out.shape[1] // rows):
        first = channels + HIST_ROWS * g
        at = slice(g * rows, (g + 1) * rows)
        hist_out[:, at] = flat[first : first + NB]
        bias_out[:, at] = flat[first + NB : first + NB + 1]


def grad_kernel(target, recv, mixed_early, mixed_late, *refs):
    outs, (chosen, grads, lowest) = refs[:-3], refs[-3:]
    tiles_dev = target.shape[0]
    find_lowest(target, lowest, tiles_dev)
    part = recv.shape[1]
    rows = TILE // len(outs)
    for s in range(tiles_dev):
        for f in range(FAN):
            slot = slot_of(target, lowest, s, f, tiles_dev)
            chosen[s, f * part : (f + 1) * part] = recv[slot]
        mixed = jnp.concatenate([mixed_early[s], mixed_late[s]], axis=1)
        grads[s] = contract(mixed, chosen[s], (1, 1))
    for shift, out in enumerate(outs):
        first = pl.multiple_of(peer(shift, len(outs)) * rows, rows)
        out[...] = grads[:, pl.ds(first, rows)].astype(out.dtype)


def final_kernel(scale, halves, *refs):
    parts, out = refs[:-1], refs[-1]
    count = len(parts) // halves
    sums = []
    for half in range(halves):
        mine = parts[half * count : (half + 1) * count]
        total = mine[0][...].astype(F32)
        for part in mine[1:]:
            total += part[...].astype(F32)
        sums.append(total * scale)
    for f in range(FAN):
        pieces = []
        for total in sums:
            wide = total.shape[2] // FAN
            pieces.append(total[:, :, f * wide : (f + 1) * wide])
        out[:, f] = jnp.concatenate(pieces, axis=2)


def to_peers(pieces):
    count = len(pieces)
    got = [pieces[0]]
    for shift in range(1, count):
        pairs = [(i, (i + shift) % count) for i in range(count)]
        got.append(lax.ppermute(pieces[shift], "tm", pairs))
    return got


def to_units(pieces):
    got = [pieces[0]]
    for k in range(1, len(pieces)):
        got.append(lax.ppermute(pieces[k], "unit", [(i, i ^ k) for i in range(len(pieces))]))
    return got


def call(kernel, name, micros, **kw):
    limit = pltpu.CompilerParams(vmem_limit_bytes=VMEM_LIMIT)
    cost = pl.CostEstimate(
        flops=int(micros * FLOPS_A_MICRO), bytes_accessed=1 << 20, transcendentals=0
    )
    return pl.pallas_call(kernel, name=name, compiler_params=limit, cost_estimate=cost, **kw)


def vmem():
    return pl.BlockSpec(memory_space=pltpu.VMEM)


def smem():
    return pl.BlockSpec(memory_space=SMEM)


def whole(shape, at=None):
    spot = at or (0,) * len(shape)
    return pl.BlockSpec(shape, lambda *_: spot)


def per_tile(shape, axis=0):
    return pl.BlockSpec(shape, lambda s: tuple(s if a == axis else 0 for a in range(len(shape))))


def struct(shape, dtype):
    return jax.ShapeDtypeStruct(shape, dtype)


def shards(
    spikes, stimulus, bias, hist_weight, stim_filter, coupling_mix, coupling_target, coupling_weight
):
    time_dev, units_dev = spikes.shape
    tiles_dev = units_dev // TILE
    channels = stimulus.shape[1]
    unit_count = lax.axis_size("unit")
    time_count = lax.axis_size("tm")
    time_total = time_dev * time_count
    slots = unit_count * CAP
    late = time_dev - LAG
    toep = jnp.asarray(toeplitz())
    toep_spec = whole((2 * LAG, NB * LAG))

    hbm = pl.BlockSpec(memory_space=pltpu.HBM)
    find_scratch = SMEM((unit_count,), jnp.int32)
    x, mixed_late, part_late, tail, filt, turned = call(
        late_kernel,
        "late",
        5,
        in_specs=[smem(), smem(), hbm, hbm, hbm],
        out_shape=[
            struct((tiles_dev, TILE, time_dev), BF),
            struct((tiles_dev, TILE, late), BF),
            struct((unit_count, CAP * TILE + NAME_ROWS, late), BF),
            struct((tiles_dev, TILE, LAG), BF),
            struct((2 * LAG, 2 * LAG), BF),
            struct((tiles_dev, FAN * TILE, TILE), BF),
        ],
        scratch_shapes=[
            pltpu.VMEM((time_dev, units_dev), jnp.int32),
            pltpu.VMEM((tiles_dev, FAN, TILE, TILE), BF),
            pltpu.VMEM((2 * LAG, NB * LAG), BF),
            pltpu.VMEM((slots, TILE, late), F32),
            find_scratch,
            find_scratch,
            pltpu.SemaphoreType.DMA((2 + time_dev // LAG,)),
        ],
    )(coupling_target, coupling_mix, spikes, coupling_weight, toep)
    got_late = lax.all_to_all(part_late, "unit", 0, 0, tiled=True)
    halo = lax.ppermute(tail, "tm", [(i, i + 1) for i in range(time_count - 1)])

    mixed_early, *part_early = call(
        early_kernel,
        "early",
        2,
        in_specs=[smem()] + [vmem()] * 4,
        out_shape=[struct((tiles_dev, TILE, LAG), BF)]
        + [struct((CAP, TILE, LAG), BF)] * unit_count,
        scratch_shapes=[pltpu.VMEM((slots, TILE, LAG), F32), find_scratch],
    )(coupling_target, halo, x, filt, turned)
    got_early = to_units(part_early)
    ids = call(
        names_kernel,
        "names",
        1,
        grid=(1,),
        in_specs=[whole((unit_count, NAME_ROWS, LAG), (0, CAP * TILE // NAME_ROWS, 0))],
        out_specs=smem(),
        out_shape=struct((slots,), jnp.int32),
    )(got_late)

    x_spec = per_tile((1, TILE, time_dev))
    halo_spec = per_tile((1, TILE, LAG))
    stim_spec = whole(stimulus.shape)
    logit = call(
        logit_kernel,
        "logit",
        5,
        grid=(tiles_dev,),
        in_specs=[
            x_spec,
            halo_spec,
            toep_spec,
            per_tile((NB, TILE), 1),
            per_tile((1, TILE), 1),
            per_tile((TILE, channels)),
            stim_spec,
        ],
        out_specs=x_spec,
        out_shape=struct((tiles_dev, TILE, time_dev), F32),
        scratch_shapes=[pltpu.VMEM((TILE, TILE), F32)],
    )(x, halo, toep, hist_weight, bias.reshape(1, -1), stim_filter, stimulus)

    rows = TILE // time_count
    resids, sends = [], []
    for at, part in enumerate(HALVES):
        resid, send = call(
            functools.partial(resid_kernel, sum(HALVES[:at])),
            "resid",
            2,
            in_specs=[smem()] + [vmem()] * (3 + unit_count),
            out_shape=[
                struct((tiles_dev, part, time_dev), F32),
                struct((slots, part, time_dev), BF),
            ],
            scratch_shapes=[
                pltpu.VMEM((tiles_dev, part, time_dev), F32),
                pltpu.VMEM((tiles_dev, part, time_dev), BF),
            ],
        )(ids, got_late, logit, x, *got_early)
        resids.append(resid)
        sends.append(send)

    own_rows = units_dev // time_count
    wide = -(-(channels + HIST_ROWS * time_count) // TILE) * TILE
    *pieces, sends[-1] = call(
        own_kernel,
        "own",
        6,
        grid=(tiles_dev,),
        in_specs=[x_spec, halo_spec, toep_spec, stim_spec]
        + [per_tile((1, part, time_dev)) for part in HALVES]
        + [pl.BlockSpec(memory_space=pl.ANY)],
        out_specs=[whole((own_rows, wide))] * time_count + [pl.BlockSpec(memory_space=pl.ANY)],
        out_shape=[struct((own_rows, wide), F32)] * time_count
        + [struct(sends[-1].shape, BF)],
        input_output_aliases={4 + len(HALVES): time_count},
        scratch_shapes=[
            pltpu.VMEM((time_dev, wide), BF),
            pltpu.VMEM((units_dev, wide), F32),
            pltpu.VMEM((own_rows, wide), F32),
        ],
    )(x, halo, toep, stimulus, *resids, sends[-1])
    grad_bias, grad_hist, grad_stim = call(
        functools.partial(finish_kernel, 1.0 / time_total),
        "finish",
        1,
        out_shape=[
            struct((1, units_dev), F32),
            struct((NB, units_dev), F32),
            struct((own_rows, channels), F32),
        ],
    )(*to_peers(pieces))

    grads = []
    for send, part in zip(sends, HALVES, strict=True):
        got = lax.all_to_all(send, "unit", 0, 0, tiled=True)
        pieces = call(
            grad_kernel,
            "grad",
            2,
            in_specs=[smem()] + [vmem()] * 3,
            out_shape=[struct((tiles_dev, rows, FAN * part), BF)] * time_count,
            scratch_shapes=[
                pltpu.VMEM((tiles_dev, FAN * part, time_dev), BF),
                pltpu.VMEM((tiles_dev, TILE, FAN * part), F32),
                find_scratch,
            ],
        )(coupling_target, got, mixed_early, mixed_late)
        grads += to_peers(pieces)
    grad_coupling = call(
        functools.partial(final_kernel, 1.0 / time_total, len(HALVES)),
        "final",
        2,
        out_shape=struct((tiles_dev, FAN, rows, TILE), F32),
    )(*grads)
    return (grad_bias.reshape(-1), grad_hist, grad_stim, grad_coupling)


def solution(mesh):
    return jax.shard_map(
        shards,
        mesh=mesh,
        in_specs=(
            P("tm", "unit"),
            P("tm", None),
            P("unit"),
            P(None, "unit"),
            P("unit", None),
            P(),
            P("unit", None),
            P("unit", None, None, None),
        ),
        out_specs=(
            P("unit"),
            P(None, "unit"),
            P(("unit", "tm"), None),
            P("unit", None, "tm", None),
        ),
        check_vma=False,
    )
```

time: 145 us -> 117 us (0.81)
  waiting for transfers between devices: 40 us -> 22.6 us
  Pallas kernels: 39.2 us -> 28.2 us
  starting transfers between devices: 34.5 us -> 38.1 us
  local copies, waits for them, and re-layouts: 27.6 us -> 25.4 us
    ppermute x3 -> x7, waiting for transfers between devices: 22.1 us -> 4.11 us  [to_units(): lax.ppermute(pieces[k], 'unit', [(i, i ^ k) for i in range(len(pieces))])]
    pallas_call x6 -> x7, Pallas kernels: 22.5 us -> 14.8 us  [the longest x1 5.87 us: shards(): call(late_kernel, 'late', 5, in_specs=[smem(), smem(), hbm, hbm, hbm], ou...]
    ppermute x1, waiting for transfers between devices: 0.01 us -> 5.88 us  [shards(): halo = lax.ppermute(tail, 'tm', [(i, i + 1) for i in range(time_count - 1)])]
    all_to_all x2, waiting for transfers between devices: 9.23 us -> 4.6 us  [shards(): got = lax.all_to_all(send, 'unit', 0, 0, tiled=True)]
    ppermute x3 -> x7, starting transfers between devices: 3.84 us -> 6.34 us  [to_units(): lax.ppermute(pieces[k], 'unit', [(i, i ^ k) for i in range(len(pieces))])]
    unnamed x72 -> x82, local copies, waits for them, and re-layouts: 27.6 us -> 25.4 us
    pallas_call x1, Pallas kernels: 2.98 us -> 1.05 us  [shards(): call(functools.partial(final_kernel, 1.0 / time_total, len(HALVES)), 'fin...]
    ppermute x1, starting transfers between devices: 4.94 us -> 3.48 us  [shards(): halo = lax.ppermute(tail, 'tm', [(i, i + 1) for i in range(time_count - 1)])]
  transfers between devices with their start and end apart: 16 -> 20, of which waited for: 5 -> 8; matrix products, arithmetic and copies ran while one was open for 2% -> 1% of each run, Pallas kernels for 21% -> 17%
where the time goes in v3:
time: 117 us; the launch traced here: 115 us
  starting transfers between devices  38.1 us (33%)
  Pallas kernels  28.2 us (24%)
  local copies, waits for them, and re-layouts  25.4 us (22%)
  waiting for transfers between devices  22.6 us (19%)
    unnamed x82, local copies, waits for them, and re-layouts  25.4 us
    ppermute x9, starting transfers between devices, to_peers(): got.append(lax.ppermute(pieces[shift], 'tm', pairs))  15.8 us
    ppermute x9, waiting for transfers between devices, to_peers(): got.append(lax.ppermute(pieces[shift], 'tm', pairs))  8.01 us
    all_to_all x2, starting transfers between devices, shards(): got = lax.all_to_all(send, 'unit', 0, 0, tiled=True)  7.11 us
    pallas_call x1, Pallas kernels, shards(): call(own_kernel, 'own', 6, grid=(tiles_dev,), in_specs=[x_spec, halo_spec...  6.71 us
    ppermute x7, starting transfers between devices, to_units(): lax.ppermute(pieces[k], 'unit', [(i, i ^ k) for i in range(len(pieces))])  6.34 us
    ppermute x1, waiting for transfers between devices, shards(): halo = lax.ppermute(tail, 'tm', [(i, i + 1) for i in range(time_count - 1)])  5.88 us
    pallas_call x1, Pallas kernels, shards(): call(late_kernel, 'late', 5, in_specs=[smem(), smem(), hbm, hbm, hbm], ou...  5.87 us
  transfers between devices with their start and end apart: 20, of which 8 were waited for; matrix products, arithmetic and copies ran while one was open for 1% of the time, Pallas kernels for 17%

profile of v3, /device:TPU:0, one launch (start us, length us, event | category | flops | bytes accessed | tf_op | source)
XLA Modules:
  0.0 115.2 jit_solution(955358107734789955)
XLA Ops:
  1.4 1.6 %copy-done.2 = s32[512,1024]{1,0:T(8,128)S(1)} copy-done((s32[512,1024]{1,0:T(8,128)S(1)}, s32[512,1024]{1,0:T(8,128)}, u32[]{:S(2)}) %copy-start.2) | copy-done | bytes 2097176
  5.9 5.9 %late.1 = (bf16[8,128,512]{2,1,0:T(8,128)(2,1)S(1)}, bf16[8,128,384]{2,1,0:T(8,128)(2,1)S(1)}, bf16[8,272,384]{2,1,0:T(8,128)(2,1)}, bf16[8,128,128]{2,1,0:T(8,1...) custom-call(s32[8,4]{1,0:T(8,128)S(1)} %copy.14.target, f32[10]{0:T(128)S(1)} %copy-done.8, ...), custom_call_target="tpu_custom_call" | custom-call | flops 5500000256 | bytes 1048576 | tf_op jit(solution)/shard_map/late/pallas_call | solution.py:380
  14.7 5.3 %all-to-all-start = ((bf16[8,272,384]{2,1,0:T(8,128)(2,1)}), bf16[8,272,384]{2,1,0:T(8,128)(2,1)S(1)}, u32[]{:S(2)}, u32[]{:S(2)}) async-start(bf16[8,272,384]{2,1,0:T(8,128)(2,1)} %get-tuple-element.41), calls=%async_computation | async-start | bytes 3342336 | tf_op jit(solution)/shard_map/all_to_all | solution.py:403
  20.0 3.5 %collective-permute-start = (bf16[8,128,128]{2,1,0:T(8,128)(2,1)S(1)}, bf16[8,128,128]{2,1,0:T(8,128)(2,1)S(1)}, u32[]{:S(2)}, u32[]{:S(2)}) collective-permute-start(bf16[8,128,128]{2,1,0:T(8,128)(2,1)S(1)} %get-tuple-element.40), channel_id=1, source_target_pairs={{0,1},{1,2},{2,3},{4,5},{5,6},{6,7},{8,9},{9,10},{10,11},{12,13},{... | collective-permute-start | bytes 786440 | tf_op jit(solution)/shard_map/ppermute | solution.py:404
  23.8 5.9 %collective-permute-done.halo = bf16[8,128,128]{2,1,0:T(8,128)(2,1)S(1)} collective-permute-done((bf16[8,128,128]{2,1,0:T(8,128)(2,1)S(1)}, bf16[8,128,128]{2,1,0:T(8,128)(2,1)S(1)}, u32[]{:S(2)}, u32[]{:S(2)}) %collective-permute-start) | collective-permute-done | bytes 262176 | tf_op jit(solution)/shard_map/ppermute | solution.py:404
  32.2 1.5 %early.1 = (bf16[8,128,128]{2,1,0:T(8,128)(2,1)S(1)}, bf16[2,128,128]{2,1,0:T(8,128)(2,1)S(1)}, bf16[2,128,128]{2,1,0:T(8,128)(2,1)S(1)}, bf16[2,128,128]{2,1,0:...) custom-call(s32[8,4]{1,0:T(8,128)S(1)} %copy.14.target, ...), custom_call_target="tpu_custom_call" | custom-call | flops 2200000000 | bytes 1048576 | tf_op jit(solution)/shard_map/early/pallas_call | solution.py:406
  33.8 1.7 %collective-permute-start.2 = (bf16[2,128,128]{2,1,0:T(8,128)(2,1)S(1)}, bf16[2,128,128]{2,1,0:T(8,128)(2,1)S(1)}, u32[]{:S(2)}, u32[]{:S(2)}) collective-permute-start(bf16[2,128,128]{2,1,0:T(8,128)(2,1)S(1)} %get-tuple-element.46), channel_id=1, source_target_pairs={{0,8},{4,12},{8,0},{12,4},{16,24},{20,28},{24,16},{28,20},{1,9},{5... | collective-permute-start | bytes 196616 | tf_op jit(solution)/shard_map/ppermute | solution.py:331
  35.6 1.7 %collective-permute-start.4 = (bf16[2,128,128]{2,1,0:T(8,128)(2,1)S(1)}, bf16[2,128,128]{2,1,0:T(8,128)(2,1)S(1)}, u32[]{:S(2)}, u32[]{:S(2)}) collective-permute-start(bf16[2,128,128]{2,1,0:T(8,128)(2,1)S(1)} %get-tuple-element.48), channel_id=1, source_target_pairs={{0,16},{4,20},{8,24},{12,28},{16,0},{20,4},{24,8},{28,12},{1,17},{... | collective-permute-start | bytes 196616 | tf_op jit(solution)/shard_map/ppermute | solution.py:331
  37.4 4.9 %logit.1 = f32[8,128,512]{2,1,0:T(8,128)S(1)} custom-call(bf16[8,128,512]{2,1,0:T(8,128)(2,1)S(1)} %copy-done.17, bf16[8,128,128]{2,1,0:T(8,128)(2,1)S(1)} %collective-permute-done.halo, bf16[256,1280]{1,0:T(8,128)(2,1)S(1)} %copy-done.10, f32[10,1024]{1,0:T(8,128)S(1)} %copy-done.4, f32[1,1024]{1,0:T(1,128)S(1)} %bitcast.2, ...), custom_call_target="tpu_custom_call" | custom-call | flops 5500000256 | bytes 1048576 | tf_op jit(solution)/shard_map/logit/pallas_call | solution.py:429
  43.6 2.6 %collective-permute-start.6 = (bf16[2,128,128]{2,1,0:T(8,128)(2,1)S(1)}, bf16[2,128,128]{2,1,0:T(8,128)(2,1)S(1)}, u32[]{:S(2)}, u32[]{:S(2)}) collective-permute-start(bf16[2,128,128]{2,1,0:T(8,128)(2,1)S(1)} %get-tuple-element.50), channel_id=1, source_target_pairs={{0,24},{4,28},{8,16},{12,20},{16,8},{20,12},{24,0},{28,4},{1,25},{... | collective-permute-start | bytes 196616 | tf_op jit(solution)/shard_map/ppermute | solution.py:331
  47.1 1.8 %collective-permute-done.6.refs_6_ = bf16[2,128,128]{2,1,0:T(8,128)(2,1)S(1)} collective-permute-done((bf16[2,128,128]{2,1,0:T(8,128)(2,1)S(1)}, bf16[2,128,128]{2,1,0:T(8,128)(2,1)S(1)}, u32[]{:S(2)}, u32[]{:S(2)}) %collective-permute-start.6) | collective-permute-done | bytes 65568 | tf_op jit(solution)/shard_map/ppermute | solution.py:331
  49.0 2.2 %collective-permute-done.7.refs_7_ = bf16[2,128,128]{2,1,0:T(8,128)(2,1)S(1)} collective-permute-done((bf16[2,128,128]{2,1,0:T(8,128)(2,1)S(1)}, bf16[2,128,128]{2,1,0:T(8,128)(2,1)S(1)}, u32[]{:S(2)}, u32[]{:S(2)}) %collective-permute-start.7) | collective-permute-done | bytes 65568 | tf_op jit(solution)/shard_map/ppermute | solution.py:331
  54.6 3.6 %all-to-all-start.1 = ((bf16[16,64,512]{2,1,0:T(8,128)(2,1)}), bf16[16,64,512]{2,1,0:T(8,128)(2,1)S(1)}, u32[]{:S(2)}, u32[]{:S(2)}) async-start(bf16[16,64,512]{2,1,0:T(8,128)(2,1)} %copy-done), calls=%async_computation.1 | async-start | bytes 2097152 | tf_op jit(solution)/shard_map/all_to_all | solution.py:501
  59.0 1.6 %copy-done.14 = f32[8,128,512]{2,1,0:T(8,128)S(1)} copy-done((f32[8,128,512]{2,1,0:T(8,128)S(1)}, f32[8,128,512]{2,1,0:T(8,128)}, u32[]{:S(2)}) %copy-start.14) | copy-done | bytes 2097176
  64.4 6.7 %own.1 = (f32[256,128]{1,0:T(8,128)S(1)}, f32[256,128]{1,0:T(8,128)}, f32[256,128]{1,0:T(8,128)S(1)}, f32[256,128]{1,0:T(8,128)S(1)}, bf16[16,64,512]{2,1,0:T(8,128)(2,1)S(1)}) custom-call(bf16[8,128,512]{2,1,0:T(8,128)(2,1)S(1)} %copy-done.20, bf16[8,128,128]{2,1,0:T(8,128)(2,1)S(1)} %collective-permute-done.halo, ...), custom_call_target="tpu_custom_call", output_to_operand_aliasing={{4}: (6, {})} | custom-call | flops 6600000000 | bytes 1048576 | tf_op jit(solution)/shard_map/own/pallas_call | solution.py:470
  73.5 3.6 %all-to-all-start.2 = ((bf16[16,64,512]{2,1,0:T(8,128)(2,1)}), bf16[16,64,512]{2,1,0:T(8,128)(2,1)S(1)}, u32[]{:S(2)}, u32[]{:S(2)}) async-start(bf16[16,64,512]{2,1,0:T(8,128)(2,1)} %copy-done.1), calls=%async_computation.2 | async-start | bytes 2097152 | tf_op jit(solution)/shard_map/all_to_all | solution.py:501
  77.1 2.4 %collective-permute-start.8 = (f32[256,128]{1,0:T(8,128)}, f32[256,128]{1,0:T(8,128)S(1)}, u32[]{:S(2)}, u32[]{:S(2)}) collective-permute-start(f32[256,128]{1,0:T(8,128)} %get-tuple-element.56), channel_id=1, source_target_pairs={{0,1},{1,2},{2,3},{3,0},{4,5},{5,6},{6,7},{7,4},{8,9},{9,10},{10,1... | collective-permute-start | bytes 393224 | tf_op jit(solution)/shard_map/ppermute | solution.py:324
  79.5 2.7 %collective-permute-start.9 = (f32[256,128]{1,0:T(8,128)S(1)}, f32[256,128]{1,0:T(8,128)S(1)}, u32[]{:S(2)}, u32[]{:S(2)}) collective-permute-start(f32[256,128]{1,0:T(8,128)S(1)} %get-tuple-element.57), channel_id=1, source_target_pairs={{0,2},{1,3},{2,0},{3,1},{4,6},{5,7},{6,4},{7,5},{8,10},{9,11},{10,... | collective-permute-start | bytes 393224 | tf_op jit(solution)/shard_map/ppermute | solution.py:324
  84.6 2.3 %grad.2 = (bf16[8,32,256]{2,1,0:T(8,128)(2,1)S(1)}, bf16[8,32,256]{2,1,0:T(8,128)(2,1)}, bf16[8,32,256]{2,1,0:T(8,128)(2,1)}, bf16[8,32,256]{2,1,0:T(8,128)(2,1)S(1)}) custom-call(s32[8,4]{1,0:T(8,128)S(1)} %copy.14.target, bf16[16,64,512]{2,1,0:T(8,128)(2,1)S(1)} %all-to-all-done.1.recv, bf16[8,128,128]{2,1,0:T(8,128)(2,1)S(1)} %copy-done.33, ...), custom_call_target="tpu_custom_call" | custom-call | flops 2200000000 | bytes 1048576 | tf_op jit(solution)/shard_map/grad/pallas_call | solution.py:502
  88.6 3.9 %all-to-all-done.2.recv = bf16[16,64,512]{2,1,0:T(8,128)(2,1)S(1)} async-done(((bf16[16,64,512]{2,1,0:T(8,128)(2,1)}), bf16[16,64,512]{2,1,0:T(8,128)(2,1)S(1)}, u32[]{:S(2)}, u32[]{:S(2)}) %all-to-all-start.2) | async-done | bytes 1048608 | tf_op jit(solution)/shard_map/all_to_all | solution.py:501
  94.6 1.6 %grad.3 = (bf16[8,32,256]{2,1,0:T(8,128)(2,1)S(1)}, bf16[8,32,256]{2,1,0:T(8,128)(2,1)S(1)}, bf16[8,32,256]{2,1,0:T(8,128)(2,1)S(1)}, bf16[8,32,256]{2,1,0:T(8,128)(2,1)S(1)}) custom-call(s32[8,4]{1,0:T(8,128)S(1)} %copy.14.target, bf16[16,64,512]{2,1,0:T(8,128)(2,1)S(1)} %all-to-all-done.2.recv, bf16[8,128,128]{2,1,0:T(8,128)(2,1)S(1)} %copy-done.34, ...), custom_call_target="tpu_custom_call" | custom-call | flops 2200000000 | bytes 1048576 | tf_op jit(solution)/shard_map/grad/pallas_call | solution.py:502
  96.2 4.5 %collective-permute-start.13 = (bf16[8,32,256]{2,1,0:T(8,128)(2,1)S(1)}, bf16[8,32,256]{2,1,0:T(8,128)(2,1)S(1)}, u32[]{:S(2)}, u32[]{:S(2)}) collective-permute-start(bf16[8,32,256]{2,1,0:T(8,128)(2,1)S(1)} %get-tuple-element.68), channel_id=1, source_target_pairs={{0,3},{1,0},{2,1},{3,2},{4,7},{5,4},{6,5},{7,6},{8,11},{9,8},{10,9... | collective-permute-start | bytes 393224 | tf_op jit(solution)/shard_map/ppermute | solution.py:324
  101.7 3.0 %collective-permute-start.16 = (bf16[8,32,256]{2,1,0:T(8,128)(2,1)S(1)}, bf16[8,32,256]{2,1,0:T(8,128)(2,1)S(1)}, u32[]{:S(2)}, u32[]{:S(2)}) collective-permute-start(bf16[8,32,256]{2,1,0:T(8,128)(2,1)S(1)} %get-tuple-element.73), channel_id=1, source_target_pairs={{0,3},{1,0},{2,1},{3,2},{4,7},{5,4},{6,5},{7,6},{8,11},{9,8},{10,9... | collective-permute-start | bytes 393224 | tf_op jit(solution)/shard_map/ppermute | solution.py:324
  109.1 5.1 %collective-permute-done.15.refs_6_ = bf16[8,32,256]{2,1,0:T(8,128)(2,1)S(1)} collective-permute-done((bf16[8,32,256]{2,1,0:T(8,128)(2,1)S(1)}, bf16[8,32,256]{2,1,0:T(8,128)(2,1)S(1)}, u32[]{:S(2)}, u32[]{:S(2)}) %collective-permute-start.15) | collective-permute-done | bytes 131104 | tf_op jit(solution)/shard_map/ppermute | solution.py:324
  (109 shorter events, 34.8 us)
Async XLA Ops:
  14.7 31.6 %all-to-all-start = ((bf16[8,272,384]{2,1,0:T(8,128)(2,1)}), bf16[8,272,384]{2,1,0:T(8,128)(2,1)S(1)}, u32[]{:S(2)}, u32[]{:S(2)}) async-start(bf16[8,272,384]{2,1,0:T(8,128)(2,1)} %get-tuple-element.41), calls=%async_computation | async-start | bytes 3342336 | tf_op jit(solution)/shard_map/all_to_all | solution.py:403
  20.0 9.7 %collective-permute-start = (bf16[8,128,128]{2,1,0:T(8,128)(2,1)S(1)}, bf16[8,128,128]{2,1,0:T(8,128)(2,1)S(1)}, u32[]{:S(2)}, u32[]{:S(2)}) collective-permute-start(bf16[8,128,128]{2,1,0:T(8,128)(2,1)S(1)} %get-tuple-element.40), channel_id=1, source_target_pairs={{0,1},{1,2},{2,3},{4,5},{5,6},{6,7},{8,9},{9,10},{10,11},{12,13},{... | collective-permute-start | bytes 786440 | tf_op jit(solution)/shard_map/ppermute | solution.py:404
  33.7 17.5 %copy-start.30 = (bf16[2,128,128]{2,1,0:T(8,128)(2,1)}, bf16[2,128,128]{2,1,0:T(8,128)(2,1)S(1)}, u32[]{:S(2)}) copy-start(bf16[2,128,128]{2,1,0:T(8,128)(2,1)S(1)} %get-tuple-element.44.refs_0_) | copy-start | bytes 196612
  33.7 9.9 %collective-permute-start.1 = (bf16[2,128,128]{2,1,0:T(8,128)(2,1)S(1)}, bf16[2,128,128]{2,1,0:T(8,128)(2,1)S(1)}, u32[]{:S(2)}, u32[]{:S(2)}) collective-permute-start(bf16[2,128,128]{2,1,0:T(8,128)(2,1)S(1)} %get-tuple-element.45), channel_id=1, source_target_pairs={{0,4},{4,0},{8,12},{12,8},{16,20},{20,16},{24,28},{28,24},{1,5},{5... | collective-permute-start | bytes 196616 | tf_op jit(solution)/shard_map/ppermute | solution.py:331
  33.8 12.4 %collective-permute-start.2 = (bf16[2,128,128]{2,1,0:T(8,128)(2,1)S(1)}, bf16[2,128,128]{2,1,0:T(8,128)(2,1)S(1)}, u32[]{:S(2)}, u32[]{:S(2)}) collective-permute-start(bf16[2,128,128]{2,1,0:T(8,128)(2,1)S(1)} %get-tuple-element.46), channel_id=1, source_target_pairs={{0,8},{4,12},{8,0},{12,4},{16,24},{20,28},{24,16},{28,20},{1,9},{5... | collective-permute-start | bytes 196616 | tf_op jit(solution)/shard_map/ppermute | solution.py:331
  35.5 11.6 %collective-permute-start.3 = (bf16[2,128,128]{2,1,0:T(8,128)(2,1)S(1)}, bf16[2,128,128]{2,1,0:T(8,128)(2,1)S(1)}, u32[]{:S(2)}, u32[]{:S(2)}) collective-permute-start(bf16[2,128,128]{2,1,0:T(8,128)(2,1)S(1)} %get-tuple-element.47), channel_id=1, source_target_pairs={{0,12},{4,8},{8,4},{12,0},{16,28},{20,24},{24,20},{28,16},{1,13},{... | collective-permute-start | bytes 196616 | tf_op jit(solution)/shard_map/ppermute | solution.py:331
  35.6 11.4 %collective-permute-start.4 = (bf16[2,128,128]{2,1,0:T(8,128)(2,1)S(1)}, bf16[2,128,128]{2,1,0:T(8,128)(2,1)S(1)}, u32[]{:S(2)}, u32[]{:S(2)}) collective-permute-start(bf16[2,128,128]{2,1,0:T(8,128)(2,1)S(1)} %get-tuple-element.48), channel_id=1, source_target_pairs={{0,16},{4,20},{8,24},{12,28},{16,0},{20,4},{24,8},{28,12},{1,17},{... | collective-permute-start | bytes 196616 | tf_op jit(solution)/shard_map/ppermute | solution.py:331
  37.3 9.8 %collective-permute-start.5 = (bf16[2,128,128]{2,1,0:T(8,128)(2,1)S(1)}, bf16[2,128,128]{2,1,0:T(8,128)(2,1)S(1)}, u32[]{:S(2)}, u32[]{:S(2)}) collective-permute-start(bf16[2,128,128]{2,1,0:T(8,128)(2,1)S(1)} %get-tuple-element.49), channel_id=1, source_target_pairs={{0,20},{4,16},{8,28},{12,24},{16,4},{20,0},{24,12},{28,8},{1,21},{... | collective-permute-start | bytes 196616 | tf_op jit(solution)/shard_map/ppermute | solution.py:331
  43.6 5.3 %collective-permute-start.6 = (bf16[2,128,128]{2,1,0:T(8,128)(2,1)S(1)}, bf16[2,128,128]{2,1,0:T(8,128)(2,1)S(1)}, u32[]{:S(2)}, u32[]{:S(2)}) collective-permute-start(bf16[2,128,128]{2,1,0:T(8,128)(2,1)S(1)} %get-tuple-element.50), channel_id=1, source_target_pairs={{0,24},{4,28},{8,16},{12,20},{16,8},{20,12},{24,0},{28,4},{1,25},{... | collective-permute-start | bytes 196616 | tf_op jit(solution)/shard_map/ppermute | solution.py:331
  46.2 5.0 %collective-permute-start.7 = (bf16[2,128,128]{2,1,0:T(8,128)(2,1)S(1)}, bf16[2,128,128]{2,1,0:T(8,128)(2,1)S(1)}, u32[]{:S(2)}, u32[]{:S(2)}) collective-permute-start(bf16[2,128,128]{2,1,0:T(8,128)(2,1)S(1)} %get-tuple-element.51), channel_id=1, source_target_pairs={{0,28},{4,24},{8,20},{12,16},{16,12},{20,8},{24,4},{28,0},{1,29},{... | collective-permute-start | bytes 196616 | tf_op jit(solution)/shard_map/ppermute | solution.py:331
  54.6 18.9 %all-to-all-start.1 = ((bf16[16,64,512]{2,1,0:T(8,128)(2,1)}), bf16[16,64,512]{2,1,0:T(8,128)(2,1)S(1)}, u32[]{:S(2)}, u32[]{:S(2)}) async-start(bf16[16,64,512]{2,1,0:T(8,128)(2,1)} %copy-done), calls=%async_computation.1 | async-start | bytes 2097152 | tf_op jit(solution)/shard_map/all_to_all | solution.py:501
  72.8 10.7 %copy-start.33 = (bf16[8,128,128]{2,1,0:T(8,128)(2,1)S(1)}, bf16[8,128,128]{2,1,0:T(8,128)(2,1)}, u32[]{:S(2)}) copy-start(bf16[8,128,128]{2,1,0:T(8,128)(2,1)} %copy-done.32) | copy-start | bytes 786436
  73.5 19.0 %all-to-all-start.2 = ((bf16[16,64,512]{2,1,0:T(8,128)(2,1)}), bf16[16,64,512]{2,1,0:T(8,128)(2,1)S(1)}, u32[]{:S(2)}, u32[]{:S(2)}) async-start(bf16[16,64,512]{2,1,0:T(8,128)(2,1)} %copy-done.1), calls=%async_computation.2 | async-start | bytes 2097152 | tf_op jit(solution)/shard_map/all_to_all | solution.py:501
  77.1 19.1 %collective-permute-start.8 = (f32[256,128]{1,0:T(8,128)}, f32[256,128]{1,0:T(8,128)S(1)}, u32[]{:S(2)}, u32[]{:S(2)}) collective-permute-start(f32[256,128]{1,0:T(8,128)} %get-tuple-element.56), channel_id=1, source_target_pairs={{0,1},{1,2},{2,3},{3,0},{4,5},{5,6},{6,7},{7,4},{8,9},{9,10},{10,1... | collective-permute-start | bytes 393224 | tf_op jit(solution)/shard_map/ppermute | solution.py:324
  79.5 21.3 %collective-permute-start.9 = (f32[256,128]{1,0:T(8,128)S(1)}, f32[256,128]{1,0:T(8,128)S(1)}, u32[]{:S(2)}, u32[]{:S(2)}) collective-permute-start(f32[256,128]{1,0:T(8,128)S(1)} %get-tuple-element.57), channel_id=1, source_target_pairs={{0,2},{1,3},{2,0},{3,1},{4,6},{5,7},{6,4},{7,5},{8,10},{9,11},{10,... | collective-permute-start | bytes 393224 | tf_op jit(solution)/shard_map/ppermute | solution.py:324
  82.2 18.6 %collective-permute-start.10 = (f32[256,128]{1,0:T(8,128)S(1)}, f32[256,128]{1,0:T(8,128)S(1)}, u32[]{:S(2)}, u32[]{:S(2)}) collective-permute-start(f32[256,128]{1,0:T(8,128)S(1)} %get-tuple-element.58), channel_id=1, source_target_pairs={{0,3},{1,0},{2,1},{3,2},{4,7},{5,4},{6,5},{7,6},{8,11},{9,8},{10,9... | collective-permute-start | bytes 393224 | tf_op jit(solution)/shard_map/ppermute | solution.py:324
  87.6 14.1 %collective-permute-start.11 = (bf16[8,32,256]{2,1,0:T(8,128)(2,1)}, bf16[8,32,256]{2,1,0:T(8,128)(2,1)S(1)}, u32[]{:S(2)}, u32[]{:S(2)}) collective-permute-start(bf16[8,32,256]{2,1,0:T(8,128)(2,1)} %get-tuple-element.66), channel_id=1, source_target_pairs={{0,1},{1,2},{2,3},{3,0},{4,5},{5,6},{6,7},{7,4},{8,9},{9,10},{10,1... | collective-permute-start | bytes 393224 | tf_op jit(solution)/shard_map/ppermute | solution.py:324
  88.3 17.8 %collective-permute-start.12 = (bf16[8,32,256]{2,1,0:T(8,128)(2,1)}, bf16[8,32,256]{2,1,0:T(8,128)(2,1)S(1)}, u32[]{:S(2)}, u32[]{:S(2)}) collective-permute-start(bf16[8,32,256]{2,1,0:T(8,128)(2,1)} %get-tuple-element.67), channel_id=1, source_target_pairs={{0,2},{1,3},{2,0},{3,1},{4,6},{5,7},{6,4},{7,5},{8,10},{9,11},{10,... | collective-permute-start | bytes 393224 | tf_op jit(solution)/shard_map/ppermute | solution.py:324
  94.6 10.1 %copy-start.29 = (f32[256,128]{1,0:T(8,128)S(1)}, f32[256,128]{1,0:T(8,128)}, u32[]{:S(2)}) copy-start(f32[256,128]{1,0:T(8,128)} %copy-done.28) | copy-start | bytes 393220
  96.2 11.4 %collective-permute-start.13 = (bf16[8,32,256]{2,1,0:T(8,128)(2,1)S(1)}, bf16[8,32,256]{2,1,0:T(8,128)(2,1)S(1)}, u32[]{:S(2)}, u32[]{:S(2)}) collective-permute-start(bf16[8,32,256]{2,1,0:T(8,128)(2,1)S(1)} %get-tuple-element.68), channel_id=1, source_target_pairs={{0,3},{1,0},{2,1},{3,2},{4,7},{5,4},{6,5},{7,6},{8,11},{9,8},{10,9... | collective-permute-start | bytes 393224 | tf_op jit(solution)/shard_map/ppermute | solution.py:324
  100.8 8.3 %collective-permute-start.14 = (bf16[8,32,256]{2,1,0:T(8,128)(2,1)S(1)}, bf16[8,32,256]{2,1,0:T(8,128)(2,1)S(1)}, u32[]{:S(2)}, u32[]{:S(2)}) collective-permute-start(bf16[8,32,256]{2,1,0:T(8,128)(2,1)S(1)} %get-tuple-element.71), channel_id=1, source_target_pairs={{0,1},{1,2},{2,3},{3,0},{4,5},{5,6},{6,7},{7,4},{8,9},{9,10},{10,1... | collective-permute-start | bytes 393224 | tf_op jit(solution)/shard_map/ppermute | solution.py:324
  100.8 13.4 %collective-permute-start.15 = (bf16[8,32,256]{2,1,0:T(8,128)(2,1)S(1)}, bf16[8,32,256]{2,1,0:T(8,128)(2,1)S(1)}, u32[]{:S(2)}, u32[]{:S(2)}) collective-permute-start(bf16[8,32,256]{2,1,0:T(8,128)(2,1)S(1)} %get-tuple-element.72), channel_id=1, source_target_pairs={{0,2},{1,3},{2,0},{3,1},{4,6},{5,7},{6,4},{7,5},{8,10},{9,11},{10,... | collective-permute-start | bytes 393224 | tf_op jit(solution)/shard_map/ppermute | solution.py:324
  101.7 12.4 %collective-permute-start.16 = (bf16[8,32,256]{2,1,0:T(8,128)(2,1)S(1)}, bf16[8,32,256]{2,1,0:T(8,128)(2,1)S(1)}, u32[]{:S(2)}, u32[]{:S(2)}) collective-permute-start(bf16[8,32,256]{2,1,0:T(8,128)(2,1)S(1)} %get-tuple-element.73), channel_id=1, source_target_pairs={{0,3},{1,0},{2,1},{3,2},{4,7},{5,4},{6,5},{7,6},{8,11},{9,8},{10,9... | collective-permute-start | bytes 393224 | tf_op jit(solution)/shard_map/ppermute | solution.py:324
  104.7 9.5 %copy-start.36 = (bf16[8,32,256]{2,1,0:T(8,128)(2,1)S(1)}, bf16[8,32,256]{2,1,0:T(8,128)(2,1)}, u32[]{:S(2)}) copy-start(bf16[8,32,256]{2,1,0:T(8,128)(2,1)} %copy-done.35) | copy-start | bytes 393220
  (35 other events, 86.0 us)

commit v4 on v3

v4 whole, which is shorter than its diff:
```python
import functools
import math

import jax
import jax.numpy as jnp
import numpy as np
from jax import lax
from jax.experimental import pallas as pl
from jax.experimental.pallas import tpu as pltpu
from jax.sharding import PartitionSpec as P

TILE = 128
FAN = 4
CAP = 2
NB = 10
LAG = 128
HALVES = (64, 64)
BF = jnp.bfloat16
F32 = jnp.float32
SMEM = pltpu.SMEM
VMEM_LIMIT = 20 << 20
FLOPS_A_MICRO = 1.1e9
HIST_ROWS = 16
NAME_ROWS = 16


def raised_cosine(count, lag):
    low = math.log(2.0)
    high = math.log(lag + 1.0)
    spacing = (high - low) / (count - 1)
    stretched = np.log(np.arange(1, lag + 1).astype(np.float64) + 1.0)
    centers = low + spacing * np.arange(count).astype(np.float64)
    phases = np.clip(
        (stretched[None, :] - centers[:, None]) * (math.pi / (2.0 * spacing)), -math.pi, math.pi
    )
    shapes = 0.5 * (1.0 + np.cos(phases))
    return (shapes / np.sum(shapes, axis=1, keepdims=True)).astype(np.float32).astype(BF)


def toeplitz():
    basis = raised_cosine(NB, LAG)
    lag = LAG + np.arange(LAG)[None, :] - np.arange(2 * LAG)[:, None]
    inside = (lag >= 1) & (lag <= LAG)
    blocks = np.where(inside[None], basis[:, np.clip(lag - 1, 0, LAG - 1)], np.zeros((), BF))
    return np.ascontiguousarray(blocks.transpose(1, 0, 2).reshape(2 * LAG, NB * LAG))


def contract(a, b, dims):
    return lax.dot_general(a, b, ((dims[:1], dims[1:]), ((), ())), preferred_element_type=F32)


def find_slots(target, slots, lowest, highest, tiles_dev):
    for o in range(lowest.shape[0]):
        lowest[o] = tiles_dev
        highest[o] = -1
    for s in range(tiles_dev):
        for f in range(FAN):
            o = lax.div(target[f, s], tiles_dev)
            tile = lax.rem(target[f, s], tiles_dev)
            lowest[o] = jnp.minimum(lowest[o], tile)
            highest[o] = jnp.maximum(highest[o], tile)
    for s in range(tiles_dev):
        for f in range(FAN):
            o = lax.div(target[f, s], tiles_dev)
            tile = lax.rem(target[f, s], tiles_dev)
            slots[s * FAN + f] = o * CAP + (tile != lowest[o]).astype(jnp.int32)


def mixing_filter(mix, toep, filt):
    total = jnp.zeros((2 * LAG, LAG), F32)
    for b in range(NB):
        total += mix[b] * toep[:, b * LAG : (b + 1) * LAG].astype(F32)
    high = total.astype(BF)
    filt[:, :LAG] = high
    filt[:, LAG:] = (total - high.astype(F32)).astype(BF)


def mix_window(window, filt):
    both = jnp.dot(window, filt, preferred_element_type=F32)
    return (both[:, :LAG] + both[:, LAG:]).astype(BF)


def add_partials(slots, turned, mixed, total):
    total[...] = jnp.zeros_like(total)
    for s in range(turned.shape[0]):
        products = jnp.dot(turned[s], mixed[s], preferred_element_type=F32)
        for f in range(FAN):
            total[slots[s * FAN + f]] += products[f * TILE : (f + 1) * TILE]


def late_kernel(target_hbm, mix_hbm, spikes, weight, toep, *refs):
    x, mixed, tail, filt, turned, slots = refs[:6]
    parts = refs[6:-9]
    target, mix, counts, weights, bases, total, lowest, highest, sems = refs[-9:]
    tiles_dev = x.shape[0]
    blocks = x.shape[2] // LAG
    pulls = [
        pltpu.make_async_copy(toep, bases, sems.at[0]),
        pltpu.make_async_copy(weight, weights, sems.at[1]),
        pltpu.make_async_copy(target_hbm, target, sems.at[2]),
        pltpu.make_async_copy(mix_hbm, mix, sems.at[3]),
    ]
    for k in range(blocks):
        at = pl.ds(k * LAG, LAG)
        pulls.append(pltpu.make_async_copy(spikes.at[at], counts.at[at], sems.at[4 + k]))
    for pull in pulls:
        pull.start()

    pulls[2].wait()
    find_slots(target, slots, lowest, highest, tiles_dev)
    pulls[3].wait()
    pulls[0].wait()
    mixing_filter(mix, bases, filt)
    before = None
    for k in range(blocks):
        pulls[4 + k].wait()
        now = counts[k * LAG : (k + 1) * LAG].astype(F32).T.astype(BF)
        x[:, :, k * LAG : (k + 1) * LAG] = now.reshape(tiles_dev, TILE, LAG)
        if k:
            got = mix_window(jnp.concatenate([before, now], axis=1), filt[...])
            mixed[:, :, (k - 1) * LAG : k * LAG] = got.reshape(tiles_dev, TILE, LAG)
        before = now
    tail[...] = before.reshape(tiles_dev, TILE, LAG)

    pulls[1].wait()
    for s in range(tiles_dev):
        for f in range(FAN):
            turned[s, f * TILE : (f + 1) * TILE] = weights[s, f].astype(F32).T.astype(BF)
    add_partials(slots, turned, mixed, total)

    row = lax.broadcasted_iota(jnp.int32, (NAME_ROWS, mixed.shape[2]), 0)
    me = lax.axis_index("unit")
    for k, part in enumerate(parts):
        o = jnp.bitwise_xor(me, k)
        high = highest[o]
        low = jnp.where(high < 0, -1, lowest[o])
        for q in range(CAP):
            part[q * TILE : (q + 1) * TILE] = total[o * CAP + q].astype(BF)
        names = jnp.where(row == 0, low, jnp.where(row == 1, high, 0))
        part[CAP * TILE :] = names.astype(F32).astype(BF)


def early_kernel(slots, halo, x, filt, turned, kept, mixed_out, *refs):
    outs, total = refs[:-2], refs[-1]
    del kept
    units = x.shape[0] * TILE
    window = jnp.concatenate(
        [halo[...].reshape(units, LAG), x[:, :, :LAG].reshape(units, LAG)], axis=1
    )
    mixed_out[...] = mix_window(window, filt[...]).reshape(mixed_out.shape)
    add_partials(slots, turned, mixed_out, total)
    me = lax.axis_index("unit")
    for k, out in enumerate(outs):
        for q in range(CAP):
            out[q] = total[jnp.bitwise_xor(me, k) * CAP + q].astype(BF)


def names_kernel(*refs):
    got, ids = refs[:-1], refs[-1]
    for k, part in enumerate(got):
        block = part[...].astype(F32)
        for q in range(CAP):
            ids[k * CAP + q] = jnp.max(block[q : q + 1]).astype(jnp.int32)


def windows(extended, count):
    return jnp.concatenate([extended[:, k * LAG : (k + 2) * LAG] for k in range(count)], axis=0)


def add_history(total, window, toep, columns):
    count = window.shape[0] // TILE
    for c in range(0, NB, 2):
        both = jnp.dot(window, toep[:, c * LAG : (c + 2) * LAG], preferred_element_type=F32)
        for b in (c, c + 1):
            weight = columns[:, b : b + 1]
            piece = both[:, (b - c) * LAG : (b - c + 1) * LAG]
            total = [
                total[k] + weight * piece[k * TILE : (k + 1) * TILE] for k in range(count)
            ]
    return total


def logit_kernel(x, toep, hist_weight, bias, stim_filter, stimulus, out, columns_out, rows):
    rows[...] = jnp.zeros_like(rows)
    rows[:NB] = hist_weight[...]
    rows[NB : NB + 1] = bias[...]
    blocks = x.shape[2] // LAG

    def one(s, _):
        units = pl.ds(pl.multiple_of(s * TILE, TILE), TILE)
        columns = rows[:, units].T
        columns_out[s] = columns
        start = contract(stim_filter[:, units], stimulus[...], (0, 0)) + columns[:, NB : NB + 1]
        total = [start[:, k * LAG : (k + 1) * LAG] for k in range(blocks)]
        window = windows(x[s], blocks - 1)
        total[1:] = add_history(total[1:], window, toep, columns)
        for k in range(blocks):
            out[s, :, k * LAG : (k + 1) * LAG] = total[k]
        return 0

    lax.fori_loop(0, x.shape[0], one, 0)


def logit_early_kernel(x, halo, toep, columns, logit, out):
    def one(s, _):
        window = jnp.concatenate([halo[s], x[s, :, :LAG]], axis=1)
        (out[s],) = add_history([logit[s, :, :LAG]], window, toep, columns[s])
        return 0

    lax.fori_loop(0, x.shape[0], one, 0)


def resid_kernel(first, ids, logit, logit_early, x, *refs):
    count = ids.shape[0] // CAP
    late, early, (resid, *sends) = refs[:count], refs[count : 2 * count], refs[2 * count : -2]
    total, rounded = refs[-2:]
    part = resid.shape[1]
    mine = slice(first, first + part)
    total[:, :, LAG:] = logit[:, mine, LAG:]
    total[:, :, :LAG] = logit_early[:, mine]
    for k in range(count):
        for q in range(CAP):
            tile = ids[k * CAP + q]

            @pl.when(tile >= 0)
            def _():
                start = q * TILE + first
                total[tile, :, LAG:] += late[k][start : start + part].astype(F32)
                total[tile, :, :LAG] += early[k][q, mine].astype(F32)

    for j in range(logit.shape[0]):
        r = x[j, mine].astype(F32) - jnp.exp(total[j])
        resid[j] = r
        rounded[j] = r.astype(BF)
    for k in range(count):
        for q in range(CAP):
            tile = ids[k * CAP + q]

            @pl.when(tile >= 0)
            def _():
                sends[k][q] = rounded[tile]

            @pl.when(tile < 0)
            def _():
                sends[k][q] = jnp.zeros(sends[k].shape[1:], BF)


def peer(shift, count):
    return lax.rem(lax.axis_index("tm") + shift, count)


def own_kernel(x, halo, toep, stimulus, resid_a, resid_b, *refs):
    outs, (wide, stim, sums) = refs[:-3], refs[-3:]
    channels = stimulus.shape[0]
    rows = sums.shape[0]
    blocks = x.shape[2] // LAG
    wide[...] = jnp.zeros_like(wide)
    wide[:channels] = stimulus[...]
    sums[...] = jnp.zeros_like(sums)
    lane = lax.broadcasted_iota(jnp.int32, (TILE, sums.shape[1]), 1)

    def one(s, _):
        resid = jnp.concatenate([resid_a[s], resid_b[s]], axis=0)
        units = pl.ds(pl.multiple_of(s * TILE, TILE), TILE)
        stim[units] = contract(resid.astype(BF), wide[...], (1, 1))
        window = windows(jnp.concatenate([halo[s], x[s]], axis=1), blocks)
        parts = [resid[:, k * LAG : (k + 1) * LAG] for k in range(blocks)]
        columns = []
        for c in range(0, NB, 2):
            both = jnp.dot(window, toep[:, c * LAG : (c + 2) * LAG], preferred_element_type=F32)
            for b in (c, c + 1):
                piece = both[:, (b - c) * LAG : (b - c + 1) * LAG]
                total = parts[0] * piece[:TILE]
                for k in range(1, blocks):
                    total += parts[k] * piece[k * TILE : (k + 1) * TILE]
                columns.append(jnp.sum(total, axis=1, keepdims=True))
        column = jnp.sum(sum(parts[1:], parts[0]), axis=1, keepdims=True)
        high = column.astype(BF).astype(F32)
        first = channels + HIST_ROWS * lax.div(s * TILE, rows)
        block = jnp.zeros((TILE, sums.shape[1]), F32)
        for b, column in enumerate(columns + [high, column - high]):
            block = jnp.where(lane == first + b, column, block)
        at = pl.ds(pl.multiple_of(lax.rem(s * TILE, rows), TILE), TILE)
        sums[at] += block
        return 0

    lax.fori_loop(0, x.shape[0], one, 0)
    for shift, out in enumerate(outs):
        first = pl.multiple_of(peer(shift, len(outs)) * rows, TILE)
        out[...] = (stim[pl.ds(first, rows)] + sums[...]).astype(out.dtype)


def finish_kernel(scale, *refs):
    parts, (bias_out, hist_out, stim_out) = refs[:-3], refs[-3:]
    total = parts[0][...]
    for part in parts[1:]:
        total += part[:, part.shape[1] - total.shape[1] :].astype(F32)
    total *= scale
    channels, rows = stim_out.shape
    flat = total.T
    stim_out[...] = flat[:channels]
    for g in range(hist_out.shape[1] // rows):
        first = channels + HIST_ROWS * g
        at = slice(g * rows, (g + 1) * rows)
        hist_out[:, at] = flat[first : first + NB]
        bias_out[:, at] = flat[first + NB : first + NB + 1] + flat[first + NB + 1 : first + NB + 2]


def grad_kernel(count, extras, slots, mixed_early, mixed_late, *refs):
    recv, extra = refs[:count], refs[count : count + extras]
    outs, (table, chosen, grads) = refs[count + extras : -3], refs[-3:]
    part = recv[0].shape[1]
    rows = TILE // len(outs)
    me = lax.axis_index("unit")
    for k in range(count):
        table[pl.ds(jnp.bitwise_xor(me, k) * CAP, CAP)] = recv[k][...]
    for s in range(mixed_early.shape[0]):
        for f in range(FAN):
            chosen[s, f * part : (f + 1) * part] = table[slots[s * FAN + f]]
        mixed = jnp.concatenate([mixed_early[s], mixed_late[s]], axis=1)
        grads[s] = contract(mixed, chosen[s], (1, 1))
    for shift, out in enumerate(outs):
        first = pl.multiple_of(peer(shift, len(outs)) * rows, rows)
        block = grads[:, pl.ds(first, rows)].astype(out.dtype)
        out[:, : FAN * part] = block.reshape(out.shape[0], FAN * part)
        if extras and shift:
            out[:, FAN * part :] = extra[shift - 1][...]


def final_kernel(scale, parts_in, *refs):
    pieces_in, out = refs[:-1], refs[-1]
    halves = len(parts_in)
    count = len(pieces_in) // halves
    sums = []
    for half, part in enumerate(parts_in):
        wide = FAN * part
        mine = pieces_in[half * count : (half + 1) * count]
        total = mine[0][:, :wide].astype(F32)
        for piece in mine[1:]:
            total += piece[:, :wide].astype(F32)
        sums.append((total * scale).reshape(out.shape[0], out.shape[2], wide))
    for f in range(FAN):
        pieces = [
            total[:, :, f * part : (f + 1) * part]
            for total, part in zip(sums, parts_in, strict=True)
        ]
        out[:, f] = jnp.concatenate(pieces, axis=2)


def to_peers(pieces):
    count = len(pieces)
    got = [pieces[0]]
    for shift in range(1, count):
        pairs = [(i, (i + shift) % count) for i in range(count)]
        got.append(lax.ppermute(pieces[shift], "tm", pairs))
    return got


def to_units(pieces):
    got = [pieces[0]]
    for k in range(1, len(pieces)):
        got.append(lax.ppermute(pieces[k], "unit", [(i, i ^ k) for i in range(len(pieces))]))
    return got


def call(kernel, name, micros, **kw):
    limit = pltpu.CompilerParams(vmem_limit_bytes=VMEM_LIMIT)
    cost = pl.CostEstimate(
        flops=int(micros * FLOPS_A_MICRO), bytes_accessed=1 << 20, transcendentals=0
    )
    return pl.pallas_call(kernel, name=name, compiler_params=limit, cost_estimate=cost, **kw)


def vmem():
    return pl.BlockSpec(memory_space=pltpu.VMEM)


def smem():
    return pl.BlockSpec(memory_space=SMEM)


def whole(shape, at=None):
    spot = at or (0,) * len(shape)
    return pl.BlockSpec(shape, lambda *_: spot)


def per_tile(shape, axis=0):
    return pl.BlockSpec(shape, lambda s: tuple(s if a == axis else 0 for a in range(len(shape))))


def struct(shape, dtype):
    return jax.ShapeDtypeStruct(shape, dtype)


def shards(
    spikes, stimulus, bias, hist_weight, stim_filter, coupling_mix, coupling_target, coupling_weight
):
    time_dev, units_dev = spikes.shape
    tiles_dev = units_dev // TILE
    channels = stimulus.shape[1]
    unit_count = lax.axis_size("unit")
    time_count = lax.axis_size("tm")
    time_total = time_dev * time_count
    slots = unit_count * CAP
    late = time_dev - LAG
    toep = jnp.asarray(toeplitz())
    toep_spec = whole((2 * LAG, NB * LAG))

    hbm = pl.BlockSpec(memory_space=pltpu.HBM)
    entry = [coupling_target.T, coupling_mix, spikes, coupling_weight, toep]
    entry = [pltpu.with_memory_space_constraint(a, pltpu.HBM) for a in entry]
    x, mixed_late, tail, filt, turned, slot_table, *part_late = call(
        late_kernel,
        "late",
        5,
        in_specs=[hbm] * len(entry),
        out_specs=[vmem()] * 5 + [smem()] + [vmem()] * unit_count,
        out_shape=[
            struct((tiles_dev, TILE, time_dev), BF),
            struct((tiles_dev, TILE, late), BF),
            struct((tiles_dev, TILE, LAG), BF),
            struct((2 * LAG, 2 * LAG), BF),
            struct((tiles_dev, FAN * TILE, TILE), BF),
            struct((tiles_dev * FAN,), jnp.int32),
        ]
        + [struct((CAP * TILE + NAME_ROWS, late), BF)] * unit_count,
        scratch_shapes=[
            SMEM((FAN, tiles_dev), jnp.int32),
            SMEM(coupling_mix.shape, F32),
            pltpu.VMEM((time_dev, units_dev), jnp.int32),
            pltpu.VMEM((tiles_dev, FAN, TILE, TILE), BF),
            pltpu.VMEM((2 * LAG, NB * LAG), BF),
            pltpu.VMEM((slots, TILE, late), F32),
            SMEM((unit_count,), jnp.int32),
            SMEM((unit_count,), jnp.int32),
            pltpu.SemaphoreType.DMA((4 + time_dev // LAG,)),
        ],
    )(*entry)
    halo = lax.ppermute(tail, "tm", [(i, i + 1) for i in range(time_count - 1)])
    got_late = to_units(part_late)

    stimulus_t = stimulus.T
    logit_shape = struct((tiles_dev, TILE, time_dev), F32)
    logit, columns = call(
        logit_kernel,
        "logit",
        4,
        in_specs=[vmem()] * 6,
        out_shape=[logit_shape, struct((tiles_dev, TILE, TILE), F32)],
        scratch_shapes=[pltpu.VMEM((TILE, units_dev), F32)],
    )(x, toep, hist_weight, bias.reshape(1, -1), stim_filter.T, stimulus_t)
    anywhere = pl.BlockSpec(memory_space=pl.ANY)
    mixed_early, *part_early, logit = call(
        early_kernel,
        "early",
        2,
        in_specs=[smem()] + [vmem()] * 4 + [anywhere],
        out_specs=[vmem()] * (1 + unit_count) + [anywhere],
        out_shape=[struct((tiles_dev, TILE, LAG), BF)]
        + [struct((CAP, TILE, LAG), BF)] * unit_count
        + [logit_shape],
        scratch_shapes=[pltpu.VMEM((slots, TILE, LAG), F32)],
        input_output_aliases={5: 1 + unit_count},
    )(slot_table, halo, x, filt, turned, logit)
    got_early = to_units(part_early)
    logit_early = call(
        logit_early_kernel,
        "logit_early",
        1,
        in_specs=[vmem()] * 5,
        out_shape=struct((tiles_dev, TILE, LAG), F32),
    )(x, halo, toep, columns, logit)
    ids = call(
        names_kernel,
        "names",
        1,
        grid=(1,),
        in_specs=[whole((NAME_ROWS, LAG), (CAP * TILE // NAME_ROWS, 0))] * unit_count,
        out_specs=smem(),
        out_shape=struct((slots,), jnp.int32),
    )(*got_late)

    rows = TILE // time_count
    resids, sends = [], []
    for at, part in enumerate(HALVES):
        resid, *send = call(
            functools.partial(resid_kernel, sum(HALVES[:at])),
            "resid",
            2,
            in_specs=[smem()] + [vmem()] * (3 + 2 * unit_count),
            out_shape=[struct((tiles_dev, part, time_dev), F32)]
            + [struct((CAP, part, time_dev), BF)] * unit_count,
            scratch_shapes=[
                pltpu.VMEM((tiles_dev, part, time_dev), F32),
                pltpu.VMEM((tiles_dev, part, time_dev), BF),
            ],
        )(ids, logit, logit_early, x, *got_late, *got_early)
        resids.append(resid)
        sends.append(send)

    own_rows = units_dev // time_count
    wide = -(-(channels + HIST_ROWS * time_count) // TILE) * TILE
    own, *extra = call(
        own_kernel,
        "own",
        4,
        in_specs=[vmem()] * 6,
        out_shape=[
            struct((own_rows, wide), F32 if shift == 0 else BF) for shift in range(time_count)
        ],
        scratch_shapes=[
            pltpu.VMEM((wide, time_dev), BF),
            pltpu.VMEM((units_dev, wide), F32),
            pltpu.VMEM((own_rows, wide), F32),
        ],
    )(x, halo, toep, stimulus_t, *resids)

    grads = []
    for send, part in zip(sends, HALVES, strict=True):
        got = to_units(send)
        extras = [] if grads else extra
        widths = [FAN * part] + [FAN * part + (wide if extras else 0)] * (time_count - 1)
        pieces = call(
            functools.partial(grad_kernel, unit_count, len(extras)),
            "grad",
            2,
            in_specs=[smem()] + [vmem()] * (2 + unit_count + len(extras)),
            out_shape=[struct((own_rows, width), BF) for width in widths],
            scratch_shapes=[
                pltpu.VMEM((slots, part, time_dev), BF),
                pltpu.VMEM((tiles_dev, FAN * part, time_dev), BF),
                pltpu.VMEM((tiles_dev, TILE, FAN * part), F32),
            ],
        )(slot_table, mixed_early, mixed_late, *got, *extras)
        grads += to_peers(pieces)
    grad_bias, grad_hist, grad_stim = call(
        functools.partial(finish_kernel, 1.0 / time_total),
        "finish",
        1,
        out_shape=[
            struct((1, units_dev), F32),
            struct((NB, units_dev), F32),
            struct((channels, own_rows), F32),
        ],
    )(own, *grads[1:time_count])
    grad_coupling = call(
        functools.partial(final_kernel, 1.0 / time_total, HALVES),
        "final",
        2,
        out_shape=struct((tiles_dev, FAN, TILE // time_count, TILE), F32),
    )(*grads)
    return (grad_bias.reshape(-1), grad_hist, grad_stim.T, grad_coupling)


def solution(mesh):
    return jax.shard_map(
        shards,
        mesh=mesh,
        in_specs=(
            P("tm", "unit"),
            P("tm", None),
            P("unit"),
            P(None, "unit"),
            P("unit", None),
            P(),
            P("unit", None),
            P("unit", None, None, None),
        ),
        out_specs=(
            P("unit"),
            P(None, "unit"),
            P(("unit", "tm"), None),
            P("unit", None, "tm", None),
        ),
        check_vma=False,
    )
```

time: 117 us -> 101 us (0.86)
  local copies, waits for them, and re-layouts: 25.4 us -> 0.02 us
  waiting for transfers between devices: 22.6 us -> 29.7 us
  starting transfers between devices: 38.1 us -> 42.8 us
  Pallas kernels: 28.2 us -> 26.8 us
    unnamed x82 -> x10, local copies, waits for them, and re-layouts: 25.4 us -> 0.02 us
    ppermute x7 -> x28, starting transfers between devices: 6.34 us -> 29.2 us  [to_units(): lax.ppermute(pieces[k], 'unit', [(i, i ^ k) for i in range(len(pieces))])]
    all_to_all x3 -> x0, starting transfers between devices: 12.4 us -> none  [the longest x2 7.11 us: shards(): got = lax.all_to_all(send, 'unit', 0, 0, tiled=True)]
    ppermute x7 -> x28, waiting for transfers between devices: 4.11 us -> 13.5 us  [to_units(): lax.ppermute(pieces[k], 'unit', [(i, i ^ k) for i in range(len(pieces))])]
    ppermute x9 -> x6, waiting for transfers between devices: 8.01 us -> 16.2 us  [to_peers(): got.append(lax.ppermute(pieces[shift], 'tm', pairs))]
    ppermute x9 -> x6, starting transfers between devices: 15.8 us -> 8.71 us  [to_peers(): got.append(lax.ppermute(pieces[shift], 'tm', pairs))]
    ppermute x1, waiting for transfers between devices: 5.88 us -> 0.01 us  [shards(): halo = lax.ppermute(tail, 'tm', [(i, i + 1) for i in range(time_count - 1)])]
    all_to_all x3 -> x0, waiting for transfers between devices: 4.6 us -> none  [the longest x2 4.6 us: shards(): got = lax.all_to_all(send, 'unit', 0, 0, tiled=True)]
  transfers between devices with their start and end apart: 20 -> 35, of which waited for: 8 -> 10; matrix products, arithmetic and copies ran while one was open for 1% -> 0% of each run, Pallas kernels for 17% -> 19%
where the time goes in v4:
time: 101 us; the launch traced here: 100 us
  starting transfers between devices  42.8 us (42%)
  waiting for transfers between devices  29.7 us (29%)
  Pallas kernels  26.8 us (27%)
    ppermute x28, starting transfers between devices, to_units(): lax.ppermute(pieces[k], 'unit', [(i, i ^ k) for i in range(len(pieces))])  29.2 us
    ppermute x6, waiting for transfers between devices, to_peers(): got.append(lax.ppermute(pieces[shift], 'tm', pairs))  16.2 us
    ppermute x28, waiting for transfers between devices, to_units(): lax.ppermute(pieces[k], 'unit', [(i, i ^ k) for i in range(len(pieces))])  13.5 us
    ppermute x6, starting transfers between devices, to_peers(): got.append(lax.ppermute(pieces[shift], 'tm', pairs))  8.71 us
    pallas_call x1, Pallas kernels, shards(): call(late_kernel, 'late', 5, in_specs=[hbm] * len(entry), out_specs=[vmem...  5.44 us
    pallas_call x1, Pallas kernels, shards(): call(own_kernel, 'own', 4, in_specs=[vmem()] * 6, out_shape=[struct((own_...  5.41 us
    ppermute x1, starting transfers between devices, shards(): halo = lax.ppermute(tail, 'tm', [(i, i + 1) for i in range(time_count - 1)])  4.94 us
    pallas_call x1, Pallas kernels, shards(): call(logit_kernel, 'logit', 4, in_specs=[vmem()] * 6, out_shape=[logit_sh...  4.1 us
  transfers between devices with their start and end apart: 35, of which 10 were waited for; matrix products, arithmetic and copies ran while one was open for 0% of the time, Pallas kernels for 19%

profile of v4, /device:TPU:0, one launch (start us, length us, event | category | flops | bytes accessed | tf_op | source)
XLA Modules:
  0.0 100.2 jit_solution(16947573435577102873)
XLA Ops:
  0.7 5.4 %late.1 = (bf16[8,128,512]{2,1,0:T(8,128)(2,1)S(1)}, bf16[8,128,384]{2,1,0:T(8,128)(2,1)S(1)}, bf16[8,128,128]{2,1,0:T(8,128)(2,1)S(1)}, bf16[256,256]{1,0:T(8,1...) custom-call(s32[4,8]{1,0:T(4,128)} %bitcast.10, ...), custom_call_target="tpu_custom_call" | custom-call | flops 5500000256 | bytes 1048576 | tf_op jit(solution)/shard_map/late/pallas_call | solution.py:412
  6.1 4.9 %collective-permute-start = (bf16[8,128,128]{2,1,0:T(8,128)(2,1)S(1)}, bf16[8,128,128]{2,1,0:T(8,128)(2,1)S(1)}, u32[]{:S(2)}, u32[]{:S(2)}) collective-permute-start(bf16[8,128,128]{2,1,0:T(8,128)(2,1)S(1)} %get-tuple-element.64), channel_id=1, source_target_pairs={{0,1},{1,2},{2,3},{4,5},{5,6},{6,7},{8,9},{9,10},{10,11},{12,13},{... | collective-permute-start | bytes 786440 | tf_op jit(solution)/shard_map/ppermute | solution.py:439
  11.2 1.6 %collective-permute-start.2 = (bf16[272,384]{1,0:T(8,128)(2,1)S(1)}, bf16[272,384]{1,0:T(8,128)(2,1)S(1)}, u32[]{:S(2)}, u32[]{:S(2)}) collective-permute-start(bf16[272,384]{1,0:T(8,128)(2,1)S(1)} %get-tuple-element.67), channel_id=1, source_target_pairs={{0,8},{4,12},{8,0},{12,4},{16,24},{20,28},{24,16},{28,20},{1,9},{5... | collective-permute-start | bytes 626696 | tf_op jit(solution)/shard_map/ppermute | solution.py:362
  13.0 1.5 %collective-permute-start.4 = (bf16[272,384]{1,0:T(8,128)(2,1)S(1)}, bf16[272,384]{1,0:T(8,128)(2,1)S(1)}, u32[]{:S(2)}, u32[]{:S(2)}) collective-permute-start(bf16[272,384]{1,0:T(8,128)(2,1)S(1)} %get-tuple-element.69), channel_id=1, source_target_pairs={{0,16},{4,20},{8,24},{12,28},{16,0},{20,4},{24,8},{28,12},{1,17},{... | collective-permute-start | bytes 626696 | tf_op jit(solution)/shard_map/ppermute | solution.py:362
  14.7 4.5 %collective-permute-done.2.refs_2_ = bf16[272,384]{1,0:T(8,128)(2,1)S(1)} collective-permute-done((bf16[272,384]{1,0:T(8,128)(2,1)S(1)}, bf16[272,384]{1,0:T(8,128)(2,1)S(1)}, u32[]{:S(2)}, u32[]{:S(2)}) %collective-permute-start.2) | collective-permute-done | bytes 208928 | tf_op jit(solution)/shard_map/ppermute | solution.py:362
  19.2 2.5 %collective-permute-start.6 = (bf16[272,384]{1,0:T(8,128)(2,1)S(1)}, bf16[272,384]{1,0:T(8,128)(2,1)S(1)}, u32[]{:S(2)}, u32[]{:S(2)}) collective-permute-start(bf16[272,384]{1,0:T(8,128)(2,1)S(1)} %get-tuple-element.71), channel_id=1, source_target_pairs={{0,24},{4,28},{8,16},{12,20},{16,8},{20,12},{24,0},{28,4},{1,25},{... | collective-permute-start | bytes 626696 | tf_op jit(solution)/shard_map/ppermute | solution.py:362
  21.7 4.1 %logit.1 = (f32[8,128,512]{2,1,0:T(8,128)S(1)}, f32[8,128,128]{2,1,0:T(8,128)S(1)}) custom-call(bf16[8,128,512]{2,1,0:T(8,128)(2,1)S(1)} %get-tuple-element.63.x, bf16[256,1280]{1,0:T(8,128)(2,1)S(1)} %copy-done, f32[10,1024]{1,0:T(8,128)S(1)} %copy-done.2, f32[1,1024]{1,0:T(1,128)S(1)} %bitcast.9, bf16[64,1024]{1,0:T(8,128)(2,1)S(1)} %bitcast.6, ...), custom_call_target="tpu_custom_call" | custom-call | flops 4400000000 | bytes 1048576 | tf_op jit(solution)/shard_map/logit/pallas_call | solution.py:444
  27.2 1.8 %collective-permute-start.10 = (bf16[2,128,128]{2,1,0:T(8,128)(2,1)S(1)}, bf16[2,128,128]{2,1,0:T(8,128)(2,1)S(1)}, u32[]{:S(2)}, u32[]{:S(2)}) collective-permute-start(bf16[2,128,128]{2,1,0:T(8,128)(2,1)S(1)} %get-tuple-element.82), channel_id=1, source_target_pairs={{0,12},{4,8},{8,4},{12,0},{16,28},{20,24},{24,20},{28,16},{1,13},{... | collective-permute-start | bytes 196616 | tf_op jit(solution)/shard_map/ppermute | solution.py:362
  29.0 1.5 %collective-permute-start.11 = (bf16[2,128,128]{2,1,0:T(8,128)(2,1)S(1)}, bf16[2,128,128]{2,1,0:T(8,128)(2,1)S(1)}, u32[]{:S(2)}, u32[]{:S(2)}) collective-permute-start(bf16[2,128,128]{2,1,0:T(8,128)(2,1)S(1)} %get-tuple-element.83), channel_id=1, source_target_pairs={{0,16},{4,20},{8,24},{12,28},{16,0},{20,4},{24,8},{28,12},{1,17},{... | collective-permute-start | bytes 196616 | tf_op jit(solution)/shard_map/ppermute | solution.py:362
  30.5 3.0 %collective-permute-done.5.refs_5_ = bf16[272,384]{1,0:T(8,128)(2,1)S(1)} collective-permute-done((bf16[272,384]{1,0:T(8,128)(2,1)S(1)}, bf16[272,384]{1,0:T(8,128)(2,1)S(1)}, u32[]{:S(2)}, u32[]{:S(2)}) %collective-permute-start.5) | collective-permute-done | bytes 208928 | tf_op jit(solution)/shard_map/ppermute | solution.py:362
  34.2 2.0 %collective-permute-start.12 = (bf16[2,128,128]{2,1,0:T(8,128)(2,1)S(1)}, bf16[2,128,128]{2,1,0:T(8,128)(2,1)S(1)}, u32[]{:S(2)}, u32[]{:S(2)}) collective-permute-start(bf16[2,128,128]{2,1,0:T(8,128)(2,1)S(1)} %get-tuple-element.84), channel_id=1, source_target_pairs={{0,20},{4,16},{8,28},{12,24},{16,4},{20,0},{24,12},{28,8},{1,21},{... | collective-permute-start | bytes 196616 | tf_op jit(solution)/shard_map/ppermute | solution.py:362
  39.3 1.5 %collective-permute-start.9 = (bf16[2,128,128]{2,1,0:T(8,128)(2,1)S(1)}, bf16[2,128,128]{2,1,0:T(8,128)(2,1)S(1)}, u32[]{:S(2)}, u32[]{:S(2)}) collective-permute-start(bf16[2,128,128]{2,1,0:T(8,128)(2,1)S(1)} %get-tuple-element.81), channel_id=1, source_target_pairs={{0,8},{4,12},{8,0},{12,4},{16,24},{20,28},{24,16},{28,20},{1,9},{5... | collective-permute-start | bytes 196616 | tf_op jit(solution)/shard_map/ppermute | solution.py:362
  40.8 2.3 %logit_early.1 = f32[8,128,128]{2,1,0:T(8,128)S(1)} custom-call(bf16[8,128,512]{2,1,0:T(8,128)(2,1)S(1)} %get-tuple-element.63.x, bf16[8,128,128]{2,1,0:T(8,128)(2,1)S(1)} %collective-permute-done.halo, bf16[256,1280]{1,0:T(8,128)(2,1)S(1)} %copy-done, f32[8,128,128]{2,1,0:T(8,128)S(1)} %get-tuple-element.78.columns, f32[8,128,512]{2,1,0:T(8,128)S(1)} %get-tuple-element.77.logit), custom_call_target="tpu_custom_call" | custom-call | flops 1100000000 | bytes 1048576 | tf_op jit(solution)/shard_map/logit_early/pallas_call | solution.py:466
  51.4 1.9 %collective-permute-start.20 = (bf16[2,64,512]{2,1,0:T(8,128)(2,1)S(1)}, bf16[2,64,512]{2,1,0:T(8,128)(2,1)S(1)}, u32[]{:S(2)}, u32[]{:S(2)}) collective-permute-start(bf16[2,64,512]{2,1,0:T(8,128)(2,1)S(1)} %get-tuple-element.98), channel_id=1, source_target_pairs={{0,24},{4,28},{8,16},{12,20},{16,8},{20,12},{24,0},{28,4},{1,25},{... | collective-permute-start | bytes 393224 | tf_op jit(solution)/shard_map/ppermute | solution.py:362
  54.9 5.4 %own.1 = (f32[256,128]{1,0:T(8,128)S(1)}, bf16[256,128]{1,0:T(8,128)(2,1)S(1)}, bf16[256,128]{1,0:T(8,128)(2,1)S(1)}, bf16[256,128]{1,0:T(8,128)(2,1)S(1)}) custom-call(bf16[8,128,512]{2,1,0:T(8,128)(2,1)S(1)} %get-tuple-element.63.x, bf16[8,128,128]{2,1,0:T(8,128)(2,1)S(1)} %collective-permute-done.halo, bf16[256,1280]{1,0:T(8,128)(2,1)S(1)} %copy-done, ...), custom_call_target="tpu_custom_call" | custom-call | flops 4400000000 | bytes 1048576 | tf_op jit(solution)/shard_map/own/pallas_call | solution.py:503
  60.4 1.8 %collective-permute-start.27 = (bf16[2,64,512]{2,1,0:T(8,128)(2,1)S(1)}, bf16[2,64,512]{2,1,0:T(8,128)(2,1)S(1)}, u32[]{:S(2)}, u32[]{:S(2)}) collective-permute-start(bf16[2,64,512]{2,1,0:T(8,128)(2,1)S(1)} %get-tuple-element.113), channel_id=1, source_target_pairs={{0,12},{4,8},{8,4},{12,0},{16,28},{20,24},{24,20},{28,16},{1,13},{... | collective-permute-start | bytes 393224 | tf_op jit(solution)/shard_map/ppermute | solution.py:362
  67.1 1.5 %grad.2 = (bf16[256,256]{1,0:T(8,128)(2,1)S(1)}, bf16[256,384]{1,0:T(8,128)(2,1)S(1)}, bf16[256,384]{1,0:T(8,128)(2,1)S(1)}, bf16[256,384]{1,0:T(8,128)(2,1)S(1)}) custom-call(s32[32]{0:T(128)S(1)} %get-tuple-element.73.slots, bf16[8,128,128]{2,1,0:T(8,128)(2,1)S(1)} %get-tuple-element.90.mixed_early, bf16[8,128,384]{2,1,0:T(8,128)(2,1)S(1)} %get-tuple-element.91.mixed_late, ...), custom_call_target="tpu_custom_call" | custom-call | flops 2200000000 | bytes 1048576 | tf_op jit(solution)/shard_map/grad/pallas_call | solution.py:523
  68.6 1.6 %collective-permute-start.22 = (bf16[256,384]{1,0:T(8,128)(2,1)S(1)}, bf16[256,384]{1,0:T(8,128)(2,1)S(1)}, u32[]{:S(2)}, u32[]{:S(2)}) collective-permute-start(bf16[256,384]{1,0:T(8,128)(2,1)S(1)} %get-tuple-element.103), channel_id=1, source_target_pairs={{0,1},{1,2},{2,3},{3,0},{4,5},{5,6},{6,7},{7,4},{8,9},{9,10},{10,1... | collective-permute-start | bytes 589832 | tf_op jit(solution)/shard_map/ppermute | solution.py:355
  71.3 3.4 %collective-permute-done.29.refs_5_ = bf16[2,64,512]{2,1,0:T(8,128)(2,1)S(1)} collective-permute-done((bf16[2,64,512]{2,1,0:T(8,128)(2,1)S(1)}, bf16[2,64,512]{2,1,0:T(8,128)(2,1)S(1)}, u32[]{:S(2)}, u32[]{:S(2)}) %collective-permute-start.29) | collective-permute-done | bytes 131104 | tf_op jit(solution)/shard_map/ppermute | solution.py:362
  76.1 1.5 %grad.3 = (bf16[256,256]{1,0:T(8,128)(2,1)S(1)}, bf16[256,256]{1,0:T(8,128)(2,1)S(1)}, bf16[256,256]{1,0:T(8,128)(2,1)S(1)}, bf16[256,256]{1,0:T(8,128)(2,1)S(1)}) custom-call(s32[32]{0:T(128)S(1)} %get-tuple-element.73.slots, bf16[8,128,128]{2,1,0:T(8,128)(2,1)S(1)} %get-tuple-element.90.mixed_early, bf16[8,128,384]{2,1,0:T(8,128)(2,1)S(1)} %get-tuple-element.91.mixed_late, ...), custom_call_target="tpu_custom_call" | custom-call | flops 2200000000 | bytes 1048576 | tf_op jit(solution)/shard_map/grad/pallas_call | solution.py:523
  78.3 2.6 %collective-permute-start.33 = (bf16[256,256]{1,0:T(8,128)(2,1)S(1)}, bf16[256,256]{1,0:T(8,128)(2,1)S(1)}, u32[]{:S(2)}, u32[]{:S(2)}) collective-permute-start(bf16[256,256]{1,0:T(8,128)(2,1)S(1)} %get-tuple-element.120), channel_id=1, source_target_pairs={{0,2},{1,3},{2,0},{3,1},{4,6},{5,7},{6,4},{7,5},{8,10},{9,11},{10,... | collective-permute-start | bytes 393224 | tf_op jit(solution)/shard_map/ppermute | solution.py:355
  82.2 4.6 %collective-permute-done.23.refs_2_ = bf16[256,384]{1,0:T(8,128)(2,1)S(1)} collective-permute-done((bf16[256,384]{1,0:T(8,128)(2,1)S(1)}, bf16[256,384]{1,0:T(8,128)(2,1)S(1)}, u32[]{:S(2)}, u32[]{:S(2)}) %collective-permute-start.23) | collective-permute-done | bytes 196640 | tf_op jit(solution)/shard_map/ppermute | solution.py:355
  87.5 2.1 %collective-permute-done.32.refs_5_ = bf16[256,256]{1,0:T(8,128)(2,1)S(1)} collective-permute-done((bf16[256,256]{1,0:T(8,128)(2,1)S(1)}, bf16[256,256]{1,0:T(8,128)(2,1)S(1)}, u32[]{:S(2)}, u32[]{:S(2)}) %collective-permute-start.32) | collective-permute-done | bytes 131104 | tf_op jit(solution)/shard_map/ppermute | solution.py:355
  89.6 9.6 %collective-permute-done.33.refs_6_ = bf16[256,256]{1,0:T(8,128)(2,1)S(1)} collective-permute-done((bf16[256,256]{1,0:T(8,128)(2,1)S(1)}, bf16[256,256]{1,0:T(8,128)(2,1)S(1)}, u32[]{:S(2)}, u32[]{:S(2)}) %collective-permute-start.33) | collective-permute-done | bytes 131104 | tf_op jit(solution)/shard_map/ppermute | solution.py:355
  (68 shorter events, 27.0 us)
Async XLA Ops:
  6.1 15.5 %collective-permute-start = (bf16[8,128,128]{2,1,0:T(8,128)(2,1)S(1)}, bf16[8,128,128]{2,1,0:T(8,128)(2,1)S(1)}, u32[]{:S(2)}, u32[]{:S(2)}) collective-permute-start(bf16[8,128,128]{2,1,0:T(8,128)(2,1)S(1)} %get-tuple-element.64), channel_id=1, source_target_pairs={{0,1},{1,2},{2,3},{4,5},{5,6},{6,7},{8,9},{9,10},{10,11},{12,13},{... | collective-permute-start | bytes 786440 | tf_op jit(solution)/shard_map/ppermute | solution.py:439
  12.7 14.5 %collective-permute-start.3 = (bf16[272,384]{1,0:T(8,128)(2,1)S(1)}, bf16[272,384]{1,0:T(8,128)(2,1)S(1)}, u32[]{:S(2)}, u32[]{:S(2)}) collective-permute-start(bf16[272,384]{1,0:T(8,128)(2,1)S(1)} %get-tuple-element.68), channel_id=1, source_target_pairs={{0,12},{4,8},{8,4},{12,0},{16,28},{20,24},{24,20},{28,16},{1,13},{... | collective-permute-start | bytes 626696 | tf_op jit(solution)/shard_map/ppermute | solution.py:362
  13.0 16.0 %collective-permute-start.4 = (bf16[272,384]{1,0:T(8,128)(2,1)S(1)}, bf16[272,384]{1,0:T(8,128)(2,1)S(1)}, u32[]{:S(2)}, u32[]{:S(2)}) collective-permute-start(bf16[272,384]{1,0:T(8,128)(2,1)S(1)} %get-tuple-element.69), channel_id=1, source_target_pairs={{0,16},{4,20},{8,24},{12,28},{16,0},{20,4},{24,8},{28,12},{1,17},{... | collective-permute-start | bytes 626696 | tf_op jit(solution)/shard_map/ppermute | solution.py:362
  14.6 18.9 %collective-permute-start.5 = (bf16[272,384]{1,0:T(8,128)(2,1)S(1)}, bf16[272,384]{1,0:T(8,128)(2,1)S(1)}, u32[]{:S(2)}, u32[]{:S(2)}) collective-permute-start(bf16[272,384]{1,0:T(8,128)(2,1)S(1)} %get-tuple-element.70), channel_id=1, source_target_pairs={{0,20},{4,16},{8,28},{12,24},{16,4},{20,0},{24,12},{28,8},{1,21},{... | collective-permute-start | bytes 626696 | tf_op jit(solution)/shard_map/ppermute | solution.py:362
  19.2 14.3 %collective-permute-start.6 = (bf16[272,384]{1,0:T(8,128)(2,1)S(1)}, bf16[272,384]{1,0:T(8,128)(2,1)S(1)}, u32[]{:S(2)}, u32[]{:S(2)}) collective-permute-start(bf16[272,384]{1,0:T(8,128)(2,1)S(1)} %get-tuple-element.71), channel_id=1, source_target_pairs={{0,24},{4,28},{8,16},{12,20},{16,8},{20,12},{24,0},{28,4},{1,25},{... | collective-permute-start | bytes 626696 | tf_op jit(solution)/shard_map/ppermute | solution.py:362
  21.6 11.8 %collective-permute-start.7 = (bf16[272,384]{1,0:T(8,128)(2,1)S(1)}, bf16[272,384]{1,0:T(8,128)(2,1)S(1)}, u32[]{:S(2)}, u32[]{:S(2)}) collective-permute-start(bf16[272,384]{1,0:T(8,128)(2,1)S(1)} %get-tuple-element.72), channel_id=1, source_target_pairs={{0,28},{4,24},{8,20},{12,16},{16,12},{20,8},{24,4},{28,0},{1,29},{... | collective-permute-start | bytes 626696 | tf_op jit(solution)/shard_map/ppermute | solution.py:362
  27.2 10.8 %collective-permute-start.10 = (bf16[2,128,128]{2,1,0:T(8,128)(2,1)S(1)}, bf16[2,128,128]{2,1,0:T(8,128)(2,1)S(1)}, u32[]{:S(2)}, u32[]{:S(2)}) collective-permute-start(bf16[2,128,128]{2,1,0:T(8,128)(2,1)S(1)} %get-tuple-element.82), channel_id=1, source_target_pairs={{0,12},{4,8},{8,4},{12,0},{16,28},{20,24},{24,20},{28,16},{1,13},{... | collective-permute-start | bytes 196616 | tf_op jit(solution)/shard_map/ppermute | solution.py:362
  29.0 10.3 %collective-permute-start.11 = (bf16[2,128,128]{2,1,0:T(8,128)(2,1)S(1)}, bf16[2,128,128]{2,1,0:T(8,128)(2,1)S(1)}, u32[]{:S(2)}, u32[]{:S(2)}) collective-permute-start(bf16[2,128,128]{2,1,0:T(8,128)(2,1)S(1)} %get-tuple-element.83), channel_id=1, source_target_pairs={{0,16},{4,20},{8,24},{12,28},{16,0},{20,4},{24,8},{28,12},{1,17},{... | collective-permute-start | bytes 196616 | tf_op jit(solution)/shard_map/ppermute | solution.py:362
  34.2 8.8 %collective-permute-start.12 = (bf16[2,128,128]{2,1,0:T(8,128)(2,1)S(1)}, bf16[2,128,128]{2,1,0:T(8,128)(2,1)S(1)}, u32[]{:S(2)}, u32[]{:S(2)}) collective-permute-start(bf16[2,128,128]{2,1,0:T(8,128)(2,1)S(1)} %get-tuple-element.84), channel_id=1, source_target_pairs={{0,20},{4,16},{8,28},{12,24},{16,4},{20,0},{24,12},{28,8},{1,21},{... | collective-permute-start | bytes 196616 | tf_op jit(solution)/shard_map/ppermute | solution.py:362
  48.9 11.5 %collective-permute-start.17 = (bf16[2,64,512]{2,1,0:T(8,128)(2,1)S(1)}, bf16[2,64,512]{2,1,0:T(8,128)(2,1)S(1)}, u32[]{:S(2)}, u32[]{:S(2)}) collective-permute-start(bf16[2,64,512]{2,1,0:T(8,128)(2,1)S(1)} %get-tuple-element.95), channel_id=1, source_target_pairs={{0,12},{4,8},{8,4},{12,0},{16,28},{20,24},{24,20},{28,16},{1,13},{... | collective-permute-start | bytes 393224 | tf_op jit(solution)/shard_map/ppermute | solution.py:362
  49.7 12.4 %collective-permute-start.18 = (bf16[2,64,512]{2,1,0:T(8,128)(2,1)S(1)}, bf16[2,64,512]{2,1,0:T(8,128)(2,1)S(1)}, u32[]{:S(2)}, u32[]{:S(2)}) collective-permute-start(bf16[2,64,512]{2,1,0:T(8,128)(2,1)S(1)} %get-tuple-element.96), channel_id=1, source_target_pairs={{0,16},{4,20},{8,24},{12,28},{16,0},{20,4},{24,8},{28,12},{1,17},{... | collective-permute-start | bytes 393224 | tf_op jit(solution)/shard_map/ppermute | solution.py:362
  51.3 12.1 %collective-permute-start.19 = (bf16[2,64,512]{2,1,0:T(8,128)(2,1)S(1)}, bf16[2,64,512]{2,1,0:T(8,128)(2,1)S(1)}, u32[]{:S(2)}, u32[]{:S(2)}) collective-permute-start(bf16[2,64,512]{2,1,0:T(8,128)(2,1)S(1)} %get-tuple-element.97), channel_id=1, source_target_pairs={{0,20},{4,16},{8,28},{12,24},{16,4},{20,0},{24,12},{28,8},{1,21},{... | collective-permute-start | bytes 393224 | tf_op jit(solution)/shard_map/ppermute | solution.py:362
  51.4 13.4 %collective-permute-start.20 = (bf16[2,64,512]{2,1,0:T(8,128)(2,1)S(1)}, bf16[2,64,512]{2,1,0:T(8,128)(2,1)S(1)}, u32[]{:S(2)}, u32[]{:S(2)}) collective-permute-start(bf16[2,64,512]{2,1,0:T(8,128)(2,1)S(1)} %get-tuple-element.98), channel_id=1, source_target_pairs={{0,24},{4,28},{8,16},{12,20},{16,8},{20,12},{24,0},{28,4},{1,25},{... | collective-permute-start | bytes 393224 | tf_op jit(solution)/shard_map/ppermute | solution.py:362
  54.2 11.8 %collective-permute-start.21 = (bf16[2,64,512]{2,1,0:T(8,128)(2,1)S(1)}, bf16[2,64,512]{2,1,0:T(8,128)(2,1)S(1)}, u32[]{:S(2)}, u32[]{:S(2)}) collective-permute-start(bf16[2,64,512]{2,1,0:T(8,128)(2,1)S(1)} %get-tuple-element.99), channel_id=1, source_target_pairs={{0,28},{4,24},{8,20},{12,16},{16,12},{20,8},{24,4},{28,0},{1,29},{... | collective-permute-start | bytes 393224 | tf_op jit(solution)/shard_map/ppermute | solution.py:362
  60.4 8.2 %collective-permute-start.27 = (bf16[2,64,512]{2,1,0:T(8,128)(2,1)S(1)}, bf16[2,64,512]{2,1,0:T(8,128)(2,1)S(1)}, u32[]{:S(2)}, u32[]{:S(2)}) collective-permute-start(bf16[2,64,512]{2,1,0:T(8,128)(2,1)S(1)} %get-tuple-element.113), channel_id=1, source_target_pairs={{0,12},{4,8},{8,4},{12,0},{16,28},{20,24},{24,20},{28,16},{1,13},{... | collective-permute-start | bytes 393224 | tf_op jit(solution)/shard_map/ppermute | solution.py:362
  63.3 11.4 %collective-permute-start.29 = (bf16[2,64,512]{2,1,0:T(8,128)(2,1)S(1)}, bf16[2,64,512]{2,1,0:T(8,128)(2,1)S(1)}, u32[]{:S(2)}, u32[]{:S(2)}) collective-permute-start(bf16[2,64,512]{2,1,0:T(8,128)(2,1)S(1)} %get-tuple-element.115), channel_id=1, source_target_pairs={{0,20},{4,16},{8,28},{12,24},{16,4},{20,0},{24,12},{28,8},{1,21},{... | collective-permute-start | bytes 393224 | tf_op jit(solution)/shard_map/ppermute | solution.py:362
  64.8 11.3 %collective-permute-start.30 = (bf16[2,64,512]{2,1,0:T(8,128)(2,1)S(1)}, bf16[2,64,512]{2,1,0:T(8,128)(2,1)S(1)}, u32[]{:S(2)}, u32[]{:S(2)}) collective-permute-start(bf16[2,64,512]{2,1,0:T(8,128)(2,1)S(1)} %get-tuple-element.116), channel_id=1, source_target_pairs={{0,24},{4,28},{8,16},{12,20},{16,8},{20,12},{24,0},{28,4},{1,25},{... | collective-permute-start | bytes 393224 | tf_op jit(solution)/shard_map/ppermute | solution.py:362
  66.0 10.1 %collective-permute-start.31 = (bf16[2,64,512]{2,1,0:T(8,128)(2,1)S(1)}, bf16[2,64,512]{2,1,0:T(8,128)(2,1)S(1)}, u32[]{:S(2)}, u32[]{:S(2)}) collective-permute-start(bf16[2,64,512]{2,1,0:T(8,128)(2,1)S(1)} %get-tuple-element.117), channel_id=1, source_target_pairs={{0,28},{4,24},{8,20},{12,16},{16,12},{20,8},{24,4},{28,0},{1,29},{... | collective-permute-start | bytes 393224 | tf_op jit(solution)/shard_map/ppermute | solution.py:362
  68.6 12.3 %collective-permute-start.22 = (bf16[256,384]{1,0:T(8,128)(2,1)S(1)}, bf16[256,384]{1,0:T(8,128)(2,1)S(1)}, u32[]{:S(2)}, u32[]{:S(2)}) collective-permute-start(bf16[256,384]{1,0:T(8,128)(2,1)S(1)} %get-tuple-element.103), channel_id=1, source_target_pairs={{0,1},{1,2},{2,3},{3,0},{4,5},{5,6},{6,7},{7,4},{8,9},{9,10},{10,1... | collective-permute-start | bytes 589832 | tf_op jit(solution)/shard_map/ppermute | solution.py:355
  70.2 16.6 %collective-permute-start.23 = (bf16[256,384]{1,0:T(8,128)(2,1)S(1)}, bf16[256,384]{1,0:T(8,128)(2,1)S(1)}, u32[]{:S(2)}, u32[]{:S(2)}) collective-permute-start(bf16[256,384]{1,0:T(8,128)(2,1)S(1)} %get-tuple-element.104), channel_id=1, source_target_pairs={{0,2},{1,3},{2,0},{3,1},{4,6},{5,7},{6,4},{7,5},{8,10},{9,11},{10,... | collective-permute-start | bytes 589832 | tf_op jit(solution)/shard_map/ppermute | solution.py:355
  74.7 12.1 %collective-permute-start.24 = (bf16[256,384]{1,0:T(8,128)(2,1)S(1)}, bf16[256,384]{1,0:T(8,128)(2,1)S(1)}, u32[]{:S(2)}, u32[]{:S(2)}) collective-permute-start(bf16[256,384]{1,0:T(8,128)(2,1)S(1)} %get-tuple-element.105), channel_id=1, source_target_pairs={{0,3},{1,0},{2,1},{3,2},{4,7},{5,4},{6,5},{7,6},{8,11},{9,8},{10,9... | collective-permute-start | bytes 589832 | tf_op jit(solution)/shard_map/ppermute | solution.py:355
  77.6 12.0 %collective-permute-start.32 = (bf16[256,256]{1,0:T(8,128)(2,1)S(1)}, bf16[256,256]{1,0:T(8,128)(2,1)S(1)}, u32[]{:S(2)}, u32[]{:S(2)}) collective-permute-start(bf16[256,256]{1,0:T(8,128)(2,1)S(1)} %get-tuple-element.119), channel_id=1, source_target_pairs={{0,1},{1,2},{2,3},{3,0},{4,5},{5,6},{6,7},{7,4},{8,9},{9,10},{10,1... | collective-permute-start | bytes 393224 | tf_op jit(solution)/shard_map/ppermute | solution.py:355
  78.3 20.9 %collective-permute-start.33 = (bf16[256,256]{1,0:T(8,128)(2,1)S(1)}, bf16[256,256]{1,0:T(8,128)(2,1)S(1)}, u32[]{:S(2)}, u32[]{:S(2)}) collective-permute-start(bf16[256,256]{1,0:T(8,128)(2,1)S(1)} %get-tuple-element.120), channel_id=1, source_target_pairs={{0,2},{1,3},{2,0},{3,1},{4,6},{5,7},{6,4},{7,5},{8,10},{9,11},{10,... | collective-permute-start | bytes 393224 | tf_op jit(solution)/shard_map/ppermute | solution.py:355
  80.9 18.3 %collective-permute-start.34 = (bf16[256,256]{1,0:T(8,128)(2,1)S(1)}, bf16[256,256]{1,0:T(8,128)(2,1)S(1)}, u32[]{:S(2)}, u32[]{:S(2)}) collective-permute-start(bf16[256,256]{1,0:T(8,128)(2,1)S(1)} %get-tuple-element.121), channel_id=1, source_target_pairs={{0,3},{1,0},{2,1},{3,2},{4,7},{5,4},{6,5},{7,6},{8,11},{9,8},{10,9... | collective-permute-start | bytes 393224 | tf_op jit(solution)/shard_map/ppermute | solution.py:355
  (16 other events, 167.2 us)

commit v5 on v4

--- a/solution.py
+++ b/solution.py
@@ -18,8 +18,8 @@
 BF = jnp.bfloat16
 F32 = jnp.float32
 SMEM = pltpu.SMEM
-VMEM_LIMIT = 20 << 20
-FLOPS_A_MICRO = 1.1e9
+VMEM_LIMIT = 16 << 20
+FLOPS_A_MICRO = 1e7
 HIST_ROWS = 16
 NAME_ROWS = 16
 
@@ -89,8 +89,8 @@
 
 
 def late_kernel(target_hbm, mix_hbm, spikes, weight, toep, *refs):
-    x, mixed, tail, filt, turned, slots = refs[:6]
-    parts = refs[6:-9]
+    x, mixed, filt, turned, slots = refs[:5]
+    parts = refs[5:-9]
     target, mix, counts, weights, bases, total, lowest, highest, sems = refs[-9:]
     tiles_dev = x.shape[0]
     blocks = x.shape[2] // LAG
@@ -120,7 +120,6 @@
             got = mix_window(jnp.concatenate([before, now], axis=1), filt[...])
             mixed[:, :, (k - 1) * LAG : k * LAG] = got.reshape(tiles_dev, TILE, LAG)
         before = now
-    tail[...] = before.reshape(tiles_dev, TILE, LAG)
 
     pulls[1].wait()
     for s in range(tiles_dev):
@@ -128,31 +127,34 @@
             turned[s, f * TILE : (f + 1) * TILE] = weights[s, f].astype(F32).T.astype(BF)
     add_partials(slots, turned, mixed, total)
 
-    row = lax.broadcasted_iota(jnp.int32, (NAME_ROWS, mixed.shape[2]), 0)
+    row = lax.broadcasted_iota(jnp.int32, (NAME_ROWS, LAG), 0)
     me = lax.axis_index("unit")
-    for k, part in enumerate(parts):
-        o = jnp.bitwise_xor(me, k)
+    for j, part in enumerate(parts):
+        o = jnp.bitwise_xor(me, j)
+        for k in range(1, blocks):
+            for q in range(CAP):
+                at = (k * CAP + q) * TILE
+                block = total[o * CAP + q, :, (k - 1) * LAG : k * LAG]
+                part[at : at + TILE] = block.astype(BF)
         high = highest[o]
         low = jnp.where(high < 0, -1, lowest[o])
-        for q in range(CAP):
-            part[q * TILE : (q + 1) * TILE] = total[o * CAP + q].astype(BF)
         names = jnp.where(row == 0, low, jnp.where(row == 1, high, 0))
-        part[CAP * TILE :] = names.astype(F32).astype(BF)
-
-
-def early_kernel(slots, halo, x, filt, turned, kept, mixed_out, *refs):
-    outs, total = refs[:-2], refs[-1]
-    del kept
+        part[blocks * CAP * TILE :] = names.astype(F32).astype(BF)
+
+
+def early_kernel(slots, halo, x, filt, turned, *refs):
+    kept = len(refs) // 2 - 1
+    mixed_out, outs, total = refs[kept], refs[kept + 1 : -1], refs[-1]
     units = x.shape[0] * TILE
-    window = jnp.concatenate(
-        [halo[...].reshape(units, LAG), x[:, :, :LAG].reshape(units, LAG)], axis=1
-    )
+    now = halo[...].astype(F32).T.astype(BF)
+    window = jnp.concatenate([now, x[...].reshape(units, LAG)], axis=1)
     mixed_out[...] = mix_window(window, filt[...]).reshape(mixed_out.shape)
     add_partials(slots, turned, mixed_out, total)
     me = lax.axis_index("unit")
     for k, out in enumerate(outs):
         for q in range(CAP):
-            out[q] = total[jnp.bitwise_xor(me, k) * CAP + q].astype(BF)
+            block = total[jnp.bitwise_xor(me, k) * CAP + q]
+            out[q * TILE : (q + 1) * TILE] = block.astype(BF)
 
 
 def names_kernel(*refs):
@@ -167,20 +169,7 @@
     return jnp.concatenate([extended[:, k * LAG : (k + 2) * LAG] for k in range(count)], axis=0)
 
 
-def add_history(total, window, toep, columns):
-    count = window.shape[0] // TILE
-    for c in range(0, NB, 2):
-        both = jnp.dot(window, toep[:, c * LAG : (c + 2) * LAG], preferred_element_type=F32)
-        for b in (c, c + 1):
-            weight = columns[:, b : b + 1]
-            piece = both[:, (b - c) * LAG : (b - c + 1) * LAG]
-            total = [
-                total[k] + weight * piece[k * TILE : (k + 1) * TILE] for k in range(count)
-            ]
-    return total
-
-
-def logit_kernel(x, toep, hist_weight, bias, stim_filter, stimulus, out, columns_out, rows):
+def logit_kernel(x, halo, toep, hist_weight, bias, stim_filter, stimulus, out, history, rows):
     rows[...] = jnp.zeros_like(rows)
     rows[:NB] = hist_weight[...]
     rows[NB : NB + 1] = bias[...]
@@ -189,11 +178,19 @@
     def one(s, _):
         units = pl.ds(pl.multiple_of(s * TILE, TILE), TILE)
         columns = rows[:, units].T
-        columns_out[s] = columns
         start = contract(stim_filter[:, units], stimulus[...], (0, 0)) + columns[:, NB : NB + 1]
         total = [start[:, k * LAG : (k + 1) * LAG] for k in range(blocks)]
-        window = windows(x[s], blocks - 1)
-        total[1:] = add_history(total[1:], window, toep, columns)
+        before = halo[:, units].astype(F32).T.astype(BF)
+        window = windows(jnp.concatenate([before, x[s]], axis=1), blocks)
+        for c in range(0, NB, 2):
+            both = jnp.dot(window, toep[:, c * LAG : (c + 2) * LAG], preferred_element_type=F32)
+            for b in (c, c + 1):
+                weight = columns[:, b : b + 1]
+                piece = both[:, (b - c) * LAG : (b - c + 1) * LAG]
+                for k in range(blocks):
+                    part = piece[k * TILE : (k + 1) * TILE]
+                    history[s, b, :, k * LAG : (k + 1) * LAG] = part
+                    total[k] += weight * part
         for k in range(blocks):
             out[s, :, k * LAG : (k + 1) * LAG] = total[k]
         return 0
@@ -201,32 +198,23 @@
     lax.fori_loop(0, x.shape[0], one, 0)
 
 
-def logit_early_kernel(x, halo, toep, columns, logit, out):
-    def one(s, _):
-        window = jnp.concatenate([halo[s], x[s, :, :LAG]], axis=1)
-        (out[s],) = add_history([logit[s, :, :LAG]], window, toep, columns[s])
-        return 0
-
-    lax.fori_loop(0, x.shape[0], one, 0)
-
-
-def resid_kernel(first, ids, logit, logit_early, x, *refs):
+def resid_kernel(first, ids, logit, x, *refs):
     count = ids.shape[0] // CAP
-    late, early, (resid, *sends) = refs[:count], refs[count : 2 * count], refs[2 * count : -2]
-    total, rounded = refs[-2:]
+    got, (resid, *sends), (total, rounded) = refs[:count], refs[count:-2], refs[-2:]
     part = resid.shape[1]
     mine = slice(first, first + part)
-    total[:, :, LAG:] = logit[:, mine, LAG:]
-    total[:, :, :LAG] = logit_early[:, mine]
-    for k in range(count):
+    total[...] = logit[:, mine]
+    for j in range(count):
         for q in range(CAP):
-            tile = ids[k * CAP + q]
+            tile = ids[j * CAP + q]
 
             @pl.when(tile >= 0)
             def _():
-                start = q * TILE + first
-                total[tile, :, LAG:] += late[k][start : start + part].astype(F32)
-                total[tile, :, :LAG] += early[k][q, mine].astype(F32)
+                for k in range(x.shape[2] // LAG):
+                    start = (k * CAP + q) * TILE + first
+                    total[tile, :, k * LAG : (k + 1) * LAG] += got[j][start : start + part].astype(
+                        F32
+                    )
 
     for j in range(logit.shape[0]):
         r = x[j, mine].astype(F32) - jnp.exp(total[j])
@@ -249,32 +237,27 @@
     return lax.rem(lax.axis_index("tm") + shift, count)
 
 
-def own_kernel(x, halo, toep, stimulus, resid_a, resid_b, *refs):
+def own_kernel(history, stimulus, resid_a, resid_b, *refs):
     outs, (wide, stim, sums) = refs[:-3], refs[-3:]
     channels = stimulus.shape[0]
     rows = sums.shape[0]
-    blocks = x.shape[2] // LAG
     wide[...] = jnp.zeros_like(wide)
     wide[:channels] = stimulus[...]
     sums[...] = jnp.zeros_like(sums)
     lane = lax.broadcasted_iota(jnp.int32, (TILE, sums.shape[1]), 1)
 
+    def folded(value):
+        total = value[:, :LAG]
+        for k in range(LAG, value.shape[1], LAG):
+            total += value[:, k : k + LAG]
+        return jnp.sum(total, axis=1, keepdims=True)
+
     def one(s, _):
         resid = jnp.concatenate([resid_a[s], resid_b[s]], axis=0)
         units = pl.ds(pl.multiple_of(s * TILE, TILE), TILE)
         stim[units] = contract(resid.astype(BF), wide[...], (1, 1))
-        window = windows(jnp.concatenate([halo[s], x[s]], axis=1), blocks)
-        parts = [resid[:, k * LAG : (k + 1) * LAG] for k in range(blocks)]
-        columns = []
-        for c in range(0, NB, 2):
-            both = jnp.dot(window, toep[:, c * LAG : (c + 2) * LAG], preferred_element_type=F32)
-            for b in (c, c + 1):
-                piece = both[:, (b - c) * LAG : (b - c + 1) * LAG]
-                total = parts[0] * piece[:TILE]
-                for k in range(1, blocks):
-                    total += parts[k] * piece[k * TILE : (k + 1) * TILE]
-                columns.append(jnp.sum(total, axis=1, keepdims=True))
-        column = jnp.sum(sum(parts[1:], parts[0]), axis=1, keepdims=True)
+        columns = [folded(resid * history[s, b]) for b in range(NB)]
+        column = folded(resid)
         high = column.astype(BF).astype(F32)
         first = channels + HIST_ROWS * lax.div(s * TILE, rows)
         block = jnp.zeros((TILE, sums.shape[1]), F32)
@@ -284,7 +267,7 @@
         sums[at] += block
         return 0
 
-    lax.fori_loop(0, x.shape[0], one, 0)
+    lax.fori_loop(0, history.shape[0], one, 0)
     for shift, out in enumerate(outs):
         first = pl.multiple_of(peer(shift, len(outs)) * rows, TILE)
         out[...] = (stim[pl.ds(first, rows)] + sums[...]).astype(out.dtype)
@@ -392,6 +375,10 @@
     return jax.ShapeDtypeStruct(shape, dtype)
 
 
+def far(array):
+    return pltpu.with_memory_space_constraint(array, pltpu.HBM)
+
+
 def shards(
     spikes, stimulus, bias, hist_weight, stim_filter, coupling_mix, coupling_target, coupling_weight
 ):
@@ -404,26 +391,27 @@
     slots = unit_count * CAP
     late = time_dev - LAG
     toep = jnp.asarray(toeplitz())
-    toep_spec = whole((2 * LAG, NB * LAG))
+
+    tail = spikes[time_dev - LAG :].astype(BF)
+    halo = lax.ppermute(tail, "tm", [(i, i + 1) for i in range(time_count - 1)])
 
     hbm = pl.BlockSpec(memory_space=pltpu.HBM)
     entry = [coupling_target.T, coupling_mix, spikes, coupling_weight, toep]
-    entry = [pltpu.with_memory_space_constraint(a, pltpu.HBM) for a in entry]
-    x, mixed_late, tail, filt, turned, slot_table, *part_late = call(
+    message = struct((CAP * time_dev + NAME_ROWS, LAG), BF)
+    x, mixed_late, filt, turned, slot_table, *parts = call(
         late_kernel,
         "late",
         5,
         in_specs=[hbm] * len(entry),
-        out_specs=[vmem()] * 5 + [smem()] + [vmem()] * unit_count,
+        out_specs=[vmem()] * 4 + [smem()] + [vmem()] * unit_count,
         out_shape=[
             struct((tiles_dev, TILE, time_dev), BF),
             struct((tiles_dev, TILE, late), BF),
-            struct((tiles_dev, TILE, LAG), BF),
             struct((2 * LAG, 2 * LAG), BF),
             struct((tiles_dev, FAN * TILE, TILE), BF),
             struct((tiles_dev * FAN,), jnp.int32),
         ]
-        + [struct((CAP * TILE + NAME_ROWS, late), BF)] * unit_count,
+        + [message] * unit_count,
         scratch_shapes=[
             SMEM((FAN, tiles_dev), jnp.int32),
             SMEM(coupling_mix.shape, F32),
@@ -435,66 +423,64 @@
             SMEM((unit_count,), jnp.int32),
             pltpu.SemaphoreType.DMA((4 + time_dev // LAG,)),
         ],
-    )(*entry)
-    halo = lax.ppermute(tail, "tm", [(i, i + 1) for i in range(time_count - 1)])
-    got_late = to_units(part_late)
-
-    stimulus_t = stimulus.T
-    logit_shape = struct((tiles_dev, TILE, time_dev), F32)
-    logit, columns = call(
-        logit_kernel,
-        "logit",
-        4,
-        in_specs=[vmem()] * 6,
-        out_shape=[logit_shape, struct((tiles_dev, TILE, TILE), F32)],
-        scratch_shapes=[pltpu.VMEM((TILE, units_dev), F32)],
-    )(x, toep, hist_weight, bias.reshape(1, -1), stim_filter.T, stimulus_t)
+    )(*[far(a) for a in entry])
+    block_whole = whole((tiles_dev, TILE, LAG))
     anywhere = pl.BlockSpec(memory_space=pl.ANY)
-    mixed_early, *part_early, logit = call(
+    mixed_early, *parts = call(
         early_kernel,
         "early",
         2,
-        in_specs=[smem()] + [vmem()] * 4 + [anywhere],
-        out_specs=[vmem()] * (1 + unit_count) + [anywhere],
-        out_shape=[struct((tiles_dev, TILE, LAG), BF)]
-        + [struct((CAP, TILE, LAG), BF)] * unit_count
-        + [logit_shape],
+        grid=(1,),
+        in_specs=[
+            smem(),
+            whole((LAG, units_dev)),
+            block_whole,
+            whole(filt.shape),
+            whole(turned.shape),
+        ]
+        + [anywhere] * unit_count,
+        out_specs=[block_whole] + [whole((CAP * TILE, LAG))] * unit_count,
+        out_shape=[struct((tiles_dev, TILE, LAG), BF)] + [message] * unit_count,
         scratch_shapes=[pltpu.VMEM((slots, TILE, LAG), F32)],
-        input_output_aliases={5: 1 + unit_count},
-    )(slot_table, halo, x, filt, turned, logit)
-    got_early = to_units(part_early)
-    logit_early = call(
-        logit_early_kernel,
-        "logit_early",
-        1,
-        in_specs=[vmem()] * 5,
-        out_shape=struct((tiles_dev, TILE, LAG), F32),
-    )(x, halo, toep, columns, logit)
+        input_output_aliases={5 + k: 1 + k for k in range(unit_count)},
+    )(slot_table, halo, x, filt, turned, *parts)
+    got_parts = to_units(parts)
+    stimulus_t = stimulus.T
+    logit, history = call(
+        logit_kernel,
+        "logit",
+        5,
+        in_specs=[vmem()] * 7,
+        out_shape=[
+            struct((tiles_dev, TILE, time_dev), F32),
+            pltpu.VMEM((tiles_dev, NB, TILE, time_dev), F32),
+        ],
+        scratch_shapes=[pltpu.VMEM((TILE, units_dev), F32)],
+    )(x, halo, toep, hist_weight, bias.reshape(1, -1), stim_filter.T, stimulus_t)
     ids = call(
         names_kernel,
         "names",
         1,
         grid=(1,),
-        in_specs=[whole((NAME_ROWS, LAG), (CAP * TILE // NAME_ROWS, 0))] * unit_count,
+        in_specs=[whole((NAME_ROWS, LAG), (CAP * time_dev // NAME_ROWS, 0))] * unit_count,
         out_specs=smem(),
         out_shape=struct((slots,), jnp.int32),
-    )(*got_late)
-
-    rows = TILE // time_count
+    )(*got_parts)
+
     resids, sends = [], []
     for at, part in enumerate(HALVES):
         resid, *send = call(
             functools.partial(resid_kernel, sum(HALVES[:at])),
             "resid",
             2,
-            in_specs=[smem()] + [vmem()] * (3 + 2 * unit_count),
+            in_specs=[smem()] + [vmem()] * (2 + unit_count),
             out_shape=[struct((tiles_dev, part, time_dev), F32)]
             + [struct((CAP, part, time_dev), BF)] * unit_count,
             scratch_shapes=[
                 pltpu.VMEM((tiles_dev, part, time_dev), F32),
                 pltpu.VMEM((tiles_dev, part, time_dev), BF),
             ],
-        )(ids, logit, logit_early, x, *got_late, *got_early)
+        )(ids, logit, x, *got_parts)
         resids.append(resid)
         sends.append(send)
 
@@ -504,7 +490,7 @@
         own_kernel,
         "own",
         4,
-        in_specs=[vmem()] * 6,
+        in_specs=[vmem()] * 4,
         out_shape=[
             struct((own_rows, wide), F32 if shift == 0 else BF) for shift in range(time_count)
         ],
@@ -513,7 +499,7 @@
             pltpu.VMEM((units_dev, wide), F32),
             pltpu.VMEM((own_rows, wide), F32),
         ],
-    )(x, halo, toep, stimulus_t, *resids)
+    )(history, stimulus_t, *resids)
 
     grads = []
     for send, part in zip(sends, HALVES, strict=True):

time: 101 us -> 99.5 us (0.985)
  Pallas kernels: 26.8 us -> 23.1 us
  waiting for transfers between devices: 29.7 us -> 32.3 us
  starting transfers between devices: 42.8 us -> 41.2 us
  other arithmetic: 0 us -> 1.08 us
    ppermute x28 -> x21, starting transfers between devices: 29.2 us -> 20 us  [to_units(): lax.ppermute(pieces[k], 'unit', [(i, i ^ k) for i in range(len(pieces))])]
    ppermute x28 -> x21, waiting for transfers between devices: 13.5 us -> 21.9 us  [to_units(): lax.ppermute(pieces[k], 'unit', [(i, i ^ k) for i in range(len(pieces))])]
    ppermute x6, starting transfers between devices: 8.71 us -> 16.2 us  [to_peers(): got.append(lax.ppermute(pieces[shift], 'tm', pairs))]
    ppermute x6, waiting for transfers between devices: 16.2 us -> 10.1 us  [to_peers(): got.append(lax.ppermute(pieces[shift], 'tm', pairs))]
    pallas_call x4 -> x3, Pallas kernels: 13.2 us -> 9.8 us  [the longest x1 5.34 us: shards(): call(logit_kernel, 'logit', 5, in_specs=[vmem()] * 7, out_shape=[struct((...]
    another operation x0 -> x1, other arithmetic: none -> 1.08 us
  transfers between devices with their start and end apart: 35 -> 28, of which waited for: 10 -> 6; matrix products, arithmetic and copies ran while one was open for 0% -> 0% of each run, Pallas kernels for 19% -> 19%
where the time goes in v5:
time: 99.5 us; the launch traced here: 98.4 us
  starting transfers between devices  41.2 us (41%)
  waiting for transfers between devices  32.3 us (32%)
  Pallas kernels  23.1 us (23%)
  other arithmetic  1.08 us (1%)
    ppermute x21, waiting for transfers between devices, to_units(): lax.ppermute(pieces[k], 'unit', [(i, i ^ k) for i in range(len(pieces))])  21.9 us
    ppermute x21, starting transfers between devices, to_units(): lax.ppermute(pieces[k], 'unit', [(i, i ^ k) for i in range(len(pieces))])  20 us
    ppermute x6, starting transfers between devices, to_peers(): got.append(lax.ppermute(pieces[shift], 'tm', pairs))  16.2 us
    ppermute x6, waiting for transfers between devices, to_peers(): got.append(lax.ppermute(pieces[shift], 'tm', pairs))  10.1 us
    pallas_call x1, Pallas kernels, shards(): call(logit_kernel, 'logit', 5, in_specs=[vmem()] * 7, out_shape=[struct((...  5.34 us
    pallas_call x1, Pallas kernels, shards(): call(late_kernel, 'late', 5, in_specs=[hbm] * len(entry), out_specs=[vmem...  5.22 us
    ppermute x1, starting transfers between devices, shards(): halo = lax.ppermute(tail, 'tm', [(i, i + 1) for i in range(time_count - 1)])  4.94 us
    pallas_call x2, Pallas kernels, shards(): call(functools.partial(grad_kernel, unit_count, len(extras)), 'grad', 2,...  3 us
  transfers between devices with their start and end apart: 28, of which 6 were waited for; matrix products, arithmetic and copies ran while one was open for 0% of the time, Pallas kernels for 19%

profile of v5, /device:TPU:0, one launch (start us, length us, event | category | flops | bytes accessed | tf_op | source)
XLA Modules:
  0.0 98.4 jit_solution(18336918750632872352)
XLA Ops:
  1.7 4.9 %collective-permute-start = (bf16[128,1024]{1,0:T(8,128)(2,1)S(1)}, bf16[128,1024]{1,0:T(8,128)(2,1)S(1)}, u32[]{:S(2)}, u32[]{:S(2)}) collective-permute-start(bf16[128,1024]{1,0:T(8,128)(2,1)S(1)} %slice_convert_fusion), channel_id=1, source_target_pairs={{0,1},{1,2},{2,3},{4,5},{5,6},{6,7},{8,9},{9,10},{10,11},{12,13},{... | collective-permute-start | bytes 786440 | tf_op jit(solution)/shard_map/ppermute | solution.py:396
  6.7 5.2 %late.1 = (bf16[8,128,512]{2,1,0:T(8,128)(2,1)S(1)}, bf16[8,128,384]{2,1,0:T(8,128)(2,1)S(1)}, bf16[256,256]{1,0:T(8,128)(2,1)S(1)}, bf16[8,512,128]{2,1,0:T(8,1...) custom-call(s32[4,8]{1,0:T(4,128)} %bitcast.10, ...), custom_call_target="tpu_custom_call" | custom-call | flops 50000000 | bytes 1048576 | tf_op jit(solution)/shard_map/late/pallas_call | solution.py:401
  12.2 1.5 %early.1 = (bf16[8,128,128]{2,1,0:T(8,128)(2,1)S(1)}, bf16[1040,128]{1,0:T(8,128)(2,1)S(1)}, bf16[1040,128]{1,0:T(8,128)(2,1)S(1)}, bf16[1040,128]{1,0:T(8,128)(...) custom-call(s32[32]{0:T(128)S(1)} %get-tuple-element.63.slots, ...), custom_call_target="tpu_custom_call", output_to_operand_aliasing={{1}: (5, {}), {2}: (6, {}), {3}: (7, {}), {4}: (8, {}), {5}... | custom-call | flops 20000000 | bytes 1048576 | tf_op jit(solution)/shard_map/early/pallas_call | solution.py:429
  13.8 1.6 %collective-permute-start.2 = (bf16[1040,128]{1,0:T(8,128)(2,1)S(1)}, bf16[1040,128]{1,0:T(8,128)(2,1)S(1)}, u32[]{:S(2)}, u32[]{:S(2)}) collective-permute-start(bf16[1040,128]{1,0:T(8,128)(2,1)S(1)} %get-tuple-element.76), channel_id=1, source_target_pairs={{0,8},{4,12},{8,0},{12,4},{16,24},{20,28},{24,16},{28,20},{1,9},{5... | collective-permute-start | bytes 798728 | tf_op jit(solution)/shard_map/ppermute | solution.py:345
  15.6 1.5 %collective-permute-start.4 = (bf16[1040,128]{1,0:T(8,128)(2,1)S(1)}, bf16[1040,128]{1,0:T(8,128)(2,1)S(1)}, u32[]{:S(2)}, u32[]{:S(2)}) collective-permute-start(bf16[1040,128]{1,0:T(8,128)(2,1)S(1)} %get-tuple-element.78), channel_id=1, source_target_pairs={{0,16},{4,20},{8,24},{12,28},{16,0},{20,4},{24,8},{28,12},{1,17},{... | collective-permute-start | bytes 798728 | tf_op jit(solution)/shard_map/ppermute | solution.py:345
  17.3 2.5 %collective-permute-start.6 = (bf16[1040,128]{1,0:T(8,128)(2,1)S(1)}, bf16[1040,128]{1,0:T(8,128)(2,1)S(1)}, u32[]{:S(2)}, u32[]{:S(2)}) collective-permute-start(bf16[1040,128]{1,0:T(8,128)(2,1)S(1)} %get-tuple-element.80), channel_id=1, source_target_pairs={{0,24},{4,28},{8,16},{12,20},{16,8},{20,12},{24,0},{28,4},{1,25},{... | collective-permute-start | bytes 798728 | tf_op jit(solution)/shard_map/ppermute | solution.py:345
  19.8 3.2 %collective-permute-done.2.refs_2_ = bf16[1040,128]{1,0:T(8,128)(2,1)S(1)} collective-permute-done((bf16[1040,128]{1,0:T(8,128)(2,1)S(1)}, bf16[1040,128]{1,0:T(8,128)(2,1)S(1)}, u32[]{:S(2)}, u32[]{:S(2)}) %collective-permute-start.2) | collective-permute-done | bytes 266272 | tf_op jit(solution)/shard_map/ppermute | solution.py:345
  24.3 5.3 %logit.1 = (f32[8,128,512]{2,1,0:T(8,128)S(1)}, f32[8,10,128,512]{3,2,1,0:T(8,128)S(1)}) custom-call(bf16[8,128,512]{2,1,0:T(8,128)(2,1)S(1)} %get-tuple-element.61.x, bf16[128,1024]{1,0:T(8,128)(2,1)S(1)} %collective-permute-done.halo, bf16[256,1280]{1,0:T(8,128)(2,1)S(1)} %copy-done, f32[10,1024]{1,0:T(8,128)S(1)} %copy-done.3, f32[1,1024]{1,0:T(1,128)S(1)} %bitcast.9, ...), custom_call_target="tpu_custom_call" | custom-call | flops 50000000 | bytes 1048576 | tf_op jit(solution)/shard_map/logit/pallas_call | solution.py:449
  29.7 11.1 %collective-permute-done.5.refs_5_ = bf16[1040,128]{1,0:T(8,128)(2,1)S(1)} collective-permute-done((bf16[1040,128]{1,0:T(8,128)(2,1)S(1)}, bf16[1040,128]{1,0:T(8,128)(2,1)S(1)}, u32[]{:S(2)}, u32[]{:S(2)}) %collective-permute-start.5) | collective-permute-done | bytes 266272 | tf_op jit(solution)/shard_map/ppermute | solution.py:345
  42.9 1.6 %collective-permute-start.10 = (bf16[2,64,512]{2,1,0:T(8,128)(2,1)S(1)}, bf16[2,64,512]{2,1,0:T(8,128)(2,1)S(1)}, u32[]{:S(2)}, u32[]{:S(2)}) collective-permute-start(bf16[2,64,512]{2,1,0:T(8,128)(2,1)S(1)} %get-tuple-element.91), channel_id=1, source_target_pairs={{0,12},{4,8},{8,4},{12,0},{16,28},{20,24},{24,20},{28,16},{1,13},{... | collective-permute-start | bytes 393224 | tf_op jit(solution)/shard_map/ppermute | solution.py:345
  47.3 1.5 %collective-permute-start.14 = (bf16[2,64,512]{2,1,0:T(8,128)(2,1)S(1)}, bf16[2,64,512]{2,1,0:T(8,128)(2,1)S(1)}, u32[]{:S(2)}, u32[]{:S(2)}) collective-permute-start(bf16[2,64,512]{2,1,0:T(8,128)(2,1)S(1)} %get-tuple-element.95), channel_id=1, source_target_pairs={{0,28},{4,24},{8,20},{12,16},{16,12},{20,8},{24,4},{28,0},{1,29},{... | collective-permute-start | bytes 393224 | tf_op jit(solution)/shard_map/ppermute | solution.py:345
  48.9 7.5 %collective-permute-done.11.refs_4_ = bf16[2,64,512]{2,1,0:T(8,128)(2,1)S(1)} collective-permute-done((bf16[2,64,512]{2,1,0:T(8,128)(2,1)S(1)}, bf16[2,64,512]{2,1,0:T(8,128)(2,1)S(1)}, u32[]{:S(2)}, u32[]{:S(2)}) %collective-permute-start.11) | collective-permute-done | bytes 131104 | tf_op jit(solution)/shard_map/ppermute | solution.py:345
  58.1 1.6 %collective-permute-start.19 = (bf16[2,64,512]{2,1,0:T(8,128)(2,1)S(1)}, bf16[2,64,512]{2,1,0:T(8,128)(2,1)S(1)}, u32[]{:S(2)}, u32[]{:S(2)}) collective-permute-start(bf16[2,64,512]{2,1,0:T(8,128)(2,1)S(1)} %get-tuple-element.108), channel_id=1, source_target_pairs={{0,8},{4,12},{8,0},{12,4},{16,24},{20,28},{24,16},{28,20},{1,9},{5... | collective-permute-start | bytes 393224 | tf_op jit(solution)/shard_map/ppermute | solution.py:345
  59.9 3.0 %own.1 = (f32[256,128]{1,0:T(8,128)S(1)}, bf16[256,128]{1,0:T(8,128)(2,1)S(1)}, bf16[256,128]{1,0:T(8,128)(2,1)S(1)}, bf16[256,128]{1,0:T(8,128)(2,1)S(1)}) custom-call(f32[8,10,128,512]{3,2,1,0:T(8,128)S(1)} %get-tuple-element.62.history, bf16[64,512]{1,0:T(8,128)(2,1)S(1)} %bitcast.7, f32[8,64,512]{2,1,0:T(8,128)S(1)} %get-tuple-element.83.resid_a, ...), custom_call_target="tpu_custom_call" | custom-call | flops 40000000 | bytes 1048576 | tf_op jit(solution)/shard_map/own/pallas_call | solution.py:489
  62.9 1.8 %collective-permute-start.21 = (bf16[2,64,512]{2,1,0:T(8,128)(2,1)S(1)}, bf16[2,64,512]{2,1,0:T(8,128)(2,1)S(1)}, u32[]{:S(2)}, u32[]{:S(2)}) collective-permute-start(bf16[2,64,512]{2,1,0:T(8,128)(2,1)S(1)} %get-tuple-element.110), channel_id=1, source_target_pairs={{0,16},{4,20},{8,24},{12,28},{16,0},{20,4},{24,8},{28,12},{1,17},{... | collective-permute-start | bytes 393224 | tf_op jit(solution)/shard_map/ppermute | solution.py:345
  64.7 1.5 %grad.2 = (bf16[256,256]{1,0:T(8,128)(2,1)S(1)}, bf16[256,384]{1,0:T(8,128)(2,1)S(1)}, bf16[256,384]{1,0:T(8,128)(2,1)S(1)}, bf16[256,384]{1,0:T(8,128)(2,1)S(1)}) custom-call(s32[32]{0:T(128)S(1)} %get-tuple-element.63.slots, bf16[8,128,128]{2,1,0:T(8,128)(2,1)S(1)} %get-tuple-element.86.mixed_early, bf16[8,128,384]{2,1,0:T(8,128)(2,1)S(1)} %get-tuple-element.87.mixed_late, ...), custom_call_target="tpu_custom_call" | custom-call | flops 20000000 | bytes 1048576 | tf_op jit(solution)/shard_map/grad/pallas_call | solution.py:509
  66.3 2.5 %collective-permute-start.15 = (bf16[256,384]{1,0:T(8,128)(2,1)S(1)}, bf16[256,384]{1,0:T(8,128)(2,1)S(1)}, u32[]{:S(2)}, u32[]{:S(2)}) collective-permute-start(bf16[256,384]{1,0:T(8,128)(2,1)S(1)} %get-tuple-element.99), channel_id=1, source_target_pairs={{0,1},{1,2},{2,3},{3,0},{4,5},{5,6},{6,7},{7,4},{8,9},{9,10},{10,1... | collective-permute-start | bytes 589832 | tf_op jit(solution)/shard_map/ppermute | solution.py:338
  68.8 2.5 %collective-permute-start.23 = (bf16[2,64,512]{2,1,0:T(8,128)(2,1)S(1)}, bf16[2,64,512]{2,1,0:T(8,128)(2,1)S(1)}, u32[]{:S(2)}, u32[]{:S(2)}) collective-permute-start(bf16[2,64,512]{2,1,0:T(8,128)(2,1)S(1)} %get-tuple-element.112), channel_id=1, source_target_pairs={{0,24},{4,28},{8,16},{12,20},{16,8},{20,12},{24,0},{28,4},{1,25},{... | collective-permute-start | bytes 393224 | tf_op jit(solution)/shard_map/ppermute | solution.py:345
  71.4 2.6 %collective-permute-start.16 = (bf16[256,384]{1,0:T(8,128)(2,1)S(1)}, bf16[256,384]{1,0:T(8,128)(2,1)S(1)}, u32[]{:S(2)}, u32[]{:S(2)}) collective-permute-start(bf16[256,384]{1,0:T(8,128)(2,1)S(1)} %get-tuple-element.100), channel_id=1, source_target_pairs={{0,2},{1,3},{2,0},{3,1},{4,6},{5,7},{6,4},{7,5},{8,10},{9,11},{10,... | collective-permute-start | bytes 589832 | tf_op jit(solution)/shard_map/ppermute | solution.py:338
  74.0 7.1 %collective-permute-start.17 = (bf16[256,384]{1,0:T(8,128)(2,1)S(1)}, bf16[256,384]{1,0:T(8,128)(2,1)S(1)}, u32[]{:S(2)}, u32[]{:S(2)}) collective-permute-start(bf16[256,384]{1,0:T(8,128)(2,1)S(1)} %get-tuple-element.101), channel_id=1, source_target_pairs={{0,3},{1,0},{2,1},{3,2},{4,7},{5,4},{6,5},{7,6},{8,11},{9,8},{10,9... | collective-permute-start | bytes 589832 | tf_op jit(solution)/shard_map/ppermute | solution.py:338
  81.1 1.5 %grad.3 = (bf16[256,256]{1,0:T(8,128)(2,1)S(1)}, bf16[256,256]{1,0:T(8,128)(2,1)S(1)}, bf16[256,256]{1,0:T(8,128)(2,1)S(1)}, bf16[256,256]{1,0:T(8,128)(2,1)S(1)}) custom-call(s32[32]{0:T(128)S(1)} %get-tuple-element.63.slots, bf16[8,128,128]{2,1,0:T(8,128)(2,1)S(1)} %get-tuple-element.86.mixed_early, bf16[8,128,384]{2,1,0:T(8,128)(2,1)S(1)} %get-tuple-element.87.mixed_late, ...), custom_call_target="tpu_custom_call" | custom-call | flops 20000000 | bytes 1048576 | tf_op jit(solution)/shard_map/grad/pallas_call | solution.py:509
  83.3 3.2 %collective-permute-start.27 = (bf16[256,256]{1,0:T(8,128)(2,1)S(1)}, bf16[256,256]{1,0:T(8,128)(2,1)S(1)}, u32[]{:S(2)}, u32[]{:S(2)}) collective-permute-start(bf16[256,256]{1,0:T(8,128)(2,1)S(1)} %get-tuple-element.117), channel_id=1, source_target_pairs={{0,3},{1,0},{2,1},{3,2},{4,7},{5,4},{6,5},{7,6},{8,11},{9,8},{10,9... | collective-permute-start | bytes 393224 | tf_op jit(solution)/shard_map/ppermute | solution.py:338
  87.3 3.7 %collective-permute-done.25.refs_5_ = bf16[256,256]{1,0:T(8,128)(2,1)S(1)} collective-permute-done((bf16[256,256]{1,0:T(8,128)(2,1)S(1)}, bf16[256,256]{1,0:T(8,128)(2,1)S(1)}, u32[]{:S(2)}, u32[]{:S(2)}) %collective-permute-start.25) | collective-permute-done | bytes 131104 | tf_op jit(solution)/shard_map/ppermute | solution.py:338
  91.0 6.4 %collective-permute-done.26.refs_6_ = bf16[256,256]{1,0:T(8,128)(2,1)S(1)} collective-permute-done((bf16[256,256]{1,0:T(8,128)(2,1)S(1)}, bf16[256,256]{1,0:T(8,128)(2,1)S(1)}, u32[]{:S(2)}, u32[]{:S(2)}) %collective-permute-start.26) | collective-permute-done | bytes 131104 | tf_op jit(solution)/shard_map/ppermute | solution.py:338
  (54 shorter events, 12.6 us)
Async XLA Ops:
  1.7 10.5 %collective-permute-start = (bf16[128,1024]{1,0:T(8,128)(2,1)S(1)}, bf16[128,1024]{1,0:T(8,128)(2,1)S(1)}, u32[]{:S(2)}, u32[]{:S(2)}) collective-permute-start(bf16[128,1024]{1,0:T(8,128)(2,1)S(1)} %slice_convert_fusion), channel_id=1, source_target_pairs={{0,1},{1,2},{2,3},{4,5},{5,6},{6,7},{8,9},{9,10},{10,11},{12,13},{... | collective-permute-start | bytes 786440 | tf_op jit(solution)/shard_map/ppermute | solution.py:396
  13.8 9.3 %collective-permute-start.2 = (bf16[1040,128]{1,0:T(8,128)(2,1)S(1)}, bf16[1040,128]{1,0:T(8,128)(2,1)S(1)}, u32[]{:S(2)}, u32[]{:S(2)}) collective-permute-start(bf16[1040,128]{1,0:T(8,128)(2,1)S(1)} %get-tuple-element.76), channel_id=1, source_target_pairs={{0,8},{4,12},{8,0},{12,4},{16,24},{20,28},{24,16},{28,20},{1,9},{5... | collective-permute-start | bytes 798728 | tf_op jit(solution)/shard_map/ppermute | solution.py:345
  15.3 14.3 %collective-permute-start.3 = (bf16[1040,128]{1,0:T(8,128)(2,1)S(1)}, bf16[1040,128]{1,0:T(8,128)(2,1)S(1)}, u32[]{:S(2)}, u32[]{:S(2)}) collective-permute-start(bf16[1040,128]{1,0:T(8,128)(2,1)S(1)} %get-tuple-element.77), channel_id=1, source_target_pairs={{0,12},{4,8},{8,4},{12,0},{16,28},{20,24},{24,20},{28,16},{1,13},{... | collective-permute-start | bytes 798728 | tf_op jit(solution)/shard_map/ppermute | solution.py:345
  15.6 14.1 %collective-permute-start.4 = (bf16[1040,128]{1,0:T(8,128)(2,1)S(1)}, bf16[1040,128]{1,0:T(8,128)(2,1)S(1)}, u32[]{:S(2)}, u32[]{:S(2)}) collective-permute-start(bf16[1040,128]{1,0:T(8,128)(2,1)S(1)} %get-tuple-element.78), channel_id=1, source_target_pairs={{0,16},{4,20},{8,24},{12,28},{16,0},{20,4},{24,8},{28,12},{1,17},{... | collective-permute-start | bytes 798728 | tf_op jit(solution)/shard_map/ppermute | solution.py:345
  17.2 23.7 %collective-permute-start.5 = (bf16[1040,128]{1,0:T(8,128)(2,1)S(1)}, bf16[1040,128]{1,0:T(8,128)(2,1)S(1)}, u32[]{:S(2)}, u32[]{:S(2)}) collective-permute-start(bf16[1040,128]{1,0:T(8,128)(2,1)S(1)} %get-tuple-element.79), channel_id=1, source_target_pairs={{0,20},{4,16},{8,28},{12,24},{16,4},{20,0},{24,12},{28,8},{1,21},{... | collective-permute-start | bytes 798728 | tf_op jit(solution)/shard_map/ppermute | solution.py:345
  17.3 23.5 %collective-permute-start.6 = (bf16[1040,128]{1,0:T(8,128)(2,1)S(1)}, bf16[1040,128]{1,0:T(8,128)(2,1)S(1)}, u32[]{:S(2)}, u32[]{:S(2)}) collective-permute-start(bf16[1040,128]{1,0:T(8,128)(2,1)S(1)} %get-tuple-element.80), channel_id=1, source_target_pairs={{0,24},{4,28},{8,16},{12,20},{16,8},{20,12},{24,0},{28,4},{1,25},{... | collective-permute-start | bytes 798728 | tf_op jit(solution)/shard_map/ppermute | solution.py:345
  23.0 17.8 %collective-permute-start.7 = (bf16[1040,128]{1,0:T(8,128)(2,1)S(1)}, bf16[1040,128]{1,0:T(8,128)(2,1)S(1)}, u32[]{:S(2)}, u32[]{:S(2)}) collective-permute-start(bf16[1040,128]{1,0:T(8,128)(2,1)S(1)} %get-tuple-element.81), channel_id=1, source_target_pairs={{0,28},{4,24},{8,20},{12,16},{16,12},{20,8},{24,4},{28,0},{1,29},{... | collective-permute-start | bytes 798728 | tf_op jit(solution)/shard_map/ppermute | solution.py:345
  44.4 12.0 %collective-permute-start.11 = (bf16[2,64,512]{2,1,0:T(8,128)(2,1)S(1)}, bf16[2,64,512]{2,1,0:T(8,128)(2,1)S(1)}, u32[]{:S(2)}, u32[]{:S(2)}) collective-permute-start(bf16[2,64,512]{2,1,0:T(8,128)(2,1)S(1)} %get-tuple-element.92), channel_id=1, source_target_pairs={{0,16},{4,20},{8,24},{12,28},{16,0},{20,4},{24,8},{28,12},{1,17},{... | collective-permute-start | bytes 393224 | tf_op jit(solution)/shard_map/ppermute | solution.py:345
  45.9 12.0 %collective-permute-start.12 = (bf16[2,64,512]{2,1,0:T(8,128)(2,1)S(1)}, bf16[2,64,512]{2,1,0:T(8,128)(2,1)S(1)}, u32[]{:S(2)}, u32[]{:S(2)}) collective-permute-start(bf16[2,64,512]{2,1,0:T(8,128)(2,1)S(1)} %get-tuple-element.93), channel_id=1, source_target_pairs={{0,20},{4,16},{8,28},{12,24},{16,4},{20,0},{24,12},{28,8},{1,21},{... | collective-permute-start | bytes 393224 | tf_op jit(solution)/shard_map/ppermute | solution.py:345
  45.9 12.2 %collective-permute-start.13 = (bf16[2,64,512]{2,1,0:T(8,128)(2,1)S(1)}, bf16[2,64,512]{2,1,0:T(8,128)(2,1)S(1)}, u32[]{:S(2)}, u32[]{:S(2)}) collective-permute-start(bf16[2,64,512]{2,1,0:T(8,128)(2,1)S(1)} %get-tuple-element.94), channel_id=1, source_target_pairs={{0,24},{4,28},{8,16},{12,20},{16,8},{20,12},{24,0},{28,4},{1,25},{... | collective-permute-start | bytes 393224 | tf_op jit(solution)/shard_map/ppermute | solution.py:345
  47.3 12.4 %collective-permute-start.14 = (bf16[2,64,512]{2,1,0:T(8,128)(2,1)S(1)}, bf16[2,64,512]{2,1,0:T(8,128)(2,1)S(1)}, u32[]{:S(2)}, u32[]{:S(2)}) collective-permute-start(bf16[2,64,512]{2,1,0:T(8,128)(2,1)S(1)} %get-tuple-element.95), channel_id=1, source_target_pairs={{0,28},{4,24},{8,20},{12,16},{16,12},{20,8},{24,4},{28,0},{1,29},{... | collective-permute-start | bytes 393224 | tf_op jit(solution)/shard_map/ppermute | solution.py:345
  48.8 14.0 %collective-permute-start.8 = (bf16[2,64,512]{2,1,0:T(8,128)(2,1)S(1)}, bf16[2,64,512]{2,1,0:T(8,128)(2,1)S(1)}, u32[]{:S(2)}, u32[]{:S(2)}) collective-permute-start(bf16[2,64,512]{2,1,0:T(8,128)(2,1)S(1)} %get-tuple-element.89), channel_id=1, source_target_pairs={{0,4},{4,0},{8,12},{12,8},{16,20},{20,16},{24,28},{28,24},{1,5},{5... | collective-permute-start | bytes 393224 | tf_op jit(solution)/shard_map/ppermute | solution.py:345
  57.9 8.3 %collective-permute-start.18 = (bf16[2,64,512]{2,1,0:T(8,128)(2,1)S(1)}, bf16[2,64,512]{2,1,0:T(8,128)(2,1)S(1)}, u32[]{:S(2)}, u32[]{:S(2)}) collective-permute-start(bf16[2,64,512]{2,1,0:T(8,128)(2,1)S(1)} %get-tuple-element.107), channel_id=1, source_target_pairs={{0,4},{4,0},{8,12},{12,8},{16,20},{20,16},{24,28},{28,24},{1,5},{5... | collective-permute-start | bytes 393224 | tf_op jit(solution)/shard_map/ppermute | solution.py:345
  58.1 10.8 %collective-permute-start.19 = (bf16[2,64,512]{2,1,0:T(8,128)(2,1)S(1)}, bf16[2,64,512]{2,1,0:T(8,128)(2,1)S(1)}, u32[]{:S(2)}, u32[]{:S(2)}) collective-permute-start(bf16[2,64,512]{2,1,0:T(8,128)(2,1)S(1)} %get-tuple-element.108), channel_id=1, source_target_pairs={{0,8},{4,12},{8,0},{12,4},{16,24},{20,28},{24,16},{28,20},{1,9},{5... | collective-permute-start | bytes 393224 | tf_op jit(solution)/shard_map/ppermute | solution.py:345
  59.7 11.6 %collective-permute-start.20 = (bf16[2,64,512]{2,1,0:T(8,128)(2,1)S(1)}, bf16[2,64,512]{2,1,0:T(8,128)(2,1)S(1)}, u32[]{:S(2)}, u32[]{:S(2)}) collective-permute-start(bf16[2,64,512]{2,1,0:T(8,128)(2,1)S(1)} %get-tuple-element.109), channel_id=1, source_target_pairs={{0,12},{4,8},{8,4},{12,0},{16,28},{20,24},{24,20},{28,16},{1,13},{... | collective-permute-start | bytes 393224 | tf_op jit(solution)/shard_map/ppermute | solution.py:345
  62.9 8.5 %collective-permute-start.21 = (bf16[2,64,512]{2,1,0:T(8,128)(2,1)S(1)}, bf16[2,64,512]{2,1,0:T(8,128)(2,1)S(1)}, u32[]{:S(2)}, u32[]{:S(2)}) collective-permute-start(bf16[2,64,512]{2,1,0:T(8,128)(2,1)S(1)} %get-tuple-element.110), channel_id=1, source_target_pairs={{0,16},{4,20},{8,24},{12,28},{16,0},{20,4},{24,8},{28,12},{1,17},{... | collective-permute-start | bytes 393224 | tf_op jit(solution)/shard_map/ppermute | solution.py:345
  64.7 9.3 %collective-permute-start.22 = (bf16[2,64,512]{2,1,0:T(8,128)(2,1)S(1)}, bf16[2,64,512]{2,1,0:T(8,128)(2,1)S(1)}, u32[]{:S(2)}, u32[]{:S(2)}) collective-permute-start(bf16[2,64,512]{2,1,0:T(8,128)(2,1)S(1)} %get-tuple-element.111), channel_id=1, source_target_pairs={{0,20},{4,16},{8,28},{12,24},{16,4},{20,0},{24,12},{28,8},{1,21},{... | collective-permute-start | bytes 393224 | tf_op jit(solution)/shard_map/ppermute | solution.py:345
  66.3 17.0 %collective-permute-start.15 = (bf16[256,384]{1,0:T(8,128)(2,1)S(1)}, bf16[256,384]{1,0:T(8,128)(2,1)S(1)}, u32[]{:S(2)}, u32[]{:S(2)}) collective-permute-start(bf16[256,384]{1,0:T(8,128)(2,1)S(1)} %get-tuple-element.99), channel_id=1, source_target_pairs={{0,1},{1,2},{2,3},{3,0},{4,5},{5,6},{6,7},{7,4},{8,9},{9,10},{10,1... | collective-permute-start | bytes 589832 | tf_op jit(solution)/shard_map/ppermute | solution.py:338
  68.8 12.3 %collective-permute-start.23 = (bf16[2,64,512]{2,1,0:T(8,128)(2,1)S(1)}, bf16[2,64,512]{2,1,0:T(8,128)(2,1)S(1)}, u32[]{:S(2)}, u32[]{:S(2)}) collective-permute-start(bf16[2,64,512]{2,1,0:T(8,128)(2,1)S(1)} %get-tuple-element.112), channel_id=1, source_target_pairs={{0,24},{4,28},{8,16},{12,20},{16,8},{20,12},{24,0},{28,4},{1,25},{... | collective-permute-start | bytes 393224 | tf_op jit(solution)/shard_map/ppermute | solution.py:345
  71.4 9.8 %collective-permute-start.24 = (bf16[2,64,512]{2,1,0:T(8,128)(2,1)S(1)}, bf16[2,64,512]{2,1,0:T(8,128)(2,1)S(1)}, u32[]{:S(2)}, u32[]{:S(2)}) collective-permute-start(bf16[2,64,512]{2,1,0:T(8,128)(2,1)S(1)} %get-tuple-element.113), channel_id=1, source_target_pairs={{0,28},{4,24},{8,20},{12,16},{16,12},{20,8},{24,4},{28,0},{1,29},{... | collective-permute-start | bytes 393224 | tf_op jit(solution)/shard_map/ppermute | solution.py:345
  71.4 15.2 %collective-permute-start.16 = (bf16[256,384]{1,0:T(8,128)(2,1)S(1)}, bf16[256,384]{1,0:T(8,128)(2,1)S(1)}, u32[]{:S(2)}, u32[]{:S(2)}) collective-permute-start(bf16[256,384]{1,0:T(8,128)(2,1)S(1)} %get-tuple-element.100), channel_id=1, source_target_pairs={{0,2},{1,3},{2,0},{3,1},{4,6},{5,7},{6,4},{7,5},{8,10},{9,11},{10,... | collective-permute-start | bytes 589832 | tf_op jit(solution)/shard_map/ppermute | solution.py:338
  74.0 12.5 %collective-permute-start.17 = (bf16[256,384]{1,0:T(8,128)(2,1)S(1)}, bf16[256,384]{1,0:T(8,128)(2,1)S(1)}, u32[]{:S(2)}, u32[]{:S(2)}) collective-permute-start(bf16[256,384]{1,0:T(8,128)(2,1)S(1)} %get-tuple-element.101), channel_id=1, source_target_pairs={{0,3},{1,0},{2,1},{3,2},{4,7},{5,4},{6,5},{7,6},{8,11},{9,8},{10,9... | collective-permute-start | bytes 589832 | tf_op jit(solution)/shard_map/ppermute | solution.py:338
  82.7 14.6 %collective-permute-start.26 = (bf16[256,256]{1,0:T(8,128)(2,1)S(1)}, bf16[256,256]{1,0:T(8,128)(2,1)S(1)}, u32[]{:S(2)}, u32[]{:S(2)}) collective-permute-start(bf16[256,256]{1,0:T(8,128)(2,1)S(1)} %get-tuple-element.116), channel_id=1, source_target_pairs={{0,2},{1,3},{2,0},{3,1},{4,6},{5,7},{6,4},{7,5},{8,10},{9,11},{10,... | collective-permute-start | bytes 393224 | tf_op jit(solution)/shard_map/ppermute | solution.py:338
  83.3 14.1 %collective-permute-start.27 = (bf16[256,256]{1,0:T(8,128)(2,1)S(1)}, bf16[256,256]{1,0:T(8,128)(2,1)S(1)}, u32[]{:S(2)}, u32[]{:S(2)}) collective-permute-start(bf16[256,256]{1,0:T(8,128)(2,1)S(1)} %get-tuple-element.117), channel_id=1, source_target_pairs={{0,3},{1,0},{2,1},{3,2},{4,7},{5,4},{6,5},{7,6},{8,11},{9,8},{10,9... | collective-permute-start | bytes 393224 | tf_op jit(solution)/shard_map/ppermute | solution.py:338
  (9 other events, 86.9 us)

commit v6 on v5

--- a/solution.py
+++ b/solution.py
@@ -155,14 +155,6 @@
         for q in range(CAP):
             block = total[jnp.bitwise_xor(me, k) * CAP + q]
             out[q * TILE : (q + 1) * TILE] = block.astype(BF)
-
-
-def names_kernel(*refs):
-    got, ids = refs[:-1], refs[-1]
-    for k, part in enumerate(got):
-        block = part[...].astype(F32)
-        for q in range(CAP):
-            ids[k * CAP + q] = jnp.max(block[q : q + 1]).astype(jnp.int32)
 
 
 def windows(extended, count):
@@ -198,46 +190,52 @@
     lax.fori_loop(0, x.shape[0], one, 0)
 
 
-def resid_kernel(first, ids, logit, x, *refs):
-    count = ids.shape[0] // CAP
-    got, (resid, *sends), (total, rounded) = refs[:count], refs[count:-2], refs[-2:]
-    part = resid.shape[1]
-    mine = slice(first, first + part)
-    total[...] = logit[:, mine]
+def resid_kernel(parts, logit, x, *refs):
+    total, rounded, ids = refs[-3:]
+    refs = refs[:-3]
+    count = (len(refs) - 1) // (1 + len(parts))
+    got, resid, sends = refs[:count], refs[count], refs[count + 1 :]
+    blocks = x.shape[2] // LAG
+    for j in range(count):
+        names = got[j][blocks * CAP * TILE :].astype(F32)
+        for q in range(CAP):
+            ids[j * CAP + q] = jnp.max(names[q : q + 1]).astype(jnp.int32)
+    total[...] = logit[...]
     for j in range(count):
         for q in range(CAP):
             tile = ids[j * CAP + q]
 
             @pl.when(tile >= 0)
             def _():
-                for k in range(x.shape[2] // LAG):
-                    start = (k * CAP + q) * TILE + first
-                    total[tile, :, k * LAG : (k + 1) * LAG] += got[j][start : start + part].astype(
-                        F32
-                    )
+                for k in range(blocks):
+                    at = (k * CAP + q) * TILE
+                    total[tile, :, k * LAG : (k + 1) * LAG] += got[j][at : at + TILE].astype(F32)
 
     for j in range(logit.shape[0]):
-        r = x[j, mine].astype(F32) - jnp.exp(total[j])
+        r = x[j].astype(F32) - jnp.exp(total[j])
         resid[j] = r
         rounded[j] = r.astype(BF)
-    for k in range(count):
-        for q in range(CAP):
-            tile = ids[k * CAP + q]
-
-            @pl.when(tile >= 0)
-            def _():
-                sends[k][q] = rounded[tile]
-
-            @pl.when(tile < 0)
-            def _():
-                sends[k][q] = jnp.zeros(sends[k].shape[1:], BF)
+    for half, part in enumerate(parts):
+        first = sum(parts[:half])
+        for k in range(count):
+            send = sends[half * count + k]
+            for q in range(CAP):
+                tile = ids[k * CAP + q]
+
+                @pl.when(tile >= 0)
+                def _():
+                    send[q] = rounded[tile, first : first + part]
+
+                @pl.when(tile < 0)
+                def _():
+                    send[q] = jnp.zeros(send.shape[1:], BF)
 
 
 def peer(shift, count):
     return lax.rem(lax.axis_index("tm") + shift, count)
 
 
-def own_kernel(history, stimulus, resid_a, resid_b, *refs):
+def own_kernel(history, stimulus, residuals, *refs):
     outs, (wide, stim, sums) = refs[:-3], refs[-3:]
     channels = stimulus.shape[0]
     rows = sums.shape[0]
@@ -253,7 +251,7 @@
         return jnp.sum(total, axis=1, keepdims=True)
 
     def one(s, _):
-        resid = jnp.concatenate([resid_a[s], resid_b[s]], axis=0)
+        resid = residuals[s]
         units = pl.ds(pl.multiple_of(s * TILE, TILE), TILE)
         stim[units] = contract(resid.astype(BF), wide[...], (1, 1))
         columns = [folded(resid * history[s, b]) for b in range(NB)]
@@ -457,32 +455,20 @@
         ],
         scratch_shapes=[pltpu.VMEM((TILE, units_dev), F32)],
     )(x, halo, toep, hist_weight, bias.reshape(1, -1), stim_filter.T, stimulus_t)
-    ids = call(
-        names_kernel,
-        "names",
-        1,
-        grid=(1,),
-        in_specs=[whole((NAME_ROWS, LAG), (CAP * time_dev // NAME_ROWS, 0))] * unit_count,
-        out_specs=smem(),
-        out_shape=struct((slots,), jnp.int32),
-    )(*got_parts)
-
-    resids, sends = [], []
-    for at, part in enumerate(HALVES):
-        resid, *send = call(
-            functools.partial(resid_kernel, sum(HALVES[:at])),
-            "resid",
-            2,
-            in_specs=[smem()] + [vmem()] * (2 + unit_count),
-            out_shape=[struct((tiles_dev, part, time_dev), F32)]
-            + [struct((CAP, part, time_dev), BF)] * unit_count,
-            scratch_shapes=[
-                pltpu.VMEM((tiles_dev, part, time_dev), F32),
-                pltpu.VMEM((tiles_dev, part, time_dev), BF),
-            ],
-        )(ids, logit, x, *got_parts)
-        resids.append(resid)
-        sends.append(send)
+    resid, *sends = call(
+        functools.partial(resid_kernel, HALVES),
+        "resid",
+        2,
+        in_specs=[vmem()] * (2 + unit_count),
+        out_shape=[struct((tiles_dev, TILE, time_dev), F32)]
+        + [struct((CAP, part, time_dev), BF) for part in HALVES for _ in range(unit_count)],
+        scratch_shapes=[
+            pltpu.VMEM((tiles_dev, TILE, time_dev), F32),
+            pltpu.VMEM((tiles_dev, TILE, time_dev), BF),
+            SMEM((slots,), jnp.int32),
+        ],
+    )(logit, x, *got_parts)
+    sends = [sends[half * unit_count : (half + 1) * unit_count] for half in range(len(HALVES))]
 
     own_rows = units_dev // time_count
     wide = -(-(channels + HIST_ROWS * time_count) // TILE) * TILE
@@ -490,7 +476,7 @@
         own_kernel,
         "own",
         4,
-        in_specs=[vmem()] * 4,
+        in_specs=[vmem()] * 3,
         out_shape=[
             struct((own_rows, wide), F32 if shift == 0 else BF) for shift in range(time_count)
         ],
@@ -499,7 +485,7 @@
             pltpu.VMEM((units_dev, wide), F32),
             pltpu.VMEM((own_rows, wide), F32),
         ],
-    )(history, stimulus_t, *resids)
+    )(history, stimulus_t, resid)
 
     grads = []
     for send, part in zip(sends, HALVES, strict=True):

time: 99.5 us -> 99.3 us (level)
  starting transfers between devices: 41.2 us -> 43.4 us
  Pallas kernels: 23.1 us -> 21.5 us
    ppermute x21, starting transfers between devices: 20 us -> 22.6 us  [to_units(): lax.ppermute(pieces[k], 'unit', [(i, i ^ k) for i in range(len(pieces))])]
    pallas_call x4 -> x2, Pallas kernels: 6.21 us -> 4.52 us  [the longest x1 2.97 us: shards(): call(own_kernel, 'own', 4, in_specs=[vmem()] * 3, out_shape=[struct((own_...]
    ppermute x21, waiting for transfers between devices: 21.9 us -> 20.8 us  [to_units(): lax.ppermute(pieces[k], 'unit', [(i, i ^ k) for i in range(len(pieces))])]
  transfers between devices with their start and end apart: 28 -> 28, of which waited for: 6 -> 8; matrix products, arithmetic and copies ran while one was open for 0% -> 0% of each run, Pallas kernels for 19% -> 18%
where the time goes in v6:
time: 99.3 us; the launch traced here: 98.5 us
  starting transfers between devices  43.4 us (44%)
  waiting for transfers between devices  31.8 us (32%)
  Pallas kernels  21.5 us (22%)
  other arithmetic  1.08 us (1%)
    ppermute x21, starting transfers between devices, to_units(): lax.ppermute(pieces[k], 'unit', [(i, i ^ k) for i in range(len(pieces))])  22.6 us
    ppermute x21, waiting for transfers between devices, to_units(): lax.ppermute(pieces[k], 'unit', [(i, i ^ k) for i in range(len(pieces))])  20.8 us
    ppermute x6, starting transfers between devices, to_peers(): got.append(lax.ppermute(pieces[shift], 'tm', pairs))  15.8 us
    ppermute x6, waiting for transfers between devices, to_peers(): got.append(lax.ppermute(pieces[shift], 'tm', pairs))  10.7 us
    pallas_call x1, Pallas kernels, shards(): call(logit_kernel, 'logit', 5, in_specs=[vmem()] * 7, out_shape=[struct((...  5.5 us
    pallas_call x1, Pallas kernels, shards(): call(late_kernel, 'late', 5, in_specs=[hbm] * len(entry), out_specs=[vmem...  5.2 us
    ppermute x1, starting transfers between devices, shards(): halo = lax.ppermute(tail, 'tm', [(i, i + 1) for i in range(time_count - 1)])  4.94 us
    pallas_call x2, Pallas kernels, shards(): call(functools.partial(grad_kernel, unit_count, len(extras)), 'grad', 2,...  2.98 us
  transfers between devices with their start and end apart: 28, of which 8 were waited for; matrix products, arithmetic and copies ran while one was open for 0% of the time, Pallas kernels for 18%

profile of v6, /device:TPU:0, one launch (start us, length us, event | category | flops | bytes accessed | tf_op | source)
XLA Modules:
  0.0 98.5 jit_solution(3179374420826228127)
XLA Ops:
  1.7 4.9 %collective-permute-start = (bf16[128,1024]{1,0:T(8,128)(2,1)S(1)}, bf16[128,1024]{1,0:T(8,128)(2,1)S(1)}, u32[]{:S(2)}, u32[]{:S(2)}) collective-permute-start(bf16[128,1024]{1,0:T(8,128)(2,1)S(1)} %slice_convert_fusion), channel_id=1, source_target_pairs={{0,1},{1,2},{2,3},{4,5},{5,6},{6,7},{8,9},{9,10},{10,11},{12,13},{... | collective-permute-start | bytes 786440 | tf_op jit(solution)/shard_map/ppermute | solution.py:394
  6.7 5.2 %late.1 = (bf16[8,128,512]{2,1,0:T(8,128)(2,1)S(1)}, bf16[8,128,384]{2,1,0:T(8,128)(2,1)S(1)}, bf16[256,256]{1,0:T(8,128)(2,1)S(1)}, bf16[8,512,128]{2,1,0:T(8,1...) custom-call(s32[4,8]{1,0:T(4,128)} %bitcast.10, ...), custom_call_target="tpu_custom_call" | custom-call | flops 50000000 | bytes 1048576 | tf_op jit(solution)/shard_map/late/pallas_call | solution.py:399
  12.2 1.5 %early.1 = (bf16[8,128,128]{2,1,0:T(8,128)(2,1)S(1)}, bf16[1040,128]{1,0:T(8,128)(2,1)S(1)}, bf16[1040,128]{1,0:T(8,128)(2,1)S(1)}, bf16[1040,128]{1,0:T(8,128)(...) custom-call(s32[32]{0:T(128)S(1)} %get-tuple-element.63.slots, ...), custom_call_target="tpu_custom_call", output_to_operand_aliasing={{1}: (5, {}), {2}: (6, {}), {3}: (7, {}), {4}: (8, {}), {5}... | custom-call | flops 20000000 | bytes 1048576 | tf_op jit(solution)/shard_map/early/pallas_call | solution.py:427
  13.8 1.6 %collective-permute-start.2 = (bf16[1040,128]{1,0:T(8,128)(2,1)S(1)}, bf16[1040,128]{1,0:T(8,128)(2,1)S(1)}, u32[]{:S(2)}, u32[]{:S(2)}) collective-permute-start(bf16[1040,128]{1,0:T(8,128)(2,1)S(1)} %get-tuple-element.76), channel_id=1, source_target_pairs={{0,8},{4,12},{8,0},{12,4},{16,24},{20,28},{24,16},{28,20},{1,9},{5... | collective-permute-start | bytes 798728 | tf_op jit(solution)/shard_map/ppermute | solution.py:343
  15.7 1.5 %collective-permute-start.4 = (bf16[1040,128]{1,0:T(8,128)(2,1)S(1)}, bf16[1040,128]{1,0:T(8,128)(2,1)S(1)}, u32[]{:S(2)}, u32[]{:S(2)}) collective-permute-start(bf16[1040,128]{1,0:T(8,128)(2,1)S(1)} %get-tuple-element.78), channel_id=1, source_target_pairs={{0,16},{4,20},{8,24},{12,28},{16,0},{20,4},{24,8},{28,12},{1,17},{... | collective-permute-start | bytes 798728 | tf_op jit(solution)/shard_map/ppermute | solution.py:343
  17.4 2.4 %collective-permute-start.6 = (bf16[1040,128]{1,0:T(8,128)(2,1)S(1)}, bf16[1040,128]{1,0:T(8,128)(2,1)S(1)}, u32[]{:S(2)}, u32[]{:S(2)}) collective-permute-start(bf16[1040,128]{1,0:T(8,128)(2,1)S(1)} %get-tuple-element.80), channel_id=1, source_target_pairs={{0,24},{4,28},{8,16},{12,20},{16,8},{20,12},{24,0},{28,4},{1,25},{... | collective-permute-start | bytes 798728 | tf_op jit(solution)/shard_map/ppermute | solution.py:343
  19.8 3.3 %collective-permute-done.2.refs_2_ = bf16[1040,128]{1,0:T(8,128)(2,1)S(1)} collective-permute-done((bf16[1040,128]{1,0:T(8,128)(2,1)S(1)}, bf16[1040,128]{1,0:T(8,128)(2,1)S(1)}, u32[]{:S(2)}, u32[]{:S(2)}) %collective-permute-start.2) | collective-permute-done | bytes 266272 | tf_op jit(solution)/shard_map/ppermute | solution.py:343
  24.3 5.5 %logit.1 = (f32[8,128,512]{2,1,0:T(8,128)S(1)}, f32[8,10,128,512]{3,2,1,0:T(8,128)S(1)}) custom-call(bf16[8,128,512]{2,1,0:T(8,128)(2,1)S(1)} %get-tuple-element.60.x, bf16[128,1024]{1,0:T(8,128)(2,1)S(1)} %collective-permute-done.halo, bf16[256,1280]{1,0:T(8,128)(2,1)S(1)} %copy-done, f32[10,1024]{1,0:T(8,128)S(1)} %copy-done.3, f32[1,1024]{1,0:T(1,128)S(1)} %bitcast.9, ...), custom_call_target="tpu_custom_call" | custom-call | flops 50000000 | bytes 1048576 | tf_op jit(solution)/shard_map/logit/pallas_call | solution.py:447
  29.9 11.0 %collective-permute-done.5.refs_5_ = bf16[1040,128]{1,0:T(8,128)(2,1)S(1)} collective-permute-done((bf16[1040,128]{1,0:T(8,128)(2,1)S(1)}, bf16[1040,128]{1,0:T(8,128)(2,1)S(1)}, u32[]{:S(2)}, u32[]{:S(2)}) %collective-permute-start.5) | collective-permute-done | bytes 266272 | tf_op jit(solution)/shard_map/ppermute | solution.py:343
  40.9 1.6 %resid.1 = (f32[8,128,512]{2,1,0:T(8,128)S(1)}, bf16[2,64,512]{2,1,0:T(8,128)(2,1)S(1)}, bf16[2,64,512]{2,1,0:T(8,128)(2,1)S(1)}, bf16[2,64,512]{2,1,0:T(8,128)(...) custom-call(f32[8,128,512]{2,1,0:T(8,128)S(1)} %get-tuple-element.62, ...), custom_call_target="tpu_custom_call" | custom-call | flops 20000000 | bytes 1048576 | tf_op jit(solution)/shard_map/resid/pallas_call | solution.py:458
  44.4 1.5 %collective-permute-start.11 = (bf16[2,64,512]{2,1,0:T(8,128)(2,1)S(1)}, bf16[2,64,512]{2,1,0:T(8,128)(2,1)S(1)}, u32[]{:S(2)}, u32[]{:S(2)}) collective-permute-start(bf16[2,64,512]{2,1,0:T(8,128)(2,1)S(1)} %get-tuple-element.90), channel_id=1, source_target_pairs={{0,16},{4,20},{8,24},{12,28},{16,0},{20,4},{24,8},{28,12},{1,17},{... | collective-permute-start | bytes 393224 | tf_op jit(solution)/shard_map/ppermute | solution.py:343
  46.3 2.5 %collective-permute-start.13 = (bf16[2,64,512]{2,1,0:T(8,128)(2,1)S(1)}, bf16[2,64,512]{2,1,0:T(8,128)(2,1)S(1)}, u32[]{:S(2)}, u32[]{:S(2)}) collective-permute-start(bf16[2,64,512]{2,1,0:T(8,128)(2,1)S(1)} %get-tuple-element.92), channel_id=1, source_target_pairs={{0,24},{4,28},{8,16},{12,20},{16,8},{20,12},{24,0},{28,4},{1,25},{... | collective-permute-start | bytes 393224 | tf_op jit(solution)/shard_map/ppermute | solution.py:343
  52.1 1.5 %collective-permute-start.19 = (bf16[2,64,512]{2,1,0:T(8,128)(2,1)S(1)}, bf16[2,64,512]{2,1,0:T(8,128)(2,1)S(1)}, u32[]{:S(2)}, u32[]{:S(2)}) collective-permute-start(bf16[2,64,512]{2,1,0:T(8,128)(2,1)S(1)} %get-tuple-element.106), channel_id=1, source_target_pairs={{0,8},{4,12},{8,0},{12,4},{16,24},{20,28},{24,16},{28,20},{1,9},{5... | collective-permute-start | bytes 393224 | tf_op jit(solution)/shard_map/ppermute | solution.py:343
  53.6 4.8 %collective-permute-done.12.refs_5_ = bf16[2,64,512]{2,1,0:T(8,128)(2,1)S(1)} collective-permute-done((bf16[2,64,512]{2,1,0:T(8,128)(2,1)S(1)}, bf16[2,64,512]{2,1,0:T(8,128)(2,1)S(1)}, u32[]{:S(2)}, u32[]{:S(2)}) %collective-permute-start.12) | collective-permute-done | bytes 131104 | tf_op jit(solution)/shard_map/ppermute | solution.py:343
  58.4 1.6 %collective-permute-start.20 = (bf16[2,64,512]{2,1,0:T(8,128)(2,1)S(1)}, bf16[2,64,512]{2,1,0:T(8,128)(2,1)S(1)}, u32[]{:S(2)}, u32[]{:S(2)}) collective-permute-start(bf16[2,64,512]{2,1,0:T(8,128)(2,1)S(1)} %get-tuple-element.107), channel_id=1, source_target_pairs={{0,12},{4,8},{8,4},{12,0},{16,28},{20,24},{24,20},{28,16},{1,13},{... | collective-permute-start | bytes 393224 | tf_op jit(solution)/shard_map/ppermute | solution.py:343
  60.0 3.0 %own.1 = (f32[256,128]{1,0:T(8,128)S(1)}, bf16[256,128]{1,0:T(8,128)(2,1)S(1)}, bf16[256,128]{1,0:T(8,128)(2,1)S(1)}, bf16[256,128]{1,0:T(8,128)(2,1)S(1)}) custom-call(f32[8,10,128,512]{3,2,1,0:T(8,128)S(1)} %get-tuple-element.61.history, bf16[64,512]{1,0:T(8,128)(2,1)S(1)} %bitcast.7, f32[8,128,512]{2,1,0:T(8,128)S(1)} %get-tuple-element.82.residuals), custom_call_target="tpu_custom_call" | custom-call | flops 40000000 | bytes 1048576 | tf_op jit(solution)/shard_map/own/pallas_call | solution.py:475
  63.0 1.6 %collective-permute-start.21 = (bf16[2,64,512]{2,1,0:T(8,128)(2,1)S(1)}, bf16[2,64,512]{2,1,0:T(8,128)(2,1)S(1)}, u32[]{:S(2)}, u32[]{:S(2)}) collective-permute-start(bf16[2,64,512]{2,1,0:T(8,128)(2,1)S(1)} %get-tuple-element.108), channel_id=1, source_target_pairs={{0,16},{4,20},{8,24},{12,28},{16,0},{20,4},{24,8},{28,12},{1,17},{... | collective-permute-start | bytes 393224 | tf_op jit(solution)/shard_map/ppermute | solution.py:343
  64.6 1.5 %grad.2 = (bf16[256,256]{1,0:T(8,128)(2,1)S(1)}, bf16[256,384]{1,0:T(8,128)(2,1)S(1)}, bf16[256,384]{1,0:T(8,128)(2,1)S(1)}, bf16[256,384]{1,0:T(8,128)(2,1)S(1)}) custom-call(s32[32]{0:T(128)S(1)} %get-tuple-element.63.slots, bf16[8,128,128]{2,1,0:T(8,128)(2,1)S(1)} %get-tuple-element.84.mixed_early, bf16[8,128,384]{2,1,0:T(8,128)(2,1)S(1)} %get-tuple-element.85.mixed_late, ...), custom_call_target="tpu_custom_call" | custom-call | flops 20000000 | bytes 1048576 | tf_op jit(solution)/shard_map/grad/pallas_call | solution.py:495
  66.1 2.5 %collective-permute-start.15 = (bf16[256,384]{1,0:T(8,128)(2,1)S(1)}, bf16[256,384]{1,0:T(8,128)(2,1)S(1)}, u32[]{:S(2)}, u32[]{:S(2)}) collective-permute-start(bf16[256,384]{1,0:T(8,128)(2,1)S(1)} %get-tuple-element.97), channel_id=1, source_target_pairs={{0,1},{1,2},{2,3},{3,0},{4,5},{5,6},{6,7},{7,4},{8,9},{9,10},{10,1... | collective-permute-start | bytes 589832 | tf_op jit(solution)/shard_map/ppermute | solution.py:336
  71.2 2.6 %collective-permute-start.16 = (bf16[256,384]{1,0:T(8,128)(2,1)S(1)}, bf16[256,384]{1,0:T(8,128)(2,1)S(1)}, u32[]{:S(2)}, u32[]{:S(2)}) collective-permute-start(bf16[256,384]{1,0:T(8,128)(2,1)S(1)} %get-tuple-element.98), channel_id=1, source_target_pairs={{0,2},{1,3},{2,0},{3,1},{4,6},{5,7},{6,4},{7,5},{8,10},{9,11},{10,... | collective-permute-start | bytes 589832 | tf_op jit(solution)/shard_map/ppermute | solution.py:336
  73.8 6.8 %collective-permute-start.17 = (bf16[256,384]{1,0:T(8,128)(2,1)S(1)}, bf16[256,384]{1,0:T(8,128)(2,1)S(1)}, u32[]{:S(2)}, u32[]{:S(2)}) collective-permute-start(bf16[256,384]{1,0:T(8,128)(2,1)S(1)} %get-tuple-element.99), channel_id=1, source_target_pairs={{0,3},{1,0},{2,1},{3,2},{4,7},{5,4},{6,5},{7,6},{8,11},{9,8},{10,9... | collective-permute-start | bytes 589832 | tf_op jit(solution)/shard_map/ppermute | solution.py:336
  82.8 3.3 %collective-permute-start.27 = (bf16[256,256]{1,0:T(8,128)(2,1)S(1)}, bf16[256,256]{1,0:T(8,128)(2,1)S(1)}, u32[]{:S(2)}, u32[]{:S(2)}) collective-permute-start(bf16[256,256]{1,0:T(8,128)(2,1)S(1)} %get-tuple-element.115), channel_id=1, source_target_pairs={{0,3},{1,0},{2,1},{3,2},{4,7},{5,4},{6,5},{7,6},{8,11},{9,8},{10,9... | collective-permute-start | bytes 393224 | tf_op jit(solution)/shard_map/ppermute | solution.py:336
  86.8 3.6 %collective-permute-done.25.refs_5_ = bf16[256,256]{1,0:T(8,128)(2,1)S(1)} collective-permute-done((bf16[256,256]{1,0:T(8,128)(2,1)S(1)}, bf16[256,256]{1,0:T(8,128)(2,1)S(1)}, u32[]{:S(2)}, u32[]{:S(2)}) %collective-permute-start.25) | collective-permute-done | bytes 131104 | tf_op jit(solution)/shard_map/ppermute | solution.py:336
  90.4 7.1 %collective-permute-done.26.refs_6_ = bf16[256,256]{1,0:T(8,128)(2,1)S(1)} collective-permute-done((bf16[256,256]{1,0:T(8,128)(2,1)S(1)}, bf16[256,256]{1,0:T(8,128)(2,1)S(1)}, u32[]{:S(2)}, u32[]{:S(2)}) %collective-permute-start.26) | collective-permute-done | bytes 131104 | tf_op jit(solution)/shard_map/ppermute | solution.py:336
  (52 shorter events, 15.4 us)
Async XLA Ops:
  1.7 10.5 %collective-permute-start = (bf16[128,1024]{1,0:T(8,128)(2,1)S(1)}, bf16[128,1024]{1,0:T(8,128)(2,1)S(1)}, u32[]{:S(2)}, u32[]{:S(2)}) collective-permute-start(bf16[128,1024]{1,0:T(8,128)(2,1)S(1)} %slice_convert_fusion), channel_id=1, source_target_pairs={{0,1},{1,2},{2,3},{4,5},{5,6},{6,7},{8,9},{9,10},{10,11},{12,13},{... | collective-permute-start | bytes 786440 | tf_op jit(solution)/shard_map/ppermute | solution.py:394
  13.8 9.3 %collective-permute-start.2 = (bf16[1040,128]{1,0:T(8,128)(2,1)S(1)}, bf16[1040,128]{1,0:T(8,128)(2,1)S(1)}, u32[]{:S(2)}, u32[]{:S(2)}) collective-permute-start(bf16[1040,128]{1,0:T(8,128)(2,1)S(1)} %get-tuple-element.76), channel_id=1, source_target_pairs={{0,8},{4,12},{8,0},{12,4},{16,24},{20,28},{24,16},{28,20},{1,9},{5... | collective-permute-start | bytes 798728 | tf_op jit(solution)/shard_map/ppermute | solution.py:343
  15.3 14.5 %collective-permute-start.3 = (bf16[1040,128]{1,0:T(8,128)(2,1)S(1)}, bf16[1040,128]{1,0:T(8,128)(2,1)S(1)}, u32[]{:S(2)}, u32[]{:S(2)}) collective-permute-start(bf16[1040,128]{1,0:T(8,128)(2,1)S(1)} %get-tuple-element.77), channel_id=1, source_target_pairs={{0,12},{4,8},{8,4},{12,0},{16,28},{20,24},{24,20},{28,16},{1,13},{... | collective-permute-start | bytes 798728 | tf_op jit(solution)/shard_map/ppermute | solution.py:343
  15.7 14.2 %collective-permute-start.4 = (bf16[1040,128]{1,0:T(8,128)(2,1)S(1)}, bf16[1040,128]{1,0:T(8,128)(2,1)S(1)}, u32[]{:S(2)}, u32[]{:S(2)}) collective-permute-start(bf16[1040,128]{1,0:T(8,128)(2,1)S(1)} %get-tuple-element.78), channel_id=1, source_target_pairs={{0,16},{4,20},{8,24},{12,28},{16,0},{20,4},{24,8},{28,12},{1,17},{... | collective-permute-start | bytes 798728 | tf_op jit(solution)/shard_map/ppermute | solution.py:343
  17.2 23.7 %collective-permute-start.5 = (bf16[1040,128]{1,0:T(8,128)(2,1)S(1)}, bf16[1040,128]{1,0:T(8,128)(2,1)S(1)}, u32[]{:S(2)}, u32[]{:S(2)}) collective-permute-start(bf16[1040,128]{1,0:T(8,128)(2,1)S(1)} %get-tuple-element.79), channel_id=1, source_target_pairs={{0,20},{4,16},{8,28},{12,24},{16,4},{20,0},{24,12},{28,8},{1,21},{... | collective-permute-start | bytes 798728 | tf_op jit(solution)/shard_map/ppermute | solution.py:343
  17.4 23.5 %collective-permute-start.6 = (bf16[1040,128]{1,0:T(8,128)(2,1)S(1)}, bf16[1040,128]{1,0:T(8,128)(2,1)S(1)}, u32[]{:S(2)}, u32[]{:S(2)}) collective-permute-start(bf16[1040,128]{1,0:T(8,128)(2,1)S(1)} %get-tuple-element.80), channel_id=1, source_target_pairs={{0,24},{4,28},{8,16},{12,20},{16,8},{20,12},{24,0},{28,4},{1,25},{... | collective-permute-start | bytes 798728 | tf_op jit(solution)/shard_map/ppermute | solution.py:343
  23.1 17.8 %collective-permute-start.7 = (bf16[1040,128]{1,0:T(8,128)(2,1)S(1)}, bf16[1040,128]{1,0:T(8,128)(2,1)S(1)}, u32[]{:S(2)}, u32[]{:S(2)}) collective-permute-start(bf16[1040,128]{1,0:T(8,128)(2,1)S(1)} %get-tuple-element.81), channel_id=1, source_target_pairs={{0,28},{4,24},{8,20},{12,16},{16,12},{20,8},{24,4},{28,0},{1,29},{... | collective-permute-start | bytes 798728 | tf_op jit(solution)/shard_map/ppermute | solution.py:343
  44.4 7.7 %collective-permute-start.11 = (bf16[2,64,512]{2,1,0:T(8,128)(2,1)S(1)}, bf16[2,64,512]{2,1,0:T(8,128)(2,1)S(1)}, u32[]{:S(2)}, u32[]{:S(2)}) collective-permute-start(bf16[2,64,512]{2,1,0:T(8,128)(2,1)S(1)} %get-tuple-element.90), channel_id=1, source_target_pairs={{0,16},{4,20},{8,24},{12,28},{16,0},{20,4},{24,8},{28,12},{1,17},{... | collective-permute-start | bytes 393224 | tf_op jit(solution)/shard_map/ppermute | solution.py:343
  45.9 12.5 %collective-permute-start.12 = (bf16[2,64,512]{2,1,0:T(8,128)(2,1)S(1)}, bf16[2,64,512]{2,1,0:T(8,128)(2,1)S(1)}, u32[]{:S(2)}, u32[]{:S(2)}) collective-permute-start(bf16[2,64,512]{2,1,0:T(8,128)(2,1)S(1)} %get-tuple-element.91), channel_id=1, source_target_pairs={{0,20},{4,16},{8,28},{12,24},{16,4},{20,0},{24,12},{28,8},{1,21},{... | collective-permute-start | bytes 393224 | tf_op jit(solution)/shard_map/ppermute | solution.py:343
  46.3 16.7 %collective-permute-start.13 = (bf16[2,64,512]{2,1,0:T(8,128)(2,1)S(1)}, bf16[2,64,512]{2,1,0:T(8,128)(2,1)S(1)}, u32[]{:S(2)}, u32[]{:S(2)}) collective-permute-start(bf16[2,64,512]{2,1,0:T(8,128)(2,1)S(1)} %get-tuple-element.92), channel_id=1, source_target_pairs={{0,24},{4,28},{8,16},{12,20},{16,8},{20,12},{24,0},{28,4},{1,25},{... | collective-permute-start | bytes 393224 | tf_op jit(solution)/shard_map/ppermute | solution.py:343
  49.2 15.5 %collective-permute-start.14 = (bf16[2,64,512]{2,1,0:T(8,128)(2,1)S(1)}, bf16[2,64,512]{2,1,0:T(8,128)(2,1)S(1)}, u32[]{:S(2)}, u32[]{:S(2)}) collective-permute-start(bf16[2,64,512]{2,1,0:T(8,128)(2,1)S(1)} %get-tuple-element.93), channel_id=1, source_target_pairs={{0,28},{4,24},{8,20},{12,16},{16,12},{20,8},{24,4},{28,0},{1,29},{... | collective-permute-start | bytes 393224 | tf_op jit(solution)/shard_map/ppermute | solution.py:343
  51.0 15.2 %collective-permute-start.18 = (bf16[2,64,512]{2,1,0:T(8,128)(2,1)S(1)}, bf16[2,64,512]{2,1,0:T(8,128)(2,1)S(1)}, u32[]{:S(2)}, u32[]{:S(2)}) collective-permute-start(bf16[2,64,512]{2,1,0:T(8,128)(2,1)S(1)} %get-tuple-element.105), channel_id=1, source_target_pairs={{0,4},{4,0},{8,12},{12,8},{16,20},{20,16},{24,28},{28,24},{1,5},{5... | collective-permute-start | bytes 393224 | tf_op jit(solution)/shard_map/ppermute | solution.py:343
  52.1 16.6 %collective-permute-start.19 = (bf16[2,64,512]{2,1,0:T(8,128)(2,1)S(1)}, bf16[2,64,512]{2,1,0:T(8,128)(2,1)S(1)}, u32[]{:S(2)}, u32[]{:S(2)}) collective-permute-start(bf16[2,64,512]{2,1,0:T(8,128)(2,1)S(1)} %get-tuple-element.106), channel_id=1, source_target_pairs={{0,8},{4,12},{8,0},{12,4},{16,24},{20,28},{24,16},{28,20},{1,9},{5... | collective-permute-start | bytes 393224 | tf_op jit(solution)/shard_map/ppermute | solution.py:343
  58.4 11.7 %collective-permute-start.20 = (bf16[2,64,512]{2,1,0:T(8,128)(2,1)S(1)}, bf16[2,64,512]{2,1,0:T(8,128)(2,1)S(1)}, u32[]{:S(2)}, u32[]{:S(2)}) collective-permute-start(bf16[2,64,512]{2,1,0:T(8,128)(2,1)S(1)} %get-tuple-element.107), channel_id=1, source_target_pairs={{0,12},{4,8},{8,4},{12,0},{16,28},{20,24},{24,20},{28,16},{1,13},{... | collective-permute-start | bytes 393224 | tf_op jit(solution)/shard_map/ppermute | solution.py:343
  63.0 8.2 %collective-permute-start.21 = (bf16[2,64,512]{2,1,0:T(8,128)(2,1)S(1)}, bf16[2,64,512]{2,1,0:T(8,128)(2,1)S(1)}, u32[]{:S(2)}, u32[]{:S(2)}) collective-permute-start(bf16[2,64,512]{2,1,0:T(8,128)(2,1)S(1)} %get-tuple-element.108), channel_id=1, source_target_pairs={{0,16},{4,20},{8,24},{12,28},{16,0},{20,4},{24,8},{28,12},{1,17},{... | collective-permute-start | bytes 393224 | tf_op jit(solution)/shard_map/ppermute | solution.py:343
  64.6 9.2 %collective-permute-start.22 = (bf16[2,64,512]{2,1,0:T(8,128)(2,1)S(1)}, bf16[2,64,512]{2,1,0:T(8,128)(2,1)S(1)}, u32[]{:S(2)}, u32[]{:S(2)}) collective-permute-start(bf16[2,64,512]{2,1,0:T(8,128)(2,1)S(1)} %get-tuple-element.109), channel_id=1, source_target_pairs={{0,20},{4,16},{8,28},{12,24},{16,4},{20,0},{24,12},{28,8},{1,21},{... | collective-permute-start | bytes 393224 | tf_op jit(solution)/shard_map/ppermute | solution.py:343
  66.1 16.6 %collective-permute-start.15 = (bf16[256,384]{1,0:T(8,128)(2,1)S(1)}, bf16[256,384]{1,0:T(8,128)(2,1)S(1)}, u32[]{:S(2)}, u32[]{:S(2)}) collective-permute-start(bf16[256,384]{1,0:T(8,128)(2,1)S(1)} %get-tuple-element.97), channel_id=1, source_target_pairs={{0,1},{1,2},{2,3},{3,0},{4,5},{5,6},{6,7},{7,4},{8,9},{9,10},{10,1... | collective-permute-start | bytes 589832 | tf_op jit(solution)/shard_map/ppermute | solution.py:336
  68.7 11.9 %collective-permute-start.23 = (bf16[2,64,512]{2,1,0:T(8,128)(2,1)S(1)}, bf16[2,64,512]{2,1,0:T(8,128)(2,1)S(1)}, u32[]{:S(2)}, u32[]{:S(2)}) collective-permute-start(bf16[2,64,512]{2,1,0:T(8,128)(2,1)S(1)} %get-tuple-element.110), channel_id=1, source_target_pairs={{0,24},{4,28},{8,16},{12,20},{16,8},{20,12},{24,0},{28,4},{1,25},{... | collective-permute-start | bytes 393224 | tf_op jit(solution)/shard_map/ppermute | solution.py:343
  70.1 10.6 %collective-permute-start.24 = (bf16[2,64,512]{2,1,0:T(8,128)(2,1)S(1)}, bf16[2,64,512]{2,1,0:T(8,128)(2,1)S(1)}, u32[]{:S(2)}, u32[]{:S(2)}) collective-permute-start(bf16[2,64,512]{2,1,0:T(8,128)(2,1)S(1)} %get-tuple-element.111), channel_id=1, source_target_pairs={{0,28},{4,24},{8,20},{12,16},{16,12},{20,8},{24,4},{28,0},{1,29},{... | collective-permute-start | bytes 393224 | tf_op jit(solution)/shard_map/ppermute | solution.py:343
  71.2 14.8 %collective-permute-start.16 = (bf16[256,384]{1,0:T(8,128)(2,1)S(1)}, bf16[256,384]{1,0:T(8,128)(2,1)S(1)}, u32[]{:S(2)}, u32[]{:S(2)}) collective-permute-start(bf16[256,384]{1,0:T(8,128)(2,1)S(1)} %get-tuple-element.98), channel_id=1, source_target_pairs={{0,2},{1,3},{2,0},{3,1},{4,6},{5,7},{6,4},{7,5},{8,10},{9,11},{10,... | collective-permute-start | bytes 589832 | tf_op jit(solution)/shard_map/ppermute | solution.py:336
  73.8 12.2 %collective-permute-start.17 = (bf16[256,384]{1,0:T(8,128)(2,1)S(1)}, bf16[256,384]{1,0:T(8,128)(2,1)S(1)}, u32[]{:S(2)}, u32[]{:S(2)}) collective-permute-start(bf16[256,384]{1,0:T(8,128)(2,1)S(1)} %get-tuple-element.99), channel_id=1, source_target_pairs={{0,3},{1,0},{2,1},{3,2},{4,7},{5,4},{6,5},{7,6},{8,11},{9,8},{10,9... | collective-permute-start | bytes 589832 | tf_op jit(solution)/shard_map/ppermute | solution.py:336
  82.1 8.3 %collective-permute-start.25 = (bf16[256,256]{1,0:T(8,128)(2,1)S(1)}, bf16[256,256]{1,0:T(8,128)(2,1)S(1)}, u32[]{:S(2)}, u32[]{:S(2)}) collective-permute-start(bf16[256,256]{1,0:T(8,128)(2,1)S(1)} %get-tuple-element.113), channel_id=1, source_target_pairs={{0,1},{1,2},{2,3},{3,0},{4,5},{5,6},{6,7},{7,4},{8,9},{9,10},{10,1... | collective-permute-start | bytes 393224 | tf_op jit(solution)/shard_map/ppermute | solution.py:336
  82.2 15.3 %collective-permute-start.26 = (bf16[256,256]{1,0:T(8,128)(2,1)S(1)}, bf16[256,256]{1,0:T(8,128)(2,1)S(1)}, u32[]{:S(2)}, u32[]{:S(2)}) collective-permute-start(bf16[256,256]{1,0:T(8,128)(2,1)S(1)} %get-tuple-element.114), channel_id=1, source_target_pairs={{0,2},{1,3},{2,0},{3,1},{4,6},{5,7},{6,4},{7,5},{8,10},{9,11},{10,... | collective-permute-start | bytes 393224 | tf_op jit(solution)/shard_map/ppermute | solution.py:336
  82.8 14.7 %collective-permute-start.27 = (bf16[256,256]{1,0:T(8,128)(2,1)S(1)}, bf16[256,256]{1,0:T(8,128)(2,1)S(1)}, u32[]{:S(2)}, u32[]{:S(2)}) collective-permute-start(bf16[256,256]{1,0:T(8,128)(2,1)S(1)} %get-tuple-element.115), channel_id=1, source_target_pairs={{0,3},{1,0},{2,1},{3,2},{4,7},{5,4},{6,5},{7,6},{8,11},{9,8},{10,9... | collective-permute-start | bytes 393224 | tf_op jit(solution)/shard_map/ppermute | solution.py:336
  (9 other events, 81.2 us)

commit v7 on v6

--- a/solution.py
+++ b/solution.py
@@ -331,7 +331,7 @@
 def to_peers(pieces):
     count = len(pieces)
     got = [pieces[0]]
-    for shift in range(1, count):
+    for shift in [1, *range(count - 1, 1, -1)]:
         pairs = [(i, (i + shift) % count) for i in range(count)]
         got.append(lax.ppermute(pieces[shift], "tm", pairs))
     return got

time: 99.3 us -> 101 us (1.017)
  waiting for transfers between devices: 31.8 us -> 39.5 us
  starting transfers between devices: 43.4 us -> 38.5 us
    ppermute x6, starting transfers between devices: 15.8 us -> 11.1 us  [to_peers(): got.append(lax.ppermute(pieces[shift], 'tm', pairs))]
    ppermute x6, waiting for transfers between devices: 10.7 us -> 15.1 us  [to_peers(): got.append(lax.ppermute(pieces[shift], 'tm', pairs))]
    ppermute x21, waiting for transfers between devices: 20.8 us -> 24 us  [to_units(): lax.ppermute(pieces[k], 'unit', [(i, i ^ k) for i in range(len(pieces))])]
  transfers between devices with their start and end apart: 28 -> 28, of which waited for: 8 -> 11; matrix products, arithmetic and copies ran while one was open for 0% -> 0% of each run, Pallas kernels for 18% -> 17%
where the time goes in v7:
time: 101 us
  waiting for transfers between devices  39.5 us (39%)
  starting transfers between devices  38.5 us (38%)
  Pallas kernels  21.4 us (21%)
  other arithmetic  1.08 us (1%)
    ppermute x21, waiting for transfers between devices, to_units(): lax.ppermute(pieces[k], 'unit', [(i, i ^ k) for i in range(len(pieces))])  24 us
    ppermute x21, starting transfers between devices, to_units(): lax.ppermute(pieces[k], 'unit', [(i, i ^ k) for i in range(len(pieces))])  22.5 us
    ppermute x6, waiting for transfers between devices, to_peers(): got.append(lax.ppermute(pieces[shift], 'tm', pairs))  15.1 us
    ppermute x6, starting transfers between devices, to_peers(): got.append(lax.ppermute(pieces[shift], 'tm', pairs))  11.1 us
    pallas_call x1, Pallas kernels, shards(): call(logit_kernel, 'logit', 5, in_specs=[vmem()] * 7, out_shape=[struct((...  5.5 us
    pallas_call x1, Pallas kernels, shards(): call(late_kernel, 'late', 5, in_specs=[hbm] * len(entry), out_specs=[vmem...  5.2 us
    ppermute x1, starting transfers between devices, shards(): halo = lax.ppermute(tail, 'tm', [(i, i + 1) for i in range(time_count - 1)])  4.94 us
    pallas_call x2, Pallas kernels, shards(): call(functools.partial(grad_kernel, unit_count, len(extras)), 'grad', 2,...  2.98 us
  transfers between devices with their start and end apart: 28, of which 11 were waited for; matrix products, arithmetic and copies ran while one was open for 0% of the time, Pallas kernels for 17%

profile of v7, /device:TPU:0, one launch (start us, length us, event | category | flops | bytes accessed | tf_op | source)
XLA Modules:
  0.0 101.3 jit_solution(4444348744641387103)
XLA Ops:
  1.7 4.9 %collective-permute-start = (bf16[128,1024]{1,0:T(8,128)(2,1)S(1)}, bf16[128,1024]{1,0:T(8,128)(2,1)S(1)}, u32[]{:S(2)}, u32[]{:S(2)}) collective-permute-start(bf16[128,1024]{1,0:T(8,128)(2,1)S(1)} %slice_convert_fusion), channel_id=1, source_target_pairs={{0,1},{1,2},{2,3},{4,5},{5,6},{6,7},{8,9},{9,10},{10,11},{12,13},{... | collective-permute-start | bytes 786440 | tf_op jit(solution)/shard_map/ppermute | solution.py:394
  6.7 5.2 %late.1 = (bf16[8,128,512]{2,1,0:T(8,128)(2,1)S(1)}, bf16[8,128,384]{2,1,0:T(8,128)(2,1)S(1)}, bf16[256,256]{1,0:T(8,128)(2,1)S(1)}, bf16[8,512,128]{2,1,0:T(8,1...) custom-call(s32[4,8]{1,0:T(4,128)} %bitcast.10, ...), custom_call_target="tpu_custom_call" | custom-call | flops 50000000 | bytes 1048576 | tf_op jit(solution)/shard_map/late/pallas_call | solution.py:399
  12.2 1.5 %early.1 = (bf16[8,128,128]{2,1,0:T(8,128)(2,1)S(1)}, bf16[1040,128]{1,0:T(8,128)(2,1)S(1)}, bf16[1040,128]{1,0:T(8,128)(2,1)S(1)}, bf16[1040,128]{1,0:T(8,128)(...) custom-call(s32[32]{0:T(128)S(1)} %get-tuple-element.63.slots, ...), custom_call_target="tpu_custom_call", output_to_operand_aliasing={{1}: (5, {}), {2}: (6, {}), {3}: (7, {}), {4}: (8, {}), {5}... | custom-call | flops 20000000 | bytes 1048576 | tf_op jit(solution)/shard_map/early/pallas_call | solution.py:427
  13.8 1.6 %collective-permute-start.2 = (bf16[1040,128]{1,0:T(8,128)(2,1)S(1)}, bf16[1040,128]{1,0:T(8,128)(2,1)S(1)}, u32[]{:S(2)}, u32[]{:S(2)}) collective-permute-start(bf16[1040,128]{1,0:T(8,128)(2,1)S(1)} %get-tuple-element.76), channel_id=1, source_target_pairs={{0,8},{4,12},{8,0},{12,4},{16,24},{20,28},{24,16},{28,20},{1,9},{5... | collective-permute-start | bytes 798728 | tf_op jit(solution)/shard_map/ppermute | solution.py:343
  15.7 1.5 %collective-permute-start.4 = (bf16[1040,128]{1,0:T(8,128)(2,1)S(1)}, bf16[1040,128]{1,0:T(8,128)(2,1)S(1)}, u32[]{:S(2)}, u32[]{:S(2)}) collective-permute-start(bf16[1040,128]{1,0:T(8,128)(2,1)S(1)} %get-tuple-element.78), channel_id=1, source_target_pairs={{0,16},{4,20},{8,24},{12,28},{16,0},{20,4},{24,8},{28,12},{1,17},{... | collective-permute-start | bytes 798728 | tf_op jit(solution)/shard_map/ppermute | solution.py:343
  17.4 2.4 %collective-permute-start.6 = (bf16[1040,128]{1,0:T(8,128)(2,1)S(1)}, bf16[1040,128]{1,0:T(8,128)(2,1)S(1)}, u32[]{:S(2)}, u32[]{:S(2)}) collective-permute-start(bf16[1040,128]{1,0:T(8,128)(2,1)S(1)} %get-tuple-element.80), channel_id=1, source_target_pairs={{0,24},{4,28},{8,16},{12,20},{16,8},{20,12},{24,0},{28,4},{1,25},{... | collective-permute-start | bytes 798728 | tf_op jit(solution)/shard_map/ppermute | solution.py:343
  19.8 3.3 %collective-permute-done.2.refs_2_ = bf16[1040,128]{1,0:T(8,128)(2,1)S(1)} collective-permute-done((bf16[1040,128]{1,0:T(8,128)(2,1)S(1)}, bf16[1040,128]{1,0:T(8,128)(2,1)S(1)}, u32[]{:S(2)}, u32[]{:S(2)}) %collective-permute-start.2) | collective-permute-done | bytes 266272 | tf_op jit(solution)/shard_map/ppermute | solution.py:343
  24.3 5.5 %logit.1 = (f32[8,128,512]{2,1,0:T(8,128)S(1)}, f32[8,10,128,512]{3,2,1,0:T(8,128)S(1)}) custom-call(bf16[8,128,512]{2,1,0:T(8,128)(2,1)S(1)} %get-tuple-element.60.x, bf16[128,1024]{1,0:T(8,128)(2,1)S(1)} %collective-permute-done.halo, bf16[256,1280]{1,0:T(8,128)(2,1)S(1)} %copy-done, f32[10,1024]{1,0:T(8,128)S(1)} %copy-done.3, f32[1,1024]{1,0:T(1,128)S(1)} %bitcast.9, ...), custom_call_target="tpu_custom_call" | custom-call | flops 50000000 | bytes 1048576 | tf_op jit(solution)/shard_map/logit/pallas_call | solution.py:447
  29.9 11.0 %collective-permute-done.5.refs_5_ = bf16[1040,128]{1,0:T(8,128)(2,1)S(1)} collective-permute-done((bf16[1040,128]{1,0:T(8,128)(2,1)S(1)}, bf16[1040,128]{1,0:T(8,128)(2,1)S(1)}, u32[]{:S(2)}, u32[]{:S(2)}) %collective-permute-start.5) | collective-permute-done | bytes 266272 | tf_op jit(solution)/shard_map/ppermute | solution.py:343
  44.3 1.6 %collective-permute-start.11 = (bf16[2,64,512]{2,1,0:T(8,128)(2,1)S(1)}, bf16[2,64,512]{2,1,0:T(8,128)(2,1)S(1)}, u32[]{:S(2)}, u32[]{:S(2)}) collective-permute-start(bf16[2,64,512]{2,1,0:T(8,128)(2,1)S(1)} %get-tuple-element.90), channel_id=1, source_target_pairs={{0,16},{4,20},{8,24},{12,28},{16,0},{20,4},{24,8},{28,12},{1,17},{... | collective-permute-start | bytes 393224 | tf_op jit(solution)/shard_map/ppermute | solution.py:343
  46.4 2.4 %collective-permute-start.13 = (bf16[2,64,512]{2,1,0:T(8,128)(2,1)S(1)}, bf16[2,64,512]{2,1,0:T(8,128)(2,1)S(1)}, u32[]{:S(2)}, u32[]{:S(2)}) collective-permute-start(bf16[2,64,512]{2,1,0:T(8,128)(2,1)S(1)} %get-tuple-element.92), channel_id=1, source_target_pairs={{0,24},{4,28},{8,16},{12,20},{16,8},{20,12},{24,0},{28,4},{1,25},{... | collective-permute-start | bytes 393224 | tf_op jit(solution)/shard_map/ppermute | solution.py:343
  53.5 5.0 %collective-permute-done.12.refs_5_ = bf16[2,64,512]{2,1,0:T(8,128)(2,1)S(1)} collective-permute-done((bf16[2,64,512]{2,1,0:T(8,128)(2,1)S(1)}, bf16[2,64,512]{2,1,0:T(8,128)(2,1)S(1)}, u32[]{:S(2)}, u32[]{:S(2)}) %collective-permute-start.12) | collective-permute-done | bytes 131104 | tf_op jit(solution)/shard_map/ppermute | solution.py:343
  58.5 1.4 %collective-permute-start.20 = (bf16[2,64,512]{2,1,0:T(8,128)(2,1)S(1)}, bf16[2,64,512]{2,1,0:T(8,128)(2,1)S(1)}, u32[]{:S(2)}, u32[]{:S(2)}) collective-permute-start(bf16[2,64,512]{2,1,0:T(8,128)(2,1)S(1)} %get-tuple-element.107), channel_id=1, source_target_pairs={{0,12},{4,8},{8,4},{12,0},{16,28},{20,24},{24,20},{28,16},{1,13},{... | collective-permute-start | bytes 393224 | tf_op jit(solution)/shard_map/ppermute | solution.py:343
  59.9 3.0 %own.1 = (f32[256,128]{1,0:T(8,128)S(1)}, bf16[256,128]{1,0:T(8,128)(2,1)S(1)}, bf16[256,128]{1,0:T(8,128)(2,1)S(1)}, bf16[256,128]{1,0:T(8,128)(2,1)S(1)}) custom-call(f32[8,10,128,512]{3,2,1,0:T(8,128)S(1)} %get-tuple-element.61.history, bf16[64,512]{1,0:T(8,128)(2,1)S(1)} %bitcast.7, f32[8,128,512]{2,1,0:T(8,128)S(1)} %get-tuple-element.82.residuals), custom_call_target="tpu_custom_call" | custom-call | flops 40000000 | bytes 1048576 | tf_op jit(solution)/shard_map/own/pallas_call | solution.py:475
  62.9 1.7 %collective-permute-start.21 = (bf16[2,64,512]{2,1,0:T(8,128)(2,1)S(1)}, bf16[2,64,512]{2,1,0:T(8,128)(2,1)S(1)}, u32[]{:S(2)}, u32[]{:S(2)}) collective-permute-start(bf16[2,64,512]{2,1,0:T(8,128)(2,1)S(1)} %get-tuple-element.108), channel_id=1, source_target_pairs={{0,16},{4,20},{8,24},{12,28},{16,0},{20,4},{24,8},{28,12},{1,17},{... | collective-permute-start | bytes 393224 | tf_op jit(solution)/shard_map/ppermute | solution.py:343
  64.6 1.5 %grad.2 = (bf16[256,256]{1,0:T(8,128)(2,1)S(1)}, bf16[256,384]{1,0:T(8,128)(2,1)S(1)}, bf16[256,384]{1,0:T(8,128)(2,1)S(1)}, bf16[256,384]{1,0:T(8,128)(2,1)S(1)}) custom-call(s32[32]{0:T(128)S(1)} %get-tuple-element.63.slots, bf16[8,128,128]{2,1,0:T(8,128)(2,1)S(1)} %get-tuple-element.84.mixed_early, bf16[8,128,384]{2,1,0:T(8,128)(2,1)S(1)} %get-tuple-element.85.mixed_late, ...), custom_call_target="tpu_custom_call" | custom-call | flops 20000000 | bytes 1048576 | tf_op jit(solution)/shard_map/grad/pallas_call | solution.py:495
  66.1 2.5 %collective-permute-start.15 = (bf16[256,384]{1,0:T(8,128)(2,1)S(1)}, bf16[256,384]{1,0:T(8,128)(2,1)S(1)}, u32[]{:S(2)}, u32[]{:S(2)}) collective-permute-start(bf16[256,384]{1,0:T(8,128)(2,1)S(1)} %get-tuple-element.97), channel_id=1, source_target_pairs={{0,1},{1,2},{2,3},{3,0},{4,5},{5,6},{6,7},{7,4},{8,9},{9,10},{10,1... | collective-permute-start | bytes 589832 | tf_op jit(solution)/shard_map/ppermute | solution.py:336
  71.2 2.6 %collective-permute-start.16 = (bf16[256,384]{1,0:T(8,128)(2,1)S(1)}, bf16[256,384]{1,0:T(8,128)(2,1)S(1)}, u32[]{:S(2)}, u32[]{:S(2)}) collective-permute-start(bf16[256,384]{1,0:T(8,128)(2,1)S(1)} %get-tuple-element.98), channel_id=1, source_target_pairs={{0,3},{1,0},{2,1},{3,2},{4,7},{5,4},{6,5},{7,6},{8,11},{9,8},{10,9... | collective-permute-start | bytes 589832 | tf_op jit(solution)/shard_map/ppermute | solution.py:336
  74.2 1.7 %collective-permute-done.23.refs_6_ = bf16[2,64,512]{2,1,0:T(8,128)(2,1)S(1)} collective-permute-done((bf16[2,64,512]{2,1,0:T(8,128)(2,1)S(1)}, bf16[2,64,512]{2,1,0:T(8,128)(2,1)S(1)}, u32[]{:S(2)}, u32[]{:S(2)}) %collective-permute-start.23) | collective-permute-done | bytes 131104 | tf_op jit(solution)/shard_map/ppermute | solution.py:343
  77.3 1.5 %grad.3 = (bf16[256,256]{1,0:T(8,128)(2,1)S(1)}, bf16[256,256]{1,0:T(8,128)(2,1)S(1)}, bf16[256,256]{1,0:T(8,128)(2,1)S(1)}, bf16[256,256]{1,0:T(8,128)(2,1)S(1)}) custom-call(s32[32]{0:T(128)S(1)} %get-tuple-element.63.slots, bf16[8,128,128]{2,1,0:T(8,128)(2,1)S(1)} %get-tuple-element.84.mixed_early, bf16[8,128,384]{2,1,0:T(8,128)(2,1)S(1)} %get-tuple-element.85.mixed_late, ...), custom_call_target="tpu_custom_call" | custom-call | flops 20000000 | bytes 1048576 | tf_op jit(solution)/shard_map/grad/pallas_call | solution.py:495
  78.8 3.9 %collective-permute-start.25 = (bf16[256,256]{1,0:T(8,128)(2,1)S(1)}, bf16[256,256]{1,0:T(8,128)(2,1)S(1)}, u32[]{:S(2)}, u32[]{:S(2)}) collective-permute-start(bf16[256,256]{1,0:T(8,128)(2,1)S(1)} %get-tuple-element.113), channel_id=1, source_target_pairs={{0,1},{1,2},{2,3},{3,0},{4,5},{5,6},{6,7},{7,4},{8,9},{9,10},{10,1... | collective-permute-start | bytes 393224 | tf_op jit(solution)/shard_map/ppermute | solution.py:336
  82.8 1.5 %collective-permute-start.27 = (bf16[256,256]{1,0:T(8,128)(2,1)S(1)}, bf16[256,256]{1,0:T(8,128)(2,1)S(1)}, u32[]{:S(2)}, u32[]{:S(2)}) collective-permute-start(bf16[256,256]{1,0:T(8,128)(2,1)S(1)} %get-tuple-element.115), channel_id=1, source_target_pairs={{0,2},{1,3},{2,0},{3,1},{4,6},{5,7},{6,4},{7,5},{8,10},{9,11},{10,... | collective-permute-start | bytes 393224 | tf_op jit(solution)/shard_map/ppermute | solution.py:336
  84.3 7.5 %collective-permute-done.17.refs_3_ = bf16[256,384]{1,0:T(8,128)(2,1)S(1)} collective-permute-done((bf16[256,384]{1,0:T(8,128)(2,1)S(1)}, bf16[256,384]{1,0:T(8,128)(2,1)S(1)}, u32[]{:S(2)}, u32[]{:S(2)}) %collective-permute-start.17) | collective-permute-done | bytes 196640 | tf_op jit(solution)/shard_map/ppermute | solution.py:336
  93.7 6.5 %collective-permute-done.27.refs_7_ = bf16[256,256]{1,0:T(8,128)(2,1)S(1)} collective-permute-done((bf16[256,256]{1,0:T(8,128)(2,1)S(1)}, bf16[256,256]{1,0:T(8,128)(2,1)S(1)}, u32[]{:S(2)}, u32[]{:S(2)}) %collective-permute-start.27) | collective-permute-done | bytes 131104 | tf_op jit(solution)/shard_map/ppermute | solution.py:336
  (52 shorter events, 19.1 us)
Async XLA Ops:
  1.7 10.5 %collective-permute-start = (bf16[128,1024]{1,0:T(8,128)(2,1)S(1)}, bf16[128,1024]{1,0:T(8,128)(2,1)S(1)}, u32[]{:S(2)}, u32[]{:S(2)}) collective-permute-start(bf16[128,1024]{1,0:T(8,128)(2,1)S(1)} %slice_convert_fusion), channel_id=1, source_target_pairs={{0,1},{1,2},{2,3},{4,5},{5,6},{6,7},{8,9},{9,10},{10,11},{12,13},{... | collective-permute-start | bytes 786440 | tf_op jit(solution)/shard_map/ppermute | solution.py:394
  13.8 9.3 %collective-permute-start.2 = (bf16[1040,128]{1,0:T(8,128)(2,1)S(1)}, bf16[1040,128]{1,0:T(8,128)(2,1)S(1)}, u32[]{:S(2)}, u32[]{:S(2)}) collective-permute-start(bf16[1040,128]{1,0:T(8,128)(2,1)S(1)} %get-tuple-element.76), channel_id=1, source_target_pairs={{0,8},{4,12},{8,0},{12,4},{16,24},{20,28},{24,16},{28,20},{1,9},{5... | collective-permute-start | bytes 798728 | tf_op jit(solution)/shard_map/ppermute | solution.py:343
  15.3 14.5 %collective-permute-start.3 = (bf16[1040,128]{1,0:T(8,128)(2,1)S(1)}, bf16[1040,128]{1,0:T(8,128)(2,1)S(1)}, u32[]{:S(2)}, u32[]{:S(2)}) collective-permute-start(bf16[1040,128]{1,0:T(8,128)(2,1)S(1)} %get-tuple-element.77), channel_id=1, source_target_pairs={{0,12},{4,8},{8,4},{12,0},{16,28},{20,24},{24,20},{28,16},{1,13},{... | collective-permute-start | bytes 798728 | tf_op jit(solution)/shard_map/ppermute | solution.py:343
  15.7 14.2 %collective-permute-start.4 = (bf16[1040,128]{1,0:T(8,128)(2,1)S(1)}, bf16[1040,128]{1,0:T(8,128)(2,1)S(1)}, u32[]{:S(2)}, u32[]{:S(2)}) collective-permute-start(bf16[1040,128]{1,0:T(8,128)(2,1)S(1)} %get-tuple-element.78), channel_id=1, source_target_pairs={{0,16},{4,20},{8,24},{12,28},{16,0},{20,4},{24,8},{28,12},{1,17},{... | collective-permute-start | bytes 798728 | tf_op jit(solution)/shard_map/ppermute | solution.py:343
  17.2 23.7 %collective-permute-start.5 = (bf16[1040,128]{1,0:T(8,128)(2,1)S(1)}, bf16[1040,128]{1,0:T(8,128)(2,1)S(1)}, u32[]{:S(2)}, u32[]{:S(2)}) collective-permute-start(bf16[1040,128]{1,0:T(8,128)(2,1)S(1)} %get-tuple-element.79), channel_id=1, source_target_pairs={{0,20},{4,16},{8,28},{12,24},{16,4},{20,0},{24,12},{28,8},{1,21},{... | collective-permute-start | bytes 798728 | tf_op jit(solution)/shard_map/ppermute | solution.py:343
  17.4 23.5 %collective-permute-start.6 = (bf16[1040,128]{1,0:T(8,128)(2,1)S(1)}, bf16[1040,128]{1,0:T(8,128)(2,1)S(1)}, u32[]{:S(2)}, u32[]{:S(2)}) collective-permute-start(bf16[1040,128]{1,0:T(8,128)(2,1)S(1)} %get-tuple-element.80), channel_id=1, source_target_pairs={{0,24},{4,28},{8,16},{12,20},{16,8},{20,12},{24,0},{28,4},{1,25},{... | collective-permute-start | bytes 798728 | tf_op jit(solution)/shard_map/ppermute | solution.py:343
  23.1 17.8 %collective-permute-start.7 = (bf16[1040,128]{1,0:T(8,128)(2,1)S(1)}, bf16[1040,128]{1,0:T(8,128)(2,1)S(1)}, u32[]{:S(2)}, u32[]{:S(2)}) collective-permute-start(bf16[1040,128]{1,0:T(8,128)(2,1)S(1)} %get-tuple-element.81), channel_id=1, source_target_pairs={{0,28},{4,24},{8,20},{12,16},{16,12},{20,8},{24,4},{28,0},{1,29},{... | collective-permute-start | bytes 798728 | tf_op jit(solution)/shard_map/ppermute | solution.py:343
  44.3 7.9 %collective-permute-start.11 = (bf16[2,64,512]{2,1,0:T(8,128)(2,1)S(1)}, bf16[2,64,512]{2,1,0:T(8,128)(2,1)S(1)}, u32[]{:S(2)}, u32[]{:S(2)}) collective-permute-start(bf16[2,64,512]{2,1,0:T(8,128)(2,1)S(1)} %get-tuple-element.90), channel_id=1, source_target_pairs={{0,16},{4,20},{8,24},{12,28},{16,0},{20,4},{24,8},{28,12},{1,17},{... | collective-permute-start | bytes 393224 | tf_op jit(solution)/shard_map/ppermute | solution.py:343
  45.9 12.6 %collective-permute-start.12 = (bf16[2,64,512]{2,1,0:T(8,128)(2,1)S(1)}, bf16[2,64,512]{2,1,0:T(8,128)(2,1)S(1)}, u32[]{:S(2)}, u32[]{:S(2)}) collective-permute-start(bf16[2,64,512]{2,1,0:T(8,128)(2,1)S(1)} %get-tuple-element.91), channel_id=1, source_target_pairs={{0,20},{4,16},{8,28},{12,24},{16,4},{20,0},{24,12},{28,8},{1,21},{... | collective-permute-start | bytes 393224 | tf_op jit(solution)/shard_map/ppermute | solution.py:343
  46.4 16.5 %collective-permute-start.13 = (bf16[2,64,512]{2,1,0:T(8,128)(2,1)S(1)}, bf16[2,64,512]{2,1,0:T(8,128)(2,1)S(1)}, u32[]{:S(2)}, u32[]{:S(2)}) collective-permute-start(bf16[2,64,512]{2,1,0:T(8,128)(2,1)S(1)} %get-tuple-element.92), channel_id=1, source_target_pairs={{0,24},{4,28},{8,16},{12,20},{16,8},{20,12},{24,0},{28,4},{1,25},{... | collective-permute-start | bytes 393224 | tf_op jit(solution)/shard_map/ppermute | solution.py:343
  49.2 15.4 %collective-permute-start.14 = (bf16[2,64,512]{2,1,0:T(8,128)(2,1)S(1)}, bf16[2,64,512]{2,1,0:T(8,128)(2,1)S(1)}, u32[]{:S(2)}, u32[]{:S(2)}) collective-permute-start(bf16[2,64,512]{2,1,0:T(8,128)(2,1)S(1)} %get-tuple-element.93), channel_id=1, source_target_pairs={{0,28},{4,24},{8,20},{12,16},{16,12},{20,8},{24,4},{28,0},{1,29},{... | collective-permute-start | bytes 393224 | tf_op jit(solution)/shard_map/ppermute | solution.py:343
  50.9 15.2 %collective-permute-start.18 = (bf16[2,64,512]{2,1,0:T(8,128)(2,1)S(1)}, bf16[2,64,512]{2,1,0:T(8,128)(2,1)S(1)}, u32[]{:S(2)}, u32[]{:S(2)}) collective-permute-start(bf16[2,64,512]{2,1,0:T(8,128)(2,1)S(1)} %get-tuple-element.105), channel_id=1, source_target_pairs={{0,4},{4,0},{8,12},{12,8},{16,20},{20,16},{24,28},{28,24},{1,5},{5... | collective-permute-start | bytes 393224 | tf_op jit(solution)/shard_map/ppermute | solution.py:343
  52.1 16.5 %collective-permute-start.19 = (bf16[2,64,512]{2,1,0:T(8,128)(2,1)S(1)}, bf16[2,64,512]{2,1,0:T(8,128)(2,1)S(1)}, u32[]{:S(2)}, u32[]{:S(2)}) collective-permute-start(bf16[2,64,512]{2,1,0:T(8,128)(2,1)S(1)} %get-tuple-element.106), channel_id=1, source_target_pairs={{0,8},{4,12},{8,0},{12,4},{16,24},{20,28},{24,16},{28,20},{1,9},{5... | collective-permute-start | bytes 393224 | tf_op jit(solution)/shard_map/ppermute | solution.py:343
  58.5 11.6 %collective-permute-start.20 = (bf16[2,64,512]{2,1,0:T(8,128)(2,1)S(1)}, bf16[2,64,512]{2,1,0:T(8,128)(2,1)S(1)}, u32[]{:S(2)}, u32[]{:S(2)}) collective-permute-start(bf16[2,64,512]{2,1,0:T(8,128)(2,1)S(1)} %get-tuple-element.107), channel_id=1, source_target_pairs={{0,12},{4,8},{8,4},{12,0},{16,28},{20,24},{24,20},{28,16},{1,13},{... | collective-permute-start | bytes 393224 | tf_op jit(solution)/shard_map/ppermute | solution.py:343
  62.9 8.2 %collective-permute-start.21 = (bf16[2,64,512]{2,1,0:T(8,128)(2,1)S(1)}, bf16[2,64,512]{2,1,0:T(8,128)(2,1)S(1)}, u32[]{:S(2)}, u32[]{:S(2)}) collective-permute-start(bf16[2,64,512]{2,1,0:T(8,128)(2,1)S(1)} %get-tuple-element.108), channel_id=1, source_target_pairs={{0,16},{4,20},{8,24},{12,28},{16,0},{20,4},{24,8},{28,12},{1,17},{... | collective-permute-start | bytes 393224 | tf_op jit(solution)/shard_map/ppermute | solution.py:343
  64.6 9.1 %collective-permute-start.22 = (bf16[2,64,512]{2,1,0:T(8,128)(2,1)S(1)}, bf16[2,64,512]{2,1,0:T(8,128)(2,1)S(1)}, u32[]{:S(2)}, u32[]{:S(2)}) collective-permute-start(bf16[2,64,512]{2,1,0:T(8,128)(2,1)S(1)} %get-tuple-element.109), channel_id=1, source_target_pairs={{0,20},{4,16},{8,28},{12,24},{16,4},{20,0},{24,12},{28,8},{1,21},{... | collective-permute-start | bytes 393224 | tf_op jit(solution)/shard_map/ppermute | solution.py:343
  66.1 16.6 %collective-permute-start.15 = (bf16[256,384]{1,0:T(8,128)(2,1)S(1)}, bf16[256,384]{1,0:T(8,128)(2,1)S(1)}, u32[]{:S(2)}, u32[]{:S(2)}) collective-permute-start(bf16[256,384]{1,0:T(8,128)(2,1)S(1)} %get-tuple-element.97), channel_id=1, source_target_pairs={{0,1},{1,2},{2,3},{3,0},{4,5},{5,6},{6,7},{7,4},{8,9},{9,10},{10,1... | collective-permute-start | bytes 589832 | tf_op jit(solution)/shard_map/ppermute | solution.py:336
  68.7 7.2 %collective-permute-start.23 = (bf16[2,64,512]{2,1,0:T(8,128)(2,1)S(1)}, bf16[2,64,512]{2,1,0:T(8,128)(2,1)S(1)}, u32[]{:S(2)}, u32[]{:S(2)}) collective-permute-start(bf16[2,64,512]{2,1,0:T(8,128)(2,1)S(1)} %get-tuple-element.110), channel_id=1, source_target_pairs={{0,24},{4,28},{8,16},{12,20},{16,8},{20,12},{24,0},{28,4},{1,25},{... | collective-permute-start | bytes 393224 | tf_op jit(solution)/shard_map/ppermute | solution.py:343
  70.1 7.2 %collective-permute-start.24 = (bf16[2,64,512]{2,1,0:T(8,128)(2,1)S(1)}, bf16[2,64,512]{2,1,0:T(8,128)(2,1)S(1)}, u32[]{:S(2)}, u32[]{:S(2)}) collective-permute-start(bf16[2,64,512]{2,1,0:T(8,128)(2,1)S(1)} %get-tuple-element.111), channel_id=1, source_target_pairs={{0,28},{4,24},{8,20},{12,16},{16,12},{20,8},{24,4},{28,0},{1,29},{... | collective-permute-start | bytes 393224 | tf_op jit(solution)/shard_map/ppermute | solution.py:343
  71.2 13.1 %collective-permute-start.16 = (bf16[256,384]{1,0:T(8,128)(2,1)S(1)}, bf16[256,384]{1,0:T(8,128)(2,1)S(1)}, u32[]{:S(2)}, u32[]{:S(2)}) collective-permute-start(bf16[256,384]{1,0:T(8,128)(2,1)S(1)} %get-tuple-element.98), channel_id=1, source_target_pairs={{0,3},{1,0},{2,1},{3,2},{4,7},{5,4},{6,5},{7,6},{8,11},{9,8},{10,9... | collective-permute-start | bytes 589832 | tf_op jit(solution)/shard_map/ppermute | solution.py:336
  73.8 18.1 %collective-permute-start.17 = (bf16[256,384]{1,0:T(8,128)(2,1)S(1)}, bf16[256,384]{1,0:T(8,128)(2,1)S(1)}, u32[]{:S(2)}, u32[]{:S(2)}) collective-permute-start(bf16[256,384]{1,0:T(8,128)(2,1)S(1)} %get-tuple-element.99), channel_id=1, source_target_pairs={{0,2},{1,3},{2,0},{3,1},{4,6},{5,7},{6,4},{7,5},{8,10},{9,11},{10,... | collective-permute-start | bytes 589832 | tf_op jit(solution)/shard_map/ppermute | solution.py:336
  78.8 13.8 %collective-permute-start.25 = (bf16[256,256]{1,0:T(8,128)(2,1)S(1)}, bf16[256,256]{1,0:T(8,128)(2,1)S(1)}, u32[]{:S(2)}, u32[]{:S(2)}) collective-permute-start(bf16[256,256]{1,0:T(8,128)(2,1)S(1)} %get-tuple-element.113), channel_id=1, source_target_pairs={{0,1},{1,2},{2,3},{3,0},{4,5},{5,6},{6,7},{7,4},{8,9},{9,10},{10,1... | collective-permute-start | bytes 393224 | tf_op jit(solution)/shard_map/ppermute | solution.py:336
  82.8 10.9 %collective-permute-start.26 = (bf16[256,256]{1,0:T(8,128)(2,1)S(1)}, bf16[256,256]{1,0:T(8,128)(2,1)S(1)}, u32[]{:S(2)}, u32[]{:S(2)}) collective-permute-start(bf16[256,256]{1,0:T(8,128)(2,1)S(1)} %get-tuple-element.114), channel_id=1, source_target_pairs={{0,3},{1,0},{2,1},{3,2},{4,7},{5,4},{6,5},{7,6},{8,11},{9,8},{10,9... | collective-permute-start | bytes 393224 | tf_op jit(solution)/shard_map/ppermute | solution.py:336
  82.8 17.4 %collective-permute-start.27 = (bf16[256,256]{1,0:T(8,128)(2,1)S(1)}, bf16[256,256]{1,0:T(8,128)(2,1)S(1)}, u32[]{:S(2)}, u32[]{:S(2)}) collective-permute-start(bf16[256,256]{1,0:T(8,128)(2,1)S(1)} %get-tuple-element.115), channel_id=1, source_target_pairs={{0,2},{1,3},{2,0},{3,1},{4,6},{5,7},{6,4},{7,5},{8,10},{9,11},{10,... | collective-permute-start | bytes 393224 | tf_op jit(solution)/shard_map/ppermute | solution.py:336
  (9 other events, 81.4 us)
